TPU v7x, 128 devices: a whole 4x4x4 slice. The times are simulated.
128 devices in a mesh: tmpl: 8 (over x_hi, z), spec: 8 (over y, x_lo), expo: 2 (over core).
Axes of the slice: x: 4 (x_hi: 2, x_lo: 2; x = x_hi * 2 + x_lo), y: 4, z: 4, core: 2. Of those that a mesh axis runs over, the one named last changes fastest.
Arguments:
- flux: bfloat16 [12288, 7808], P(('tmpl', 'spec', 'expo')), may hold values from -6 to 6
- ivar: bfloat16 [12288, 7808], P(('tmpl', 'spec', 'expo')), may hold values from 0.5 to 8
- pixel_mask: int32 [12288, 61], P(('tmpl', 'spec', 'expo')), may hold values 0 or 1
- exposure_target: int32 [12288], P(('tmpl', 'spec', 'expo')), may hold values from 0 to 63, as said below
- basis: bfloat16 [128, 10, 7808], P(('tmpl', 'spec')), may hold values from -0.0625 to 0.0625
- trial_counts: int32 [3], replicated, may hold values from 1 to 64, 128 in all
- target_class: int32 [4096], P(('tmpl', 'spec', 'expo')), may hold values from 0 to 2
Outputs:
- coefficients: float32 [10, 4096, 128], P(None, ('tmpl', 'spec', 'expo'))
- fit_gain: float32 [4096, 128], P(('tmpl', 'spec', 'expo'))
- best_gain: float32 [4096], P(('tmpl', 'spec', 'expo'))
Inputs may be any that keep to these rules, and one draw needn't show every extreme that they name: `exposure_target`: every target of a group of 64 targets is named by at least one exposure of its group of 192 exposures. `trial_counts`: the counts sum to 128; class c takes the trials that follow those of the classes below it.
All inputs are finite; a program needn't handle non-finite values. No bound on the sum of `pixel_mask` on one device may be relied on, other than what follows from the above.
Results may differ from a plain program's by a relative error of at most 0.0038.
Values may be sent and summed in bfloat16 or wider, within the bound.
No kernel may reach another device: no remote copies, remote signals or barrier semaphores. Data moves between devices by JAX's collectives and lax.ppermute only.
A program may use at most 512 MiB of HBM per device.

v0:
```python
import jax
import jax.numpy as jnp
import numpy as np
from jax import lax
from jax.sharding import PartitionSpec as P


def upper_pairs(term_count):
    leading = []
    trailing = []
    for upper_idx in range(term_count):
        for lower_idx in range(upper_idx, term_count):
            leading.append(upper_idx)
            trailing.append(lower_idx)
    return (np.array(leading), np.array(trailing))


def cholesky_solve(entries, right_side, term_count):
    lookup = {}
    position = 0
    for upper_idx in range(term_count):
        for lower_idx in range(upper_idx, term_count):
            lookup[upper_idx, lower_idx] = entries[position]
            lookup[lower_idx, upper_idx] = entries[position]
            position += 1
    factor = {}
    for column in range(term_count):
        partial_value = lookup[column, column]
        for earlier in range(column):
            partial_value = partial_value - factor[column, earlier] * factor[column, earlier]
        diag_root = jnp.sqrt(partial_value)
        factor[column, column] = diag_root
        for across in range(column + 1, term_count):
            partial_value = lookup[across, column]
            for earlier in range(column):
                partial_value = partial_value - factor[across, earlier] * factor[column, earlier]
            factor[across, column] = partial_value / diag_root
    forward = []
    for across in range(term_count):
        partial_value = right_side[across]
        for earlier in range(across):
            partial_value = partial_value - factor[across, earlier] * forward[earlier]
        forward.append(partial_value / factor[across, across])
    answer = [None] * term_count
    for across in reversed(range(term_count)):
        partial_value = forward[across]
        for earlier in range(across + 1, term_count):
            partial_value = partial_value - factor[earlier, across] * answer[earlier]
        answer[across] = partial_value / factor[across, across]
    return jnp.stack(answer)


def fit_block(coadd_ivar, coadd_wflux, trial_block):
    term_count = trial_block.shape[1]
    leading, trailing = upper_pairs(term_count)
    prior_diag = (leading == trailing).astype(np.float32)
    products = (
        trial_block[:, leading, :].astype(jnp.float32)
        * trial_block[:, trailing, :].astype(jnp.float32)
    ).astype(jnp.bfloat16)
    normal = jnp.einsum("tp,gqp->qtg", coadd_ivar, products, preferred_element_type=jnp.float32)
    normal = normal + jnp.asarray(prior_diag, dtype=jnp.float32)[:, None, None]
    project = jnp.einsum(
        "tp,gkp->ktg", coadd_wflux, trial_block, preferred_element_type=jnp.float32
    )
    coefs = cholesky_solve(
        [normal[element] for element in range(normal.shape[0])],
        [project[element] for element in range(term_count)],
        term_count,
    )
    gains = jnp.sum(project * coefs, axis=0) / term_count
    return (coefs, gains)


def body(flux, ivar, pixel_mask, exposure_target, basis, trial_counts, target_class):
    count_rows, pixels = ivar.shape
    blocks = pixel_mask.shape[1]
    masked = (
        ivar.reshape(count_rows, blocks, pixels // blocks)
        * pixel_mask.astype(jnp.bfloat16)[:, :, None]
    )
    weighted_ivar = masked.reshape(count_rows, pixels)
    weighted_flux = (weighted_ivar.astype(jnp.float32) * flux.astype(jnp.float32)).astype(
        jnp.bfloat16
    )
    local_targets = target_class.shape[0]
    group_flux, group_ivar = (
        lax.all_gather(weighted_flux, "expo", axis=0, tiled=True),
        lax.all_gather(weighted_ivar, "expo", axis=0, tiled=True),
    )
    group_owner = lax.all_gather(exposure_target, "expo", axis=0, tiled=True)
    wanted = lax.axis_index("expo") * local_targets + jnp.arange(local_targets, dtype=jnp.int32)
    select = (group_owner[None, :] == wanted[:, None]).astype(jnp.bfloat16)
    summed_flux = jnp.dot(select, group_flux, preferred_element_type=jnp.float32)
    summed_ivar = jnp.dot(select, group_ivar, preferred_element_type=jnp.float32)
    coadd_wflux = summed_flux.astype(jnp.bfloat16)
    coadd_ivar = summed_ivar.astype(jnp.bfloat16)
    term_count = basis.shape[1]
    trial_total = basis.shape[0] * lax.axis_size("tmpl") * lax.axis_size("spec")
    class_ends = jnp.cumsum(trial_counts)
    initial = (
        jnp.zeros((term_count, local_targets, trial_total), jnp.float32),
        jnp.zeros((local_targets, trial_total), jnp.float32),
    )
    basis_piece = lax.all_gather(basis, ("tmpl", "spec"), axis=0, tiled=True)
    offset_trial = jnp.int32(0)
    piece_trials = basis_piece.shape[0]
    coefs, gains = fit_block(coadd_ivar, coadd_wflux, basis_piece)
    coefs = jnp.transpose(coefs, (0, 1, 2))
    trial_ids = jnp.arange(piece_trials, dtype=jnp.int32)
    trial_class = jnp.sum((trial_ids[:, None] >= class_ends[None, :]).astype(jnp.int32), axis=1)
    valid = trial_class[None, :] == target_class[:, None]
    gains = jnp.where(valid, gains, jnp.zeros_like(gains))
    zero_index = jnp.int32(0)
    all_coefs = lax.dynamic_update_slice(initial[0], coefs, (zero_index, zero_index, offset_trial))
    all_gains = lax.dynamic_update_slice(initial[1], gains, (zero_index, offset_trial))
    best_gain = jnp.max(all_gains, axis=1)
    return (all_coefs, all_gains, best_gain)


def solution(mesh):
    return jax.shard_map(
        body,
        mesh=mesh,
        in_specs=(
            P(("tmpl", "spec", "expo"), None),
            P(("tmpl", "spec", "expo"), None),
            P(("tmpl", "spec", "expo"), None),
            P(("tmpl", "spec", "expo")),
            P(("tmpl", "spec"), None, None),
            P(),
            P(("tmpl", "spec", "expo")),
        ),
        out_specs=(
            P(None, ("tmpl", "spec", "expo"), None),
            P(("tmpl", "spec", "expo"), None),
            P(("tmpl", "spec", "expo")),
        ),
        check_vma=False,
    )
```

profile of v0, /device:TPU:1, one launch (start us, length us, event | category | flops | bytes accessed | tf_op | source)
XLA Modules:
  0.0 944.6 jit_solution(7785168701475580325)
XLA Ops:
  7.2 0.0 all-gather.8.cloned.1.call-start
  7.2 0.8 convert_element_type.31
  8.0 0.1 copy.26
  8.1 1.0 mul.3054
  9.1 5.1 multiply_convert_fusion.2
  14.2 0.0 all-gather.8.cloned.1.call-update
  14.2 0.0 all-gather.6.cloned.1.call-start
  14.2 1.8 copy.27
  16.0 0.0 all-gather.6.cloned.1.call-update
  16.1 0.0 all-gather.4.cloned.1.call-start
  16.1 0.7 all-gather.4.cloned.1.call-update
  16.8 0.0 copy-start.4
  16.8 0.8 reduce-window.8
  17.7 0.7 convert_reduce_fusion
  18.3 1.2 dynamic-slice
  20.2 0.9 dynamic-update-slice
  21.1 2.9 all-reduce
  24.0 0.7 pad_clamp_fusion
  24.6 7.9 all-gather.8.cloned.1.call-done
  32.6 3.3 fusion.8.clone.5
  35.9 687.2 %all-gather.6.cloned.1.call-done = bf16[128,10,7808]{2,1,0:T(8,128)(2,1)} async-done(((bf16[2,10,7808]{2,1,0:T(8,128)(2,1)}), bf16[128,10,7808]{2,1,0:T(8,128)(2,1)}) %all-gather.6.cloned.1.call-update) | async-done | bytes 19988496 | tf_op jit(solution)/shard_map/all_gather | solution.py:105
  723.2 22.1 %copy.28 = bf16[128,10,7808]{2,0,1:T(8,128)(2,1)} copy(bf16[128,10,7808]{2,1,0:T(8,128)(2,1)} %all-gather.6.cloned.1.call-done) | data formatting | bytes 39976960 | tf_op jit(solution)/shard_map/all_gather | solution.py:105
  745.3 8.2 mini-gather-slice.5
  753.6 8.8 mini-gather-slice.4
  762.3 22.8 %gather_fusion.3 = bf16[55,128,3840]{2,1,0:T(8,128)(2,1)} fusion(bf16[128,10,3840]{2,0,1:T(8,128)(2,1)} %mini-gather-slice.5, s32[1024]{0:T(1024)S(1)} %get-tuple-element.48), kind=kCustom, calls=%fused_computation.3 | custom fusion | bytes 108134624 | tf_op jit(solution)/shard_map/gather | solution.py:59
  785.1 0.0 copy-done.2
  785.1 22.2 %gather_fusion.1 = bf16[55,128,3840]{2,1,0:T(8,128)(2,1)} fusion(bf16[128,10,3840]{2,0,1:T(8,128)(2,1)} %mini-gather-slice.5, s32[1024]{0:T(1024)S(1)} %get-tuple-element.49), kind=kCustom, calls=%fused_computation.1 | custom fusion | bytes 108134624 | tf_op jit(solution)/shard_map/gather | solution.py:58
  807.3 22.9 %gather_fusion = bf16[55,128,3968]{2,1,0:T(8,128)(2,1)} fusion(bf16[128,10,3968]{2,0,1:T(8,128)(2,1)} %mini-gather-slice.4, s32[1024]{0:T(1024)S(1)} %get-tuple-element.49), kind=kCustom, calls=%fused_computation | custom fusion | bytes 111739104 | tf_op jit(solution)/shard_map/gather | solution.py:58
  830.2 23.4 %gather_fusion.2 = bf16[55,128,3968]{2,1,0:T(8,128)(2,1)} fusion(bf16[128,10,3968]{2,0,1:T(8,128)(2,1)} %mini-gather-slice.4, s32[1024]{0:T(1024)S(1)} %get-tuple-element.48), kind=kCustom, calls=%fused_computation.2 | custom fusion | bytes 111739104 | tf_op jit(solution)/shard_map/gather | solution.py:59
  853.6 0.0 copy-done
  853.7 0.0 copy-start.5
  853.7 0.0 copy-start.6
  853.7 68.2 %fusion.10 = f32[55,32,128]{2,1,0:T(8,128)S(1)} fusion(bf16[128,55,3840]{2,0,1:T(8,128)(2,1)} %bitcast.40, bf16[128,55,3968]{2,0,1:T(8,128)(2,1)} %bitcast.37, bf16[128,55,3840]{2,0,1:T(8,128)(2,1)} %bitcast.39, bf16[128,55,3968]{2,0,1:T(8,128)(2,1)} %bitcast.38, f32[55]{0:T(128)S(1)} %copy-done.8, bf16[32,7808,1]{1,0,2:T(8,128)(2,1)S(1)} %copy-done), kind=kOutput, calls=%fused_computation.19 | convolution fusion | flops 4067880960 | bytes 221274336 | tf_op jit(solution)/shard_map/tp,gqp->qtg/dot_general | solution.py:61
  921.9 0.0 all-gather.4.cloned.1.call-done
  922.0 11.6 %convolution_bitcast_fusion = f32[10,32,128]{2,1,0:T(8,128)S(1)} fusion(bf16[128,10,7808]{2,0,1:T(8,128)(2,1)} %copy.28, bf16[192,7808]{1,0:T(8,128)(2,1)} %all-gather.4.cloned.1.call-done, s32[192]{0:T(256)S(1)} %copy-done.3, s32[32]{0:T(128)S(1)} %copy-done.5), kind=kOutput, calls=%fused_computation.20 | convolution fusion | flops 735832064 | bytes 23151488 | tf_op jit(solution)/shard_map/tp,gkp->ktg/dot_general | solution.py:63
  933.5 0.5 constant_dynamic-update-slice_fusion.9
  934.1 0.4 constant_dynamic-update-slice_fusion.8
  934.4 0.3 constant_dynamic-update-slice_fusion.7
  934.8 0.3 constant_dynamic-update-slice_fusion.6
  935.1 0.3 constant_dynamic-update-slice_fusion.5
  935.4 0.3 constant_dynamic-update-slice_fusion.4
  935.7 0.3 constant_dynamic-update-slice_fusion.3
  935.9 0.2 constant_dynamic-update-slice_fusion.2
  936.2 0.2 constant_dynamic-update-slice_fusion.1
  936.4 0.2 constant_dynamic-update-slice_fusion
  936.7 0.0 copy-start.1
  936.7 0.0 copy-done.6
  936.7 1.3 fusion.235
  (14 shorter events, 0.1 us)
Async XLA Ops:
  7.2 25.4 %all-gather.8.cloned.1.call-start = ((), (), s32[]{:S(2)}) async-start(), calls=%async_computation.2 | async-start | bytes 4497408 | tf_op jit(solution)/shard_map/all_gather | solution.py:89
  14.2 709.0 %all-gather.6.cloned.1.call-start = ((), (), s32[]{:S(2)}) async-start(), calls=%async_computation.1 | async-start | bytes 32481280 | tf_op jit(solution)/shard_map/all_gather | solution.py:105
  16.1 905.9 %all-gather.4.cloned.1.call-start = ((), (), s32[]{:S(2)}) async-start(), calls=%async_computation | async-start | bytes 4497408 | tf_op jit(solution)/shard_map/all_gather | solution.py:88
  16.8 768.3 %copy-start.4 = (s32[32]{0:T(128)}, s32[32]{0:T(128)S(1)}, u32[]{:S(2)}) copy-start(s32[32]{0:T(128)S(1)} %iota_add_fusion) | copy-start | bytes 388
  24.0 761.1 %copy-start.2 = (s32[192]{0:T(256)}, s32[192]{0:T(256)S(1)}, u32[]{:S(2)}) copy-start(s32[192]{0:T(256)S(1)} %all-reduce) | copy-start | bytes 2308
  830.2 23.4 %copy-start = (bf16[32,7808,1]{1,0,2:T(8,128)(2,1)S(1)}, bf16[32,7808,1]{1,0,2:T(8,128)(2,1)}, u32[]{:S(2)}) copy-start(bf16[32,7808,1]{1,0,2:T(8,128)(2,1)} %fusion.8.clone.5) | copy-start | bytes 1499140
  830.2 23.4 %copy-start.8 = (f32[55]{0:T(128)S(1)}, f32[55]{0:T(128)}, u32[]{:S(2)}) copy-start(f32[55]{0:T(128)} %constant.32.clone) | copy-start | bytes 664
  853.6 68.3 %copy-start.3 = (s32[192]{0:T(256)S(1)}, s32[192]{0:T(256)}, u32[]{:S(2)}) copy-start(s32[192]{0:T(256)} %copy-done.2) | copy-start | bytes 2308
  853.7 68.3 %copy-start.5 = (s32[32]{0:T(128)S(1)}, s32[32]{0:T(128)}, u32[]{:S(2)}) copy-start(s32[32]{0:T(128)} %copy-done.4) | copy-start | bytes 388
  853.7 83.1 %copy-start.6 = (s32[32]{0:T(128)S(1)}, s32[32]{0:T(128)}, u32[]{:S(2)}) copy-start(s32[32]{0:T(128)} %param.18) | copy-start | bytes 388
  853.7 83.1 %copy-start.7 = (s32[128]{0:T(128)S(1)}, s32[128]{0:T(128)}, u32[]{:S(2)}) copy-start(s32[128]{0:T(128)} %convert_reduce_fusion) | copy-start | bytes 1540
  936.7 1.4 copy-start.1
Sparse Core Ops, SparseCore 0:
  14.3 18.2 all-gather.7
  34.2 688.8 all-gather.5
  724.8 16.0 all-gather.3
where the time goes:
time: 945 us
  waiting for transfers between devices  696 us (74%)
  local copies, waits for them, and re-layouts  136 us (14%)
  matrix products  83.1 us (9%)
  between operations  14.6 us (2%)
  other arithmetic  12.4 us (1%)
    all_gather x1, waiting for transfers between devices, body(): basis_piece = lax.all_gather(basis, ('tmpl', 'spec'), axis=0, tiled=True)  687 us
    dot_general x1, matrix products, fit_block(): jnp.einsum('tp,gqp->qtg', coadd_ivar, products, preferred_element_type=jn...  68.2 us
    gather x4, local copies, waits for them, and re-layouts, fit_block(): trial_block[:, leading, :].astype(jnp.float32)  62.1 us
    gather x2, local copies, waits for them, and re-layouts, fit_block(): trial_block[:, trailing, :].astype(jnp.float32)  46.2 us
    all_gather x1, local copies, waits for them, and re-layouts, body(): basis_piece = lax.all_gather(basis, ('tmpl', 'spec'), axis=0, tiled=True)  22.1 us
  transfers between devices with their start and end apart: 3, of which 2 were waited for; matrix products, arithmetic and copies ran while one was open for 22% of the time, Pallas kernels for 0%

commit v1 on v0

v1 whole, which is shorter than its diff:
```python
import jax
import jax.numpy as jnp
import numpy as np
from jax import lax
from jax.experimental import pallas as pl
from jax.experimental.pallas import tpu as pltpu
from jax.sharding import PartitionSpec as P

AXES = ("tmpl", "spec", "expo")
SIDES = (2, 4, 4, 2, 2)
TERMS = 10
HALVES = TERMS // 2
SLICES = 16
WIDTH = 512
COMBOS = 30
ROWS = COMBOS * 16 + TERMS * 8
VMEM = 56 * 1024 * 1024


def moved(device, core=0, x_lo=0, x_hi=0, along=None, step=0):
    h, z, y, lo, c = (int(v) for v in np.unravel_index(device, SIDES))
    if along is not None:
        if (c == 0) == (along == 0):
            z = (z + step) % 4
        else:
            y = (y + step) % 4
    return int(np.ravel_multi_index((h ^ x_hi, z, y, lo ^ x_lo, c ^ core), SIDES))


def send(value, **how):
    return lax.ppermute(value, AXES, [(d, moved(d, **how)) for d in range(128)])


def combos():
    out = [(m, n, 0) for m in range(HALVES) for n in range(m + 1, HALVES)]
    out += [(m, n, 1) for m in range(HALVES) for n in range(m + 1, HALVES)]
    out += [(m, m, 0) for m in range(HALVES)]
    out += [(m, m, 1) for m in range(HALVES)]
    return out


def entry_rows():
    where = {}
    for i, (m, n, crossed) in enumerate(combos()):
        for half in range(2):
            k, l = 2 * m + half, 2 * n + (half ^ crossed)
            where.setdefault((min(k, l), max(k, l)), i * 16 + half * 8)
    return where


def prep_kernel(place, basis, out, rows):
    core = place[0]
    pixels = basis.shape[2]
    rows[...] = jnp.zeros_like(rows)
    mine = jnp.where(core == 0, basis[0].astype(jnp.float32), basis[1].astype(jnp.float32))
    for h in range(SLICES):
        width = min(WIDTH, pixels - h * WIDTH)
        for k in range(TERMS):
            rows[k * SLICES + h : k * SLICES + h + 1, :width] = mine[k : k + 1, h * WIDTH : h * WIDTH + width]
    out[...] = rows[...].astype(jnp.bfloat16).reshape(out.shape)


def weight_kernel(flux, ivar, mask, owner, out):
    step = pl.program_id(0)

    @pl.when(step < pl.num_programs(0) - 1)
    def _():
        good = mask[...].astype(jnp.float32)
        for b in range(good.shape[1]):
            lanes = slice(b * 128, (b + 1) * 128)
            masked = (ivar[:, lanes].astype(jnp.float32) * good[:, b : b + 1]).astype(jnp.bfloat16)
            out[0, 0:16, lanes] = masked
            out[0, 16:32, lanes] = (masked.astype(jnp.float32) * flux[:, lanes].astype(jnp.float32)).astype(jnp.bfloat16)

    @pl.when(step == pl.num_programs(0) - 1)
    def _():
        out[...] = jnp.zeros_like(out)
        names = owner[...].astype(jnp.float32)
        out[0, 0:16, 0 : names.shape[1]] = jnp.broadcast_to(names, (16, names.shape[1])).astype(jnp.bfloat16)


def coadd_kernel(place, own_names, other_names, own, other, coadd_ivar, coadd_wflux, outgoing):
    core = place[0]
    row = lax.broadcasted_iota(jnp.int32, (64, 96), 0)
    wanted = jnp.where(row < 32, row + core * 32, row - core * 32).astype(jnp.float32)
    sums = []
    for part in range(2):
        total = None
        for names, block in ((own_names, own), (other_names, other)):
            select = (names[0, 0:1, 0:96].astype(jnp.float32) == wanted).astype(jnp.bfloat16)
            spectra = block[0:6, part * 16 : part * 16 + 16, :].reshape(96, block.shape[2])
            piece = jnp.dot(select, spectra, preferred_element_type=jnp.float32)
            total = piece if total is None else total + piece
        sums.append(total)
    coadd_ivar[...] = sums[0].astype(jnp.bfloat16)
    coadd_wflux[...] = sums[1].astype(jnp.bfloat16)
    outgoing[...] = jnp.where(core == 0, sums[0], sums[1]).astype(jnp.bfloat16)


def solve(entries, right):
    lower, scaled, inverse = {}, {}, []
    for j in range(TERMS):
        pivot = entries[j, j]
        for e in range(j):
            pivot = pivot - lower[j, e] * scaled[j, e]
        inverse.append(1.0 / pivot)
        for i in range(j + 1, TERMS):
            value = entries[j, i]
            for e in range(j):
                value = value - lower[i, e] * scaled[j, e]
            scaled[i, j] = value
            lower[i, j] = value * inverse[j]
    forward = []
    for i in range(TERMS):
        value = right[i]
        for e in range(i):
            value = value - lower[i, e] * forward[e]
        forward.append(value)
    answer = [None] * TERMS
    for i in reversed(range(TERMS)):
        value = forward[i] * inverse[i]
        for e in range(i + 1, TERMS):
            value = value - lower[e, i] * answer[e]
        answer[i] = value
    return answer


def fit_blocks(core, parts_of_blocks, own_ivar, own_wflux, direct, swapped, even, odd, total):
    count = len(parts_of_blocks)
    pixels = own_ivar.shape[1]
    side = SLICES * 16
    row = lax.broadcasted_iota(jnp.int32, (side, side), 0)
    col = lax.broadcasted_iota(jnp.int32, (side, side), 1)
    same = ((row // 16) == (col % 16)) & ((row % 8) == (col // 32))
    half, source = (row // 8) % 2, (col // 16) % 2
    straight = (same & (half == source)).astype(jnp.float32).astype(jnp.bfloat16)
    crossed = (same & (half != source)).astype(jnp.float32).astype(jnp.bfloat16)
    for b, parts in enumerate(parts_of_blocks):
        for m in range(HALVES):
            pieces = [p[:, 2 * m : 2 * m + 2].reshape(p.shape[0] * 2 * SLICES, WIDTH) for p in parts]
            block = pieces[0] if len(pieces) == 1 else jnp.concatenate(pieces, axis=0)
            even[b, m] = jnp.dot(straight, block, preferred_element_type=jnp.float32).astype(jnp.bfloat16)
            odd[b, m] = jnp.dot(crossed, block, preferred_element_type=jnp.float32).astype(jnp.bfloat16)

    contract = (((1,), (1,)), ((), ()))

    def one_slice(h, width, first):
        start = h * WIDTH if isinstance(h, int) else pl.multiple_of(h * WIDTH, WIDTH)
        lanes = pl.ds(start, width)
        near = direct[:, lanes].astype(jnp.float32)
        far = jnp.concatenate([swapped[32:64, lanes], swapped[0:32, lanes]], axis=0).astype(jnp.float32)
        ivar_part = jnp.where(core == 0, near, far).astype(jnp.bfloat16)
        wflux_part = jnp.where(core == 0, far, near).astype(jnp.bfloat16)
        ivar = jnp.concatenate([own_ivar[:, lanes], ivar_part], axis=0)
        wflux = jnp.concatenate([own_wflux[:, lanes], wflux_part], axis=0)
        rows = pl.ds(h * 16 if isinstance(h, int) else pl.multiple_of(h * 16, 16), 16)
        for b in range(count):
            evens = [even[b, m, rows, 0:width] for m in range(HALVES)]
            odds = [odd[b, m, rows, 0:width] for m in range(HALVES)]
            products = jnp.concatenate(
                [evens[m] * (odds[n] if cross else evens[n]) for m, n, cross in combos()], axis=0
            )
            normal = lax.dot_general(products, ivar, contract, preferred_element_type=jnp.float32)
            project = lax.dot_general(
                jnp.concatenate(evens, axis=0), wflux, contract, preferred_element_type=jnp.float32
            )
            if first:
                total[b, 0 : COMBOS * 16] = normal
                total[b, COMBOS * 16 : ROWS] = project
            else:
                total[b, 0 : COMBOS * 16] += normal
                total[b, COMBOS * 16 : ROWS] += project

    full = pixels // WIDTH
    one_slice(0, WIDTH, True)

    def step(h, carry):
        one_slice(h, WIDTH, False)
        return carry

    lax.fori_loop(1, full, step, 0)
    if pixels > full * WIDTH:
        one_slice(full, pixels - full * WIDTH, False)

    entries = {}
    for (k, l), at in entry_rows().items():
        value = total[:, at : at + 8, :]
        entries[k, l] = value + 1.0 if k == l else value
    right = [total[:, COMBOS * 16 + k * 8 : COMBOS * 16 + k * 8 + 8, :] for k in range(TERMS)]
    answer = solve(entries, right)
    gain = right[0] * answer[0]
    for k in range(1, TERMS):
        gain = gain + right[k] * answer[k]
    values = answer + [gain / TERMS, jnp.zeros_like(gain)]
    lane = lax.broadcasted_iota(jnp.int32, values[0].shape, 2) // 32
    packed = []
    for group in range(4):
        packed.append([])
        for q in range(3):
            out = None
            for k in range(4):
                shift = (k - group) % 4 * 32
                value = values[4 * q + k]
                value = pltpu.roll(value, shift, 2) if shift else value
                out = value if out is None else jnp.where(lane == k, value, out)
            packed[-1].append(out)
    return packed


def first_fit_kernel(place, own, up, down, own_ivar, own_wflux, direct, swapped, out, even, odd, total):
    packed = fit_blocks(place[0], [[own], [up], [down]], own_ivar, own_wflux, direct, swapped, even, odd, total)
    for group in range(4):
        for q in range(3):
            out[group, :, q] = packed[group][q]


def last_fit_kernel(place, first, far_a, far_b, own_ivar, own_wflux, direct, swapped, *rest):
    outs, (even, odd, total) = rest[:4], rest[4:]
    packed = fit_blocks(place[0], [[far_a, far_b]], own_ivar, own_wflux, direct, swapped, even, odd, total)
    for group in range(4):
        outs[group][0:3] = first[group]
        for q in range(3):
            outs[group][3:4, q] = packed[group][q]


def final_kernel(place, counts, classes, part_0, part_1, part_2, part_3, coefs, gains, best):
    core, lo, hi, z, y = (place[i] for i in range(5))

    def shift(n):
        return jnp.where(n == 1, 3, jnp.where(n == 2, 1, jnp.where(n == 3, 2, 0)))

    def trial_of(i):
        group, b, t = i // 32, (i // 8) % 4, i % 8
        source_core = core ^ (group % 2)
        source_lo = lo ^ (group // 2)
        near, far = shift(t // 2), shift(b)
        z_of = (z + jnp.where(source_core == 0, near, far)) % 4
        y_of = (y + jnp.where(source_core == 0, far, near)) % 4
        return (hi ^ (t % 2)) * 64 + z_of * 16 + y_of * 4 + source_lo * 2 + source_core

    trial = trial_of(lax.broadcasted_iota(jnp.int32, (128, 128), 0))
    lane = lax.broadcasted_iota(jnp.int32, (128, 128), 1)
    to_lane = (trial == lane).astype(jnp.float32)
    end_0 = counts[0]
    end_1 = end_0 + counts[1]
    end_2 = end_1 + counts[2]
    trial_class = sum((trial >= end).astype(jnp.int32) for end in (end_0, end_1, end_2))
    for q in range(3):
        rows = jnp.concatenate([p[:, q].reshape(32, 128) for p in (part_0, part_1, part_2, part_3)], axis=0)
        if q == 2:
            drop = (lane // 32 == 2) & (trial_class != classes[...])
            rows = jnp.where(drop, 0.0, rows)
            best[...] = jnp.max(rows, axis=0, keepdims=True)[:, 64:96]
        turned = lax.dot_general(
            rows, to_lane, (((0,), (0,)), ((), ())), precision=lax.Precision.HIGHEST, preferred_element_type=jnp.float32
        )
        for k in range(4):
            if 4 * q + k < TERMS:
                coefs[4 * q + k] = turned[k * 32 : (k + 1) * 32]
            elif 4 * q + k == TERMS:
                gains[...] = turned[k * 32 : (k + 1) * 32]


def body(flux, ivar, pixel_mask, exposure_target, basis, trial_counts, target_class):
    pixels = flux.shape[1]
    tmpl, spec, core = (lax.axis_index(a) for a in AXES)
    place = jnp.stack([core, spec % 2, tmpl // 4, tmpl % 4, spec // 2]).astype(jnp.int32)
    smem = pl.BlockSpec(memory_space=pltpu.SMEM)
    vmem = pl.BlockSpec(memory_space=pltpu.VMEM)
    params = pltpu.CompilerParams(vmem_limit_bytes=VMEM)

    trial = pl.pallas_call(
        prep_kernel,
        out_shape=jax.ShapeDtypeStruct((1, TERMS, SLICES, WIDTH), jnp.bfloat16),
        in_specs=[smem, vmem],
        out_specs=vmem,
        scratch_shapes=[pltpu.VMEM((TERMS * SLICES, WIDTH), jnp.float32)],
        compiler_params=params,
        name="prep",
    )(place, basis)
    pair = jnp.concatenate([trial, send(trial, x_hi=1)], axis=0)

    blocks = flux.shape[0] // 16
    weighted = pl.pallas_call(
        weight_kernel,
        out_shape=jax.ShapeDtypeStruct((blocks + 1, 32, pixels), jnp.bfloat16),
        grid=(blocks + 1,),
        in_specs=[
            pl.BlockSpec((16, pixels), lambda i: (jnp.minimum(i, blocks - 1), 0)),
            pl.BlockSpec((16, pixels), lambda i: (jnp.minimum(i, blocks - 1), 0)),
            pl.BlockSpec((16, pixel_mask.shape[1]), lambda i: (jnp.minimum(i, blocks - 1), 0)),
            pl.BlockSpec((1, flux.shape[0]), lambda i: (0, 0)),
        ],
        out_specs=pl.BlockSpec((1, 32, pixels), lambda i: (i, 0, 0)),
        compiler_params=params,
        name="weight",
    )(flux, ivar, pixel_mask, exposure_target.reshape(1, -1))
    weighted_other = send(weighted, core=1)

    eight = jnp.concatenate([pair] + [send(pair, along=0, step=s) for s in (1, -1, 2)], axis=0)

    chunk = 1024
    names = pl.BlockSpec((1, 16, 128), lambda i: (blocks, 0, 0))
    spectra = pl.BlockSpec((blocks + 1, 32, chunk), lambda i: (0, 0, i))
    coadd = pl.BlockSpec((64, chunk), lambda i: (0, i))
    coadd_shape = jax.ShapeDtypeStruct((64, pixels), jnp.bfloat16)
    own_ivar, own_wflux, outgoing = pl.pallas_call(
        coadd_kernel,
        out_shape=(coadd_shape,) * 3,
        grid=(pl.cdiv(pixels, chunk),),
        in_specs=[smem, names, names, spectra, spectra],
        out_specs=(coadd,) * 3,
        compiler_params=params,
        name="coadd",
    )(place, weighted, weighted_other, weighted, weighted_other)
    direct = send(outgoing, x_lo=1)
    swapped = send(direct, core=1)

    up, down = (send(eight, along=1, step=s) for s in (1, -1))
    far_a = send(up[:4], along=1, step=1)
    far_b = send(down[4:], along=1, step=-1)

    def fit_scratch(count):
        return [
            pltpu.VMEM((count, HALVES, 16 * SLICES, WIDTH), jnp.bfloat16),
            pltpu.VMEM((count, HALVES, 16 * SLICES, WIDTH), jnp.bfloat16),
            pltpu.VMEM((count, ROWS, 128), jnp.float32),
        ]

    first = pl.pallas_call(
        first_fit_kernel,
        out_shape=jax.ShapeDtypeStruct((4, 3, 3, 8, 128), jnp.float32),
        in_specs=[smem] + [vmem] * 7,
        out_specs=vmem,
        scratch_shapes=fit_scratch(3),
        compiler_params=params,
        name="first_fit",
    )(place, eight, up, down, own_ivar, own_wflux, direct, swapped)
    parts = pl.pallas_call(
        last_fit_kernel,
        out_shape=(jax.ShapeDtypeStruct((4, 3, 8, 128), jnp.float32),) * 4,
        in_specs=[smem] + [vmem] * 7,
        out_specs=(vmem,) * 4,
        scratch_shapes=fit_scratch(1),
        compiler_params=params,
        name="last_fit",
    )(place, first, far_a, far_b, own_ivar, own_wflux, direct, swapped)

    parts = (
        parts[0],
        send(parts[1], core=1),
        send(parts[2], x_lo=1),
        send(parts[3], x_lo=1, core=1),
    )
    coefs, gains, best = pl.pallas_call(
        final_kernel,
        out_shape=(
            jax.ShapeDtypeStruct((TERMS, 32, 128), jnp.float32),
            jax.ShapeDtypeStruct((32, 128), jnp.float32),
            jax.ShapeDtypeStruct((1, 32), jnp.float32),
        ),
        in_specs=[smem, smem] + [vmem] * 5,
        out_specs=(vmem,) * 3,
        compiler_params=params,
        name="final",
    )(place, trial_counts, jnp.tile(target_class, 4).reshape(1, 128), *parts)
    return coefs, gains, best.reshape(32)


def solution(mesh):
    rows = P(AXES, None)
    return jax.shard_map(
        body,
        mesh=mesh,
        in_specs=(rows, rows, rows, P(AXES), P(("tmpl", "spec"), None, None), P(), P(AXES)),
        out_specs=(P(None, AXES, None), P(AXES, None), P(AXES)),
        check_vma=False,
    )
```

time: 945 us -> 110 us (0.12)
  waiting for transfers between devices: 696 us -> 24 us
  local copies, waits for them, and re-layouts: 136 us -> 14.7 us
  matrix products: 83.1 us -> 0 us
  Pallas kernels: 0 us -> 44.2 us
  starting transfers between devices: 0.12 us -> 24.4 us
  between operations: 14.6 us -> 0.72 us
  other arithmetic: 12.4 us -> 0.95 us
    all_gather x3 -> x0, waiting for transfers between devices: 695 us -> none  [the longest x1 687 us: body(): basis_piece = lax.all_gather(basis, ('tmpl', 'spec'), axis=0, tiled=True)]
    gather x6 -> x0, local copies, waits for them, and re-layouts: 108 us -> none  [the longest x4 62.1 us: fit_block(): trial_block[:, leading, :].astype(jnp.float32)]
    dot_general x3 -> x0, matrix products: 83.1 us -> none  [the longest x1 68.2 us: fit_block(): jnp.einsum('tp,gqp->qtg', coadd_ivar, products, preferred_element_type=jn...]
    pallas_call x0 -> x6, Pallas kernels: none -> 44.2 us  [the longest x1 17.1 us: body(): pl.pallas_call(first_fit_kernel, out_shape=jax.ShapeDtypeStruct((4, 3, 3,...]
    ppermute x0 -> x14, starting transfers between devices: none -> 24.4 us  [send(): return lax.ppermute(value, AXES, [(d, moved(d, **how)) for d in range(128)])]
    ppermute x0 -> x14, waiting for transfers between devices: none -> 24 us  [send(): return lax.ppermute(value, AXES, [(d, moved(d, **how)) for d in range(128)])]
    all_gather x1 -> x0, local copies, waits for them, and re-layouts: 22.1 us -> none  [body(): basis_piece = lax.all_gather(basis, ('tmpl', 'spec'), axis=0, tiled=True)]
  transfers between devices with their start and end apart: 3 -> 14, of which waited for: 2 -> 5; matrix products, arithmetic and copies ran while one was open for 22% -> 8% of each run, Pallas kernels for 0% -> 25%
where the time goes in v1:
time: 110 us; the launch traced here: 109 us
  Pallas kernels  44.2 us (40%)
  starting transfers between devices  24.4 us (22%)
  waiting for transfers between devices  24 us (22%)
  local copies, waits for them, and re-layouts  14.7 us (13%)
    ppermute x14, starting transfers between devices, send(): return lax.ppermute(value, AXES, [(d, moved(d, **how)) for d in range(128)])  24.4 us
    ppermute x14, waiting for transfers between devices, send(): return lax.ppermute(value, AXES, [(d, moved(d, **how)) for d in range(128)])  24 us
    pallas_call x1, Pallas kernels, body(): pl.pallas_call(first_fit_kernel, out_shape=jax.ShapeDtypeStruct((4, 3, 3,...  17.1 us
    unnamed x28, local copies, waits for them, and re-layouts  12.5 us
    pallas_call x1, Pallas kernels, body(): pl.pallas_call(last_fit_kernel, out_shape=(jax.ShapeDtypeStruct((4, 3, 8,...  9.13 us
    pallas_call x1, Pallas kernels, body(): pl.pallas_call(coadd_kernel, out_shape=(coadd_shape,) * 3, grid=(pl.cdiv(...  7.79 us
    pallas_call x1, Pallas kernels, body(): pl.pallas_call(weight_kernel, out_shape=jax.ShapeDtypeStruct((blocks + 1,...  6.28 us
  transfers between devices with their start and end apart: 14, of which 5 were waited for; matrix products, arithmetic and copies ran while one was open for 8% of the time, Pallas kernels for 25%

profile of v1, /device:TPU:1, one launch (start us, length us, event | category | flops | bytes accessed | tf_op | source)
XLA Modules:
  0.0 109.0 jit_solution(17128793469131191920)
XLA Ops:
  0.6 1.5 %copy.11.mask = s32[96,61]{1,0:T(8,128)} copy(s32[96,61]{0,1:T(8,128)} %param.9) | data formatting | bytes 46848 | tf_op args[2]
  2.1 6.3 %weight.1.own_names.own = bf16[7,32,7808]{2,1,0:T(8,128)(2,1)} custom-call(bf16[96,7808]{1,0:T(8,128)(2,1)} %flux.1, bf16[96,7808]{1,0:T(8,128)(2,1)} %ivar.1, s32[96,61]{1,0:T(8,128)} %copy.11.mask, s32[1,96]{1,0:T(1,128)} %bitcast.7), custom_call_target="tpu_custom_call" | custom-call | tf_op jit(solution)/shard_map/weight/pallas_call | solution.py:284
  8.4 1.4 %collective-permute-start.6 = (bf16[7,32,7808]{2,1,0:T(8,128)(2,1)}, bf16[7,32,7808]{2,1,0:T(8,128)(2,1)S(1)}, u32[]{:S(2)}, u32[]{:S(2)}) collective-permute-start(bf16[7,32,7808]{2,1,0:T(8,128)(2,1)} %weight.1.own_names.own), channel_id=1, source_target_pairs={{0,1},{1,0},{2,3},{3,2},{4,5},{5,4},{6,7},{7,6},{8,9},{9,8},{10,11... | collective-permute-start | bytes 10493960 | tf_op jit(solution)/shard_map/ppermute | solution.py:31
  9.8 1.8 %copy.10.basis = bf16[2,10,7808]{2,1,0:T(8,128)(2,1)} copy(bf16[2,10,7808]{2,0,1:T(2,128)(2,1)} %param.11) | data formatting | bytes 624640 | tf_op args[4]
  11.6 0.7 stack.23.place
  12.3 1.9 %prep.1 = bf16[1,10,16,512]{3,2,1,0:T(8,128)(2,1)} custom-call(s32[5]{0:T(128)} %stack.23.place, bf16[2,10,7808]{2,1,0:T(8,128)(2,1)} %copy.10.basis), custom_call_target="tpu_custom_call" | custom-call | tf_op jit(solution)/shard_map/prep/pallas_call | solution.py:272
  14.2 2.8 %collective-permute-start = (bf16[1,10,16,512]{3,2,1,0:T(8,128)(2,1)}, bf16[1,10,16,512]{3,2,1,0:T(8,128)(2,1)S(1)}, u32[]{:S(2)}, u32[]{:S(2)}) collective-permute-start(bf16[1,10,16,512]{3,2,1,0:T(8,128)(2,1)} %prep.1), channel_id=1, source_target_pairs={{0,64},{1,65},{2,66},{3,67},{4,68},{5,69},{6,70},{7,71},{8,72},{9,... | collective-permute-start | bytes 491528 | tf_op jit(solution)/shard_map/ppermute | solution.py:31
  17.0 4.7 %collective-permute-done = bf16[1,10,16,512]{3,2,1,0:T(8,128)(2,1)S(1)} collective-permute-done((bf16[1,10,16,512]{3,2,1,0:T(8,128)(2,1)}, bf16[1,10,16,512]{3,2,1,0:T(8,128)(2,1)S(1)}, u32[]{:S(2)}, u32[]{:S(2)}) %collective-permute-start) | collective-permute-done | bytes 163872 | tf_op jit(solution)/shard_map/ppermute | solution.py:31
  21.7 0.9 pad_maximum_fusion
  22.7 1.4 %collective-permute-start.1 = (bf16[2,10,16,512]{3,2,1,0:T(8,128)(2,1)S(1)}, bf16[2,10,16,512]{3,2,1,0:T(8,128)(2,1)S(1)}, u32[]{:S(2)}, u32[]{:S(2)}) collective-permute-start(bf16[2,10,16,512]{3,2,1,0:T(8,128)(2,1)S(1)} %pad_maximum_fusion), channel_id=1, source_target_pairs={{0,16},{1,5},{2,18},{3,7},{4,20},{5,9},{6,22},{7,11},{8,24},{9,13}... | collective-permute-start | bytes 983048 | tf_op jit(solution)/shard_map/ppermute | solution.py:31
  24.1 1.5 %collective-permute-start.2 = (bf16[2,10,16,512]{3,2,1,0:T(8,128)(2,1)S(1)}, bf16[2,10,16,512]{3,2,1,0:T(8,128)(2,1)S(1)}, u32[]{:S(2)}, u32[]{:S(2)}) collective-permute-start(bf16[2,10,16,512]{3,2,1,0:T(8,128)(2,1)S(1)} %pad_maximum_fusion), channel_id=1, source_target_pairs={{0,48},{1,13},{2,50},{3,15},{4,52},{5,1},{6,54},{7,3},{8,56},{9,5}... | collective-permute-start | bytes 983048 | tf_op jit(solution)/shard_map/ppermute | solution.py:31
  25.6 1.6 %constant_dynamic-update-slice_fusion.4 = bf16[8,10,16,512]{3,2,1,0:T(8,128)(2,1)} fusion(bf16[1,10,16,512]{3,2,1,0:T(8,128)(2,1)} %prep.1), kind=kLoop, calls=%fused_computation.5 | loop fusion | bytes 327680
  27.2 1.6 %collective-permute-start.3 = (bf16[2,10,16,512]{3,2,1,0:T(8,128)(2,1)S(1)}, bf16[2,10,16,512]{3,2,1,0:T(8,128)(2,1)S(1)}, u32[]{:S(2)}, u32[]{:S(2)}) collective-permute-start(bf16[2,10,16,512]{3,2,1,0:T(8,128)(2,1)S(1)} %pad_maximum_fusion), channel_id=1, source_target_pairs={{0,32},{1,9},{2,34},{3,11},{4,36},{5,13},{6,38},{7,15},{8,40},{9,1... | collective-permute-start | bytes 983048 | tf_op jit(solution)/shard_map/ppermute | solution.py:31
  28.8 0.7 constant_dynamic-update-slice_fusion.3
  29.4 0.9 collective-permute-done.1
  30.3 0.7 constant_dynamic-update-slice_fusion.2
  31.1 0.0 collective-permute-done.2
  31.1 0.8 constant_dynamic-update-slice_fusion.1
  31.9 0.0 collective-permute-done.6.other_names.other
  31.9 1.8 %copy-done = bf16[7,32,7808]{2,1,0:T(8,128)(2,1)} copy-done((bf16[7,32,7808]{2,1,0:T(8,128)(2,1)}, bf16[7,32,7808]{2,1,0:T(8,128)(2,1)S(1)}, u32[]{:S(2)}) %copy-start) | copy-done | bytes 3498008
  33.6 7.8 %coadd.1 = (bf16[64,7808]{1,0:T(8,128)(2,1)}, bf16[64,7808]{1,0:T(8,128)(2,1)}, bf16[64,7808]{1,0:T(8,128)(2,1)}) custom-call(s32[5]{0:T(128)} %stack.23.place, bf16[7,32,7808]{2,1,0:T(8,128)(2,1)} %weight.1.own_names.own, bf16[7,32,7808]{2,1,0:T(8,128)(2,1)} %copy-done, bf16[7,32,7808]{2,1,0:T(8,128)(2,1)} %weight.1.own_names.own, bf16[7,32,7808]{2,1,0:T(8,128)(2,1)} %copy-done), custom_call_target="tpu_custom_call" | custom-call | tf_op jit(solution)/shard_map/coadd/pallas_call | solution.py:307
  41.4 1.2 %collective-permute-start.7 = (bf16[64,7808]{1,0:T(8,128)(2,1)}, bf16[64,7808]{1,0:T(8,128)(2,1)S(1)}, u32[]{:S(2)}, u32[]{:S(2)}) collective-permute-start(bf16[64,7808]{1,0:T(8,128)(2,1)} %get-tuple-element.15), channel_id=1, source_target_pairs={{0,2},{1,3},{2,0},{3,1},{4,6},{5,7},{6,4},{7,5},{8,10},{9,11},{10,... | collective-permute-start | bytes 2998280 | tf_op jit(solution)/shard_map/ppermute | solution.py:31
  42.6 0.0 collective-permute-done.3
  42.6 0.8 constant_dynamic-update-slice_fusion.own
  43.4 3.7 %collective-permute-start.5 = (bf16[8,10,16,512]{3,2,1,0:T(8,128)(2,1)}, bf16[8,10,16,512]{3,2,1,0:T(8,128)(2,1)S(1)}, u32[]{:S(2)}, u32[]{:S(2)}) collective-permute-start(bf16[8,10,16,512]{3,2,1,0:T(8,128)(2,1)} %constant_dynamic-update-slice_fusion.own), channel_id=1, source_target_pairs={{0,12},{1,49},{2,14},{3,51},{4,0},{5,53},{6,2},{7,55},{8,4},{9,57}... | collective-permute-start | bytes 3932168 | tf_op jit(solution)/shard_map/ppermute | solution.py:31
  47.2 0.0 collective-permute-start.4
  47.2 15.7 %collective-permute-done.7.direct = bf16[64,7808]{1,0:T(8,128)(2,1)S(1)} collective-permute-done((bf16[64,7808]{1,0:T(8,128)(2,1)}, bf16[64,7808]{1,0:T(8,128)(2,1)S(1)}, u32[]{:S(2)}, u32[]{:S(2)}) %collective-permute-start.7) | collective-permute-done | bytes 999456 | tf_op jit(solution)/shard_map/ppermute | solution.py:31
  62.8 3.3 %collective-permute-start.8 = (bf16[64,7808]{1,0:T(8,128)(2,1)S(1)}, bf16[64,7808]{1,0:T(8,128)(2,1)S(1)}, u32[]{:S(2)}, u32[]{:S(2)}) collective-permute-start(bf16[64,7808]{1,0:T(8,128)(2,1)S(1)} %collective-permute-done.7.direct), channel_id=1, source_target_pairs={{0,1},{1,0},{2,3},{3,2},{4,5},{5,4},{6,7},{7,6},{8,9},{9,8},{10,11... | collective-permute-start | bytes 2998280 | tf_op jit(solution)/shard_map/ppermute | solution.py:31
  66.2 0.0 collective-permute-done.5.down
  66.2 3.8 %collective-permute-start.10 = (bf16[4,10,16,512]{3,2,1,0:T(8,128)(2,1)S(1)}, bf16[4,10,16,512]{3,2,1,0:T(8,128)(2,1)S(1)}, u32[]{:S(2)}, u32[]{:S(2)}) collective-permute-start(bf16[4,10,16,512]{3,2,1,0:T(8,128)(2,1)S(1)} %slice.9), channel_id=1, source_target_pairs={{0,12},{1,49},{2,14},{3,51},{4,0},{5,53},{6,2},{7,55},{8,4},{9,57}... | collective-permute-start | bytes 1966088 | tf_op jit(solution)/shard_map/ppermute | solution.py:31
  70.0 0.0 collective-permute-done.4.up
  70.1 0.1 collective-permute-start.9
  70.2 0.0 collective-permute-done.8.swapped
  70.2 0.9 copy-done.4
  71.1 0.4 copy-done.2
  71.5 17.1 %first_fit.1.first = f32[4,3,3,8,128]{4,3,2,1,0:T(8,128)} custom-call(s32[5]{0:T(128)} %stack.23.place, bf16[8,10,16,512]{3,2,1,0:T(8,128)(2,1)} %constant_dynamic-update-slice_fusion.own, bf16[8,10,16,512]{3,2,1,0:T(8,128)(2,1)} %copy-done.4, bf16[8,10,16,512]{3,2,1,0:T(8,128)(2,1)} %copy-done.3, bf16[64,7808]{1,0:T(8,128)(2,1)} %get-tuple-element.13.own_ivar, ...), custom_call_target="tpu_custom_call" | custom-call | tf_op jit(solution)/shard_map/first_fit/pallas_call | solution.py:330
  88.6 0.0 collective-permute-done.9.far_a
  88.6 0.9 copy-done.5
  89.4 0.8 copy-done.6
  90.3 9.1 %last_fit.1 = (f32[4,3,8,128]{3,2,1,0:T(8,128)}, f32[4,3,8,128]{3,2,1,0:T(8,128)}, f32[4,3,8,128]{3,2,1,0:T(8,128)}, f32[4,3,8,128]{3,2,1,0:T(8,128)}) custom-call(s32[5]{0:T(128)} %stack.23.place, f32[4,3,3,8,128]{4,3,2,1,0:T(8,128)} %first_fit.1.first, bf16[4,10,16,512]{3,2,1,0:T(8,128)(2,1)} %copy-done.6, bf16[4,10,16,512]{3,2,1,0:T(8,128)(2,1)} %copy-done.5, ...), custom_call_target="tpu_custom_call" | custom-call | tf_op jit(solution)/shard_map/last_fit/pallas_call | solution.py:339
  99.4 1.8 %collective-permute-start.11 = (f32[4,3,8,128]{3,2,1,0:T(8,128)}, f32[4,3,8,128]{3,2,1,0:T(8,128)S(1)}, u32[]{:S(2)}, u32[]{:S(2)}) collective-permute-start(f32[4,3,8,128]{3,2,1,0:T(8,128)} %get-tuple-element.17), channel_id=1, source_target_pairs={{0,1},{1,0},{2,3},{3,2},{4,5},{5,4},{6,7},{7,6},{8,9},{9,8},{10,11... | collective-permute-start | bytes 147464 | tf_op jit(solution)/shard_map/ppermute | solution.py:31
  101.2 1.2 %collective-permute-start.12 = (f32[4,3,8,128]{3,2,1,0:T(8,128)}, f32[4,3,8,128]{3,2,1,0:T(8,128)S(1)}, u32[]{:S(2)}, u32[]{:S(2)}) collective-permute-start(f32[4,3,8,128]{3,2,1,0:T(8,128)} %get-tuple-element.18), channel_id=1, source_target_pairs={{0,2},{1,3},{2,0},{3,1},{4,6},{5,7},{6,4},{7,5},{8,10},{9,11},{10,... | collective-permute-start | bytes 147464 | tf_op jit(solution)/shard_map/ppermute | solution.py:31
  102.4 0.5 collective-permute-start.13
  102.9 0.7 reshape_tile.3.classes
  103.6 0.8 collective-permute-done.12.part_2
  104.4 2.0 %collective-permute-done.13.part_3 = f32[4,3,8,128]{3,2,1,0:T(8,128)S(1)} collective-permute-done((f32[4,3,8,128]{3,2,1,0:T(8,128)}, f32[4,3,8,128]{3,2,1,0:T(8,128)S(1)}, u32[]{:S(2)}, u32[]{:S(2)}) %collective-permute-start.13) | collective-permute-done | bytes 49184 | tf_op jit(solution)/shard_map/ppermute | solution.py:31
  106.3 0.6 copy-done.9
  107.0 2.0 %final.1 = (f32[10,32,128]{2,1,0:T(8,128)}, f32[32,128]{1,0:T(8,128)}, f32[1,32]{1,0:T(1,128)}) custom-call(s32[5]{0:T(128)} %stack.23.place, s32[3]{0:T(128)} %counts.1, s32[1,128]{1,0:T(1,128)} %reshape_tile.3.classes, f32[4,3,8,128]{3,2,1,0:T(8,128)} %get-tuple-element.16.part_0, f32[4,3,8,128]{3,2,1,0:T(8,128)} %copy-done.7, f32[4,3,8,128]{3,2,1,0:T(8,128)} %copy-done.8, ...), custom_call_target="tpu_custom_call" | custom-call | tf_op jit(solution)/shard_map/final/pallas_call | solution.py:355
  (21 shorter events, 0.1 us)
Async XLA Ops:
  8.4 23.5 %collective-permute-start.6 = (bf16[7,32,7808]{2,1,0:T(8,128)(2,1)}, bf16[7,32,7808]{2,1,0:T(8,128)(2,1)S(1)}, u32[]{:S(2)}, u32[]{:S(2)}) collective-permute-start(bf16[7,32,7808]{2,1,0:T(8,128)(2,1)} %weight.1.own_names.own), channel_id=1, source_target_pairs={{0,1},{1,0},{2,3},{3,2},{4,5},{5,4},{6,7},{7,6},{8,9},{9,8},{10,11... | collective-permute-start | bytes 10493960 | tf_op jit(solution)/shard_map/ppermute | solution.py:31
  14.2 7.5 %collective-permute-start = (bf16[1,10,16,512]{3,2,1,0:T(8,128)(2,1)}, bf16[1,10,16,512]{3,2,1,0:T(8,128)(2,1)S(1)}, u32[]{:S(2)}, u32[]{:S(2)}) collective-permute-start(bf16[1,10,16,512]{3,2,1,0:T(8,128)(2,1)} %prep.1), channel_id=1, source_target_pairs={{0,64},{1,65},{2,66},{3,67},{4,68},{5,69},{6,70},{7,71},{8,72},{9,... | collective-permute-start | bytes 491528 | tf_op jit(solution)/shard_map/ppermute | solution.py:31
  22.7 7.6 %collective-permute-start.1 = (bf16[2,10,16,512]{3,2,1,0:T(8,128)(2,1)S(1)}, bf16[2,10,16,512]{3,2,1,0:T(8,128)(2,1)S(1)}, u32[]{:S(2)}, u32[]{:S(2)}) collective-permute-start(bf16[2,10,16,512]{3,2,1,0:T(8,128)(2,1)S(1)} %pad_maximum_fusion), channel_id=1, source_target_pairs={{0,16},{1,5},{2,18},{3,7},{4,20},{5,9},{6,22},{7,11},{8,24},{9,13}... | collective-permute-start | bytes 983048 | tf_op jit(solution)/shard_map/ppermute | solution.py:31
  24.1 6.9 %collective-permute-start.2 = (bf16[2,10,16,512]{3,2,1,0:T(8,128)(2,1)S(1)}, bf16[2,10,16,512]{3,2,1,0:T(8,128)(2,1)S(1)}, u32[]{:S(2)}, u32[]{:S(2)}) collective-permute-start(bf16[2,10,16,512]{3,2,1,0:T(8,128)(2,1)S(1)} %pad_maximum_fusion), channel_id=1, source_target_pairs={{0,48},{1,13},{2,50},{3,15},{4,52},{5,1},{6,54},{7,3},{8,56},{9,5}... | collective-permute-start | bytes 983048 | tf_op jit(solution)/shard_map/ppermute | solution.py:31
  27.2 15.4 %collective-permute-start.3 = (bf16[2,10,16,512]{3,2,1,0:T(8,128)(2,1)S(1)}, bf16[2,10,16,512]{3,2,1,0:T(8,128)(2,1)S(1)}, u32[]{:S(2)}, u32[]{:S(2)}) collective-permute-start(bf16[2,10,16,512]{3,2,1,0:T(8,128)(2,1)S(1)} %pad_maximum_fusion), channel_id=1, source_target_pairs={{0,32},{1,9},{2,34},{3,11},{4,36},{5,13},{6,38},{7,15},{8,40},{9,1... | collective-permute-start | bytes 983048 | tf_op jit(solution)/shard_map/ppermute | solution.py:31
  31.9 1.8 %copy-start = (bf16[7,32,7808]{2,1,0:T(8,128)(2,1)}, bf16[7,32,7808]{2,1,0:T(8,128)(2,1)S(1)}, u32[]{:S(2)}) copy-start(bf16[7,32,7808]{2,1,0:T(8,128)(2,1)S(1)} %collective-permute-done.6.other_names.other) | copy-start | bytes 10493956
  41.4 21.4 %collective-permute-start.7 = (bf16[64,7808]{1,0:T(8,128)(2,1)}, bf16[64,7808]{1,0:T(8,128)(2,1)S(1)}, u32[]{:S(2)}, u32[]{:S(2)}) collective-permute-start(bf16[64,7808]{1,0:T(8,128)(2,1)} %get-tuple-element.15), channel_id=1, source_target_pairs={{0,2},{1,3},{2,0},{3,1},{4,6},{5,7},{6,4},{7,5},{8,10},{9,11},{10,... | collective-permute-start | bytes 2998280 | tf_op jit(solution)/shard_map/ppermute | solution.py:31
  43.4 22.7 %collective-permute-start.5 = (bf16[8,10,16,512]{3,2,1,0:T(8,128)(2,1)}, bf16[8,10,16,512]{3,2,1,0:T(8,128)(2,1)S(1)}, u32[]{:S(2)}, u32[]{:S(2)}) collective-permute-start(bf16[8,10,16,512]{3,2,1,0:T(8,128)(2,1)} %constant_dynamic-update-slice_fusion.own), channel_id=1, source_target_pairs={{0,12},{1,49},{2,14},{3,51},{4,0},{5,53},{6,2},{7,55},{8,4},{9,57}... | collective-permute-start | bytes 3932168 | tf_op jit(solution)/shard_map/ppermute | solution.py:31
  47.2 22.9 %collective-permute-start.4 = (bf16[8,10,16,512]{3,2,1,0:T(8,128)(2,1)}, bf16[8,10,16,512]{3,2,1,0:T(8,128)(2,1)S(1)}, u32[]{:S(2)}, u32[]{:S(2)}) collective-permute-start(bf16[8,10,16,512]{3,2,1,0:T(8,128)(2,1)} %constant_dynamic-update-slice_fusion.own), channel_id=1, source_target_pairs={{0,4},{1,17},{2,6},{3,19},{4,8},{5,21},{6,10},{7,23},{8,12},{9,25}... | collective-permute-start | bytes 3932168 | tf_op jit(solution)/shard_map/ppermute | solution.py:31
  62.8 7.2 %copy-start.1 = (bf16[64,7808]{1,0:T(8,128)(2,1)}, bf16[64,7808]{1,0:T(8,128)(2,1)S(1)}, u32[]{:S(2)}) copy-start(bf16[64,7808]{1,0:T(8,128)(2,1)S(1)} %collective-permute-done.7.direct) | copy-start | bytes 2998276
  62.8 7.3 %collective-permute-start.8 = (bf16[64,7808]{1,0:T(8,128)(2,1)S(1)}, bf16[64,7808]{1,0:T(8,128)(2,1)S(1)}, u32[]{:S(2)}, u32[]{:S(2)}) collective-permute-start(bf16[64,7808]{1,0:T(8,128)(2,1)S(1)} %collective-permute-done.7.direct), channel_id=1, source_target_pairs={{0,1},{1,0},{2,3},{3,2},{4,5},{5,4},{6,7},{7,6},{8,9},{9,8},{10,11... | collective-permute-start | bytes 2998280 | tf_op jit(solution)/shard_map/ppermute | solution.py:31
  66.2 3.9 %copy-start.3 = (bf16[8,10,16,512]{3,2,1,0:T(8,128)(2,1)}, bf16[8,10,16,512]{3,2,1,0:T(8,128)(2,1)S(1)}, u32[]{:S(2)}) copy-start(bf16[8,10,16,512]{3,2,1,0:T(8,128)(2,1)S(1)} %collective-permute-done.5.down) | copy-start | bytes 3932164
  66.2 22.4 %collective-permute-start.10 = (bf16[4,10,16,512]{3,2,1,0:T(8,128)(2,1)S(1)}, bf16[4,10,16,512]{3,2,1,0:T(8,128)(2,1)S(1)}, u32[]{:S(2)}, u32[]{:S(2)}) collective-permute-start(bf16[4,10,16,512]{3,2,1,0:T(8,128)(2,1)S(1)} %slice.9), channel_id=1, source_target_pairs={{0,12},{1,49},{2,14},{3,51},{4,0},{5,53},{6,2},{7,55},{8,4},{9,57}... | collective-permute-start | bytes 1966088 | tf_op jit(solution)/shard_map/ppermute | solution.py:31
  70.0 1.1 copy-start.4
  70.1 18.5 %collective-permute-start.9 = (bf16[4,10,16,512]{3,2,1,0:T(8,128)(2,1)S(1)}, bf16[4,10,16,512]{3,2,1,0:T(8,128)(2,1)S(1)}, u32[]{:S(2)}, u32[]{:S(2)}) collective-permute-start(bf16[4,10,16,512]{3,2,1,0:T(8,128)(2,1)S(1)} %slice.8), channel_id=1, source_target_pairs={{0,4},{1,17},{2,6},{3,19},{4,8},{5,21},{6,10},{7,23},{8,12},{9,25}... | collective-permute-start | bytes 1966088 | tf_op jit(solution)/shard_map/ppermute | solution.py:31
  70.2 1.3 %copy-start.2 = (bf16[64,7808]{1,0:T(8,128)(2,1)}, bf16[64,7808]{1,0:T(8,128)(2,1)S(1)}, u32[]{:S(2)}) copy-start(bf16[64,7808]{1,0:T(8,128)(2,1)S(1)} %collective-permute-done.8.swapped) | copy-start | bytes 2998276
  88.6 14.3 %copy-start.10 = (s32[32]{0:T(128)S(1)}, s32[32]{0:T(128)}, u32[]{:S(2)}) copy-start(s32[32]{0:T(128)} %param.13) | copy-start | bytes 388
  88.6 0.9 copy-start.5
  89.4 0.8 copy-start.6
  99.4 4.2 %collective-permute-start.11 = (f32[4,3,8,128]{3,2,1,0:T(8,128)}, f32[4,3,8,128]{3,2,1,0:T(8,128)S(1)}, u32[]{:S(2)}, u32[]{:S(2)}) collective-permute-start(f32[4,3,8,128]{3,2,1,0:T(8,128)} %get-tuple-element.17), channel_id=1, source_target_pairs={{0,1},{1,0},{2,3},{3,2},{4,5},{5,4},{6,7},{7,6},{8,9},{9,8},{10,11... | collective-permute-start | bytes 147464 | tf_op jit(solution)/shard_map/ppermute | solution.py:31
  101.2 3.2 %collective-permute-start.12 = (f32[4,3,8,128]{3,2,1,0:T(8,128)}, f32[4,3,8,128]{3,2,1,0:T(8,128)S(1)}, u32[]{:S(2)}, u32[]{:S(2)}) collective-permute-start(f32[4,3,8,128]{3,2,1,0:T(8,128)} %get-tuple-element.18), channel_id=1, source_target_pairs={{0,2},{1,3},{2,0},{3,1},{4,6},{5,7},{6,4},{7,5},{8,10},{9,11},{10,... | collective-permute-start | bytes 147464 | tf_op jit(solution)/shard_map/ppermute | solution.py:31
  102.4 3.9 %collective-permute-start.13 = (f32[4,3,8,128]{3,2,1,0:T(8,128)}, f32[4,3,8,128]{3,2,1,0:T(8,128)S(1)}, u32[]{:S(2)}, u32[]{:S(2)}) collective-permute-start(f32[4,3,8,128]{3,2,1,0:T(8,128)} %get-tuple-element.19), channel_id=1, source_target_pairs={{0,3},{1,2},{2,1},{3,0},{4,7},{5,6},{6,5},{7,4},{8,11},{9,10},{10,... | collective-permute-start | bytes 147464 | tf_op jit(solution)/shard_map/ppermute | solution.py:31
  103.6 2.8 %copy-start.7 = (f32[4,3,8,128]{3,2,1,0:T(8,128)}, f32[4,3,8,128]{3,2,1,0:T(8,128)S(1)}, u32[]{:S(2)}) copy-start(f32[4,3,8,128]{3,2,1,0:T(8,128)S(1)} %collective-permute-done.11.part_1) | copy-start | bytes 147460
  104.4 2.0 %copy-start.8 = (f32[4,3,8,128]{3,2,1,0:T(8,128)}, f32[4,3,8,128]{3,2,1,0:T(8,128)S(1)}, u32[]{:S(2)}) copy-start(f32[4,3,8,128]{3,2,1,0:T(8,128)S(1)} %collective-permute-done.12.part_2) | copy-start | bytes 147460
  106.3 0.6 copy-start.9

commit v2 on v1

v2 whole, which is shorter than its diff:
```python
import jax
import jax.numpy as jnp
import numpy as np
from jax import lax
from jax.experimental import pallas as pl
from jax.experimental.pallas import tpu as pltpu
from jax.sharding import PartitionSpec as P

AXES = ("tmpl", "spec", "expo")
SIDES = (2, 4, 4, 2, 2)
TERMS = 10
HALVES = TERMS // 2
SLICES = 16
WIDTH = 512
COMBOS = 30
ROWS = COMBOS * 16 + TERMS * 8
VMEM = 24 * 1024 * 1024


def moved(device, core=0, x_lo=0, x_hi=0, along=None, step=0):
    h, z, y, lo, c = (int(v) for v in np.unravel_index(device, SIDES))
    if along is not None:
        if (c == 0) == (along == 0):
            z = (z + step) % 4
        else:
            y = (y + step) % 4
    return int(np.ravel_multi_index((h ^ x_hi, z, y, lo ^ x_lo, c ^ core), SIDES))


def send(value, **how):
    return lax.ppermute(value, AXES, [(d, moved(d, **how)) for d in range(128)])


def combos():
    out = [(m, n, 0) for m in range(HALVES) for n in range(m + 1, HALVES)]
    out += [(m, n, 1) for m in range(HALVES) for n in range(m + 1, HALVES)]
    out += [(m, m, 0) for m in range(HALVES)]
    out += [(m, m, 1) for m in range(HALVES)]
    return out


def entry_rows():
    where = {}
    for i, (m, n, crossed) in enumerate(combos()):
        for half in range(2):
            k, l = 2 * m + half, 2 * n + (half ^ crossed)
            where.setdefault((min(k, l), max(k, l)), i * 16 + half * 8)
    return where


def prep_kernel(place, basis, out, rows):
    core = place[0]
    pixels = basis.shape[2]
    tail = pixels - (SLICES - 1) * WIDTH
    rows[...] = jnp.zeros_like(rows)
    for k in range(TERMS):
        both = basis[k].astype(jnp.float32)
        mine = jnp.where(core == 0, both[0:1], both[1:2])
        for h in range(SLICES):
            width = WIDTH if h < SLICES - 1 else tail
            rows[k * SLICES + h : k * SLICES + h + 1, :width] = mine[:, h * WIDTH : h * WIDTH + width]
    out[...] = rows[...].astype(jnp.bfloat16).reshape(out.shape)


def weight_kernel(place, flux, ivar, mask, owner, keep, out, good):
    step, steps = pl.program_id(0), pl.num_programs(0)
    core = place[0]
    height = flux.shape[0]

    @pl.when(step == 0)
    def _():
        good[...] = mask[...].astype(jnp.float32).T

    @pl.when(step < steps - 1)
    def _():
        flags = good[pl.ds(pl.multiple_of(step * height, height), height), :]
        for b in range(flags.shape[1]):
            lanes = slice(b * 128, (b + 1) * 128)
            flag = jnp.broadcast_to(flags[:, b : b + 1], (height, 128)).astype(jnp.bfloat16)
            masked = ivar[:, lanes] * flag
            wide = masked.astype(jnp.float32)
            fluxes = wide * flux[:, lanes].astype(jnp.float32)
            keep[:, lanes] = jnp.where(core == 0, wide, fluxes).astype(jnp.bfloat16)
            out[:, lanes] = jnp.where(core == 0, fluxes, wide).astype(jnp.bfloat16)

    @pl.when(step == steps - 1)
    def _():
        names = owner[...].astype(jnp.float32)
        out[0:16, :] = jnp.zeros((16, out.shape[1]), jnp.bfloat16)
        out[0:16, 0 : names.shape[1]] = jnp.broadcast_to(names, (16, names.shape[1])).astype(jnp.bfloat16)


def coadd_kernel(place, own_names, other_names, own, other, coadd):
    core = place[0]
    count = own.shape[0]
    row = lax.broadcasted_iota(jnp.int32, (64, count), 0)
    wanted = jnp.where(row < 32, row + core * 32, row - core * 32).astype(jnp.float32)
    near = (own_names[...].astype(jnp.float32) == wanted).astype(jnp.float32)
    far = (other_names[0:1, 0:count].astype(jnp.float32) == wanted).astype(jnp.float32)
    select = jnp.concatenate([near, far], axis=1).astype(jnp.bfloat16)
    spectra = jnp.concatenate([own[...], other[...]], axis=0)
    coadd[...] = jnp.dot(select, spectra, preferred_element_type=jnp.float32).astype(jnp.bfloat16)


def join_kernel(own, up, down, far, out):
    side = SLICES * 16
    row = lax.broadcasted_iota(jnp.int32, (side, side), 0)
    col = lax.broadcasted_iota(jnp.int32, (side, side), 1)
    same = ((row // 16) == (col % 16)) & ((row % 8) == (col // 32)) & ((row // 8) % 2 == (col // 16) % 2)
    order = same.astype(jnp.float32).astype(jnp.bfloat16)
    for m in range(HALVES):
        block = jnp.concatenate(
            [p[:, 2 * m : 2 * m + 2].reshape(p.shape[0] * 2 * SLICES, WIDTH) for p in (own, up, down, far)], axis=0
        )
        turned = jnp.dot(order, block, preferred_element_type=jnp.float32).astype(jnp.bfloat16)
        out[:, m] = turned.reshape(SLICES, 16, WIDTH)


def solve(entries, right):
    lower, scaled, inverse = {}, {}, []
    for j in range(TERMS):
        pivot = entries[j, j]
        for e in range(j):
            pivot = pivot - lower[j, e] * scaled[j, e]
        inverse.append(1.0 / pivot)
        for i in range(j + 1, TERMS):
            value = entries[j, i]
            for e in range(j):
                value = value - lower[i, e] * scaled[j, e]
            scaled[i, j] = value
            lower[i, j] = value * inverse[j]
    forward = []
    for i in range(TERMS):
        value = right[i]
        for e in range(i):
            value = value - lower[i, e] * forward[e]
        forward.append(value)
    answer = [None] * TERMS
    for i in reversed(range(TERMS)):
        value = forward[i] * inverse[i]
        for e in range(i + 1, TERMS):
            value = value - lower[e, i] * answer[e]
        answer[i] = value
    return answer


def fit_blocks(core, blocks, mine, direct, over, swapped, total):
    pixels = mine.shape[1]
    contract = (((1,), (1,)), ((), ()))

    def one_slice(h, segment, at, width, first):
        static = isinstance(h, int)
        lanes = pl.ds(h * WIDTH if static else pl.multiple_of(h * WIDTH, WIDTH), width)
        near = jnp.concatenate([mine[:, lanes], direct[:, lanes]], axis=0)
        far = jnp.concatenate(
            [over[32:64, lanes], over[0:32, lanes], swapped[32:64, lanes], swapped[0:32, lanes]], axis=0
        )
        ivar = jnp.where(core == 0, near, far)
        wflux = jnp.where(core == 0, far, near)
        for b, refs in enumerate(blocks):
            evens = [refs[segment][at, m, :, 0:width] for m in range(HALVES)]
            odds = [jnp.concatenate([e[8:16], e[0:8]], axis=0) for e in evens]
            products = jnp.concatenate(
                [evens[m] * (odds[n] if cross else evens[n]) for m, n, cross in combos()], axis=0
            )
            normal = lax.dot_general(products, ivar, contract, preferred_element_type=jnp.float32)
            project = lax.dot_general(
                jnp.concatenate(evens, axis=0), wflux, contract, preferred_element_type=jnp.float32
            )
            if first:
                total[b, 0 : COMBOS * 16] = normal
                total[b, COMBOS * 16 : ROWS] = project
            else:
                total[b, 0 : COMBOS * 16] += normal
                total[b, COMBOS * 16 : ROWS] += project

    full = pixels // WIDTH
    segments = len(blocks[0])
    per = SLICES // segments
    one_slice(0, 0, 0, WIDTH, True)
    for segment in range(segments):

        def step(h, carry, segment=segment):
            one_slice(h, segment, h - segment * per, WIDTH, False)
            return carry

        lax.fori_loop(max(1, segment * per), min(full, (segment + 1) * per), step, 0)
    if pixels > full * WIDTH:
        one_slice(full, full // per, full % per, pixels - full * WIDTH, False)

    entries = {}
    for (k, l), at in entry_rows().items():
        value = total[:, at : at + 8, :]
        entries[k, l] = value + 1.0 if k == l else value
    right = [total[:, COMBOS * 16 + k * 8 : COMBOS * 16 + k * 8 + 8, :] for k in range(TERMS)]
    answer = solve(entries, right)
    gain = right[0] * answer[0]
    for k in range(1, TERMS):
        gain = gain + right[k] * answer[k]
    values = answer + [gain / TERMS, jnp.zeros_like(gain)]
    lane = lax.broadcasted_iota(jnp.int32, values[0].shape, 2) // 32
    packed = []
    for group in range(4):
        packed.append([])
        for q in range(3):
            out = None
            for k in range(4):
                shift = (k - group) % 4 * 32
                value = values[4 * q + k]
                value = pltpu.roll(value, shift, 2) if shift else value
                out = value if out is None else jnp.where(lane == k, value, out)
            packed[-1].append(out)
    return packed


def first_fit_kernel(place, own, up, down, mine, direct, over, swapped, out, total):
    packed = fit_blocks(place[0], [[own], [up], [down]], mine, direct, over, swapped, total)
    for group in range(4):
        for q in range(3):
            out[group, :, q] = packed[group][q]


def last_fit_kernel(place, first, far_a, far_b, mine, direct, over, swapped, *rest):
    outs, total = rest[:4], rest[4]
    packed = fit_blocks(place[0], [[far_a, far_b]], mine, direct, over, swapped, total)
    for group in range(4):
        outs[group][0:3] = first[group]
        for q in range(3):
            outs[group][3:4, q] = packed[group][q]


def final_kernel(place, counts, classes, part_0, part_1, part_2, part_3, coefs, gains, best):
    core, lo, hi, z, y = (place[i] for i in range(5))

    def shift(n):
        return jnp.where(n == 1, 3, jnp.where(n == 2, 1, jnp.where(n == 3, 2, 0)))

    def trial_of(i):
        group, b, t = i // 32, (i // 8) % 4, i % 8
        source_core = core ^ (group % 2)
        source_lo = lo ^ (group // 2)
        near, far = shift(t // 2), shift(b)
        z_of = (z + jnp.where(source_core == 0, near, far)) % 4
        y_of = (y + jnp.where(source_core == 0, far, near)) % 4
        return (hi ^ (t % 2)) * 64 + z_of * 16 + y_of * 4 + source_lo * 2 + source_core

    trial = trial_of(lax.broadcasted_iota(jnp.int32, (128, 128), 0))
    lane = lax.broadcasted_iota(jnp.int32, (128, 128), 1)
    to_lane = (trial == lane).astype(jnp.float32)
    end_0 = counts[0]
    end_1 = end_0 + counts[1]
    end_2 = end_1 + counts[2]
    trial_class = sum((trial >= end).astype(jnp.int32) for end in (end_0, end_1, end_2))
    for q in range(3):
        rows = jnp.concatenate([p[:, q].reshape(32, 128) for p in (part_0, part_1, part_2, part_3)], axis=0)
        if q == 2:
            drop = (lane // 32 == 2) & (trial_class != classes[...])
            rows = jnp.where(drop, 0.0, rows)
            best[...] = jnp.max(rows, axis=0, keepdims=True)[:, 64:96]
        turned = lax.dot_general(
            rows, to_lane, (((0,), (0,)), ((), ())), precision=lax.Precision.HIGHEST, preferred_element_type=jnp.float32
        )
        for k in range(4):
            if 4 * q + k < TERMS:
                coefs[4 * q + k] = turned[k * 32 : (k + 1) * 32]
            elif 4 * q + k == TERMS:
                gains[...] = turned[k * 32 : (k + 1) * 32]


def body(flux, ivar, pixel_mask, exposure_target, basis, trial_counts, target_class):
    pixels = flux.shape[1]
    tmpl, spec, core = (lax.axis_index(a) for a in AXES)
    place = jnp.stack([core, spec % 2, tmpl // 4, tmpl % 4, spec // 2]).astype(jnp.int32)
    smem = pl.BlockSpec(memory_space=pltpu.SMEM)
    vmem = pl.BlockSpec(memory_space=pltpu.VMEM)
    params = pltpu.CompilerParams(vmem_limit_bytes=VMEM)

    trial = pl.pallas_call(
        prep_kernel,
        out_shape=jax.ShapeDtypeStruct((1, TERMS, SLICES, WIDTH), jnp.bfloat16),
        in_specs=[smem, vmem],
        out_specs=vmem,
        scratch_shapes=[pltpu.VMEM((TERMS * SLICES, WIDTH), jnp.float32)],
        compiler_params=params,
        name="prep",
    )(place, jnp.transpose(basis, (1, 0, 2)))
    pair = jnp.concatenate([trial, send(trial, x_hi=1)], axis=0)

    trial, flux = lax.optimization_barrier((trial, flux))
    count = flux.shape[0]
    height = 32
    steps = count // height
    spectra = pl.BlockSpec((height, pixels), lambda i: (jnp.minimum(i, steps - 1), 0))
    owners = exposure_target.reshape(1, count)
    keep, outgoing = pl.pallas_call(
        weight_kernel,
        out_shape=(
            jax.ShapeDtypeStruct((count, pixels), jnp.bfloat16),
            jax.ShapeDtypeStruct((count + 16, pixels), jnp.bfloat16),
        ),
        grid=(steps + 1,),
        in_specs=[
            smem,
            spectra,
            spectra,
            pl.BlockSpec((pixel_mask.shape[1], count), lambda i: (0, 0)),
            pl.BlockSpec((1, count), lambda i: (0, 0)),
        ],
        out_specs=(spectra, pl.BlockSpec((height, pixels), lambda i: (i, 0))),
        scratch_shapes=[pltpu.VMEM((count, pixel_mask.shape[1]), jnp.float32)],
        compiler_params=params,
        name="weight",
    )(place, flux, ivar, pixel_mask.T, owners)
    incoming = send(outgoing, core=1)

    near = [pair] + [send(pair, along=0, step=s) for s in (1, -1, 2)]

    chunk = 2048
    rows = pl.BlockSpec((count, chunk), lambda i: (0, i))
    mine = pl.pallas_call(
        coadd_kernel,
        out_shape=jax.ShapeDtypeStruct((64, pixels), jnp.bfloat16),
        grid=(pl.cdiv(pixels, chunk),),
        in_specs=[
            smem,
            pl.BlockSpec((1, count), lambda i: (0, 0)),
            pl.BlockSpec((16, 128), lambda i: (count // 16, 0)),
            rows,
            rows,
        ],
        out_specs=pl.BlockSpec((64, chunk), lambda i: (0, i)),
        compiler_params=params,
        name="coadd",
    )(place, owners, incoming, keep, incoming)
    direct = send(mine, x_lo=1)
    over = send(mine, core=1)
    swapped = send(direct, core=1)

    eight = pl.pallas_call(
        join_kernel,
        out_shape=jax.ShapeDtypeStruct((SLICES, HALVES, 16, WIDTH), jnp.bfloat16),
        in_specs=[vmem] * 4,
        out_specs=vmem,
        compiler_params=params,
        name="join",
    )(*near)
    up, down = (send(eight, along=1, step=s) for s in (1, -1))
    far_a = send(up[: SLICES // 2], along=1, step=1)
    far_b = send(down[SLICES // 2 :], along=1, step=-1)

    first = pl.pallas_call(
        first_fit_kernel,
        out_shape=jax.ShapeDtypeStruct((4, 3, 3, 8, 128), jnp.float32),
        in_specs=[smem] + [vmem] * 7,
        out_specs=vmem,
        scratch_shapes=[pltpu.VMEM((3, ROWS, 128), jnp.float32)],
        compiler_params=params,
        name="first_fit",
    )(place, eight, up, down, mine, direct, over, swapped)
    parts = pl.pallas_call(
        last_fit_kernel,
        out_shape=(jax.ShapeDtypeStruct((4, 3, 8, 128), jnp.float32),) * 4,
        in_specs=[smem] + [vmem] * 7,
        out_specs=(vmem,) * 4,
        scratch_shapes=[pltpu.VMEM((1, ROWS, 128), jnp.float32)],
        compiler_params=params,
        name="last_fit",
    )(place, first, far_a, far_b, mine, direct, over, swapped)

    parts = (
        parts[0],
        send(parts[1], core=1),
        send(parts[2], x_lo=1),
        send(parts[3], x_lo=1, core=1),
    )
    coefs, gains, best = pl.pallas_call(
        final_kernel,
        out_shape=(
            jax.ShapeDtypeStruct((TERMS, 32, 128), jnp.float32),
            jax.ShapeDtypeStruct((32, 128), jnp.float32),
            jax.ShapeDtypeStruct((1, 32), jnp.float32),
        ),
        in_specs=[smem, smem] + [vmem] * 5,
        out_specs=(vmem,) * 3,
        compiler_params=params,
        name="final",
    )(place, trial_counts, jnp.tile(target_class, 4).reshape(1, 128), *parts)
    return coefs, gains, best.reshape(32)


def solution(mesh):
    rows = P(AXES, None)
    return jax.shard_map(
        body,
        mesh=mesh,
        in_specs=(rows, rows, rows, P(AXES), P(("tmpl", "spec"), None, None), P(), P(AXES)),
        out_specs=(P(None, AXES, None), P(AXES, None), P(AXES)),
        check_vma=False,
    )
```

time: 110 us -> 80.1 us (0.73)
  Pallas kernels: 44.2 us -> 25 us
  local copies, waits for them, and re-layouts: 14.7 us -> 5.41 us
  starting transfers between devices: 24.4 us -> 27.5 us
  waiting for transfers between devices: 24 us -> 21.1 us
    pallas_call x2 -> x3, Pallas kernels: 14.1 us -> 5.21 us  [the longest x1 2.41 us: body(): pl.pallas_call(coadd_kernel, out_shape=jax.ShapeDtypeStruct((64, pixels),...]
    unnamed x28 -> x14, local copies, waits for them, and re-layouts: 12.5 us -> 5.15 us
    pallas_call x1, Pallas kernels: 17.1 us -> 11.8 us  [body(): pl.pallas_call(first_fit_kernel, out_shape=jax.ShapeDtypeStruct((4, 3, 3,...]
    pallas_call x1, Pallas kernels: 9.13 us -> 5.66 us  [body(): pl.pallas_call(last_fit_kernel, out_shape=(jax.ShapeDtypeStruct((4, 3, 8,...]
    ppermute x14 -> x15, starting transfers between devices: 24.4 us -> 27.5 us  [send(): return lax.ppermute(value, AXES, [(d, moved(d, **how)) for d in range(128)])]
    ppermute x14 -> x15, waiting for transfers between devices: 24 us -> 21.1 us  [send(): return lax.ppermute(value, AXES, [(d, moved(d, **how)) for d in range(128)])]
    pallas_call x1, Pallas kernels: 1.89 us -> 0.66 us  [body(): pl.pallas_call(prep_kernel, out_shape=jax.ShapeDtypeStruct((1, TERMS, SLI...]
  transfers between devices with their start and end apart: 14 -> 15, of which waited for: 5 -> 7; matrix products, arithmetic and copies ran while one was open for 8% -> 0% of each run, Pallas kernels for 25% -> 18%
where the time goes in v2:
time: 80.1 us; the launch traced here: 79.8 us
  starting transfers between devices  27.5 us (34%)
  Pallas kernels  25 us (31%)
  waiting for transfers between devices  21.1 us (26%)
  local copies, waits for them, and re-layouts  5.41 us (7%)
    ppermute x15, starting transfers between devices, send(): return lax.ppermute(value, AXES, [(d, moved(d, **how)) for d in range(128)])  27.5 us
    ppermute x15, waiting for transfers between devices, send(): return lax.ppermute(value, AXES, [(d, moved(d, **how)) for d in range(128)])  21.1 us
    pallas_call x1, Pallas kernels, body(): pl.pallas_call(first_fit_kernel, out_shape=jax.ShapeDtypeStruct((4, 3, 3,...  11.8 us
    pallas_call x1, Pallas kernels, body(): pl.pallas_call(last_fit_kernel, out_shape=(jax.ShapeDtypeStruct((4, 3, 8,...  5.66 us
    unnamed x14, local copies, waits for them, and re-layouts  5.15 us
    pallas_call x1, Pallas kernels, body(): pl.pallas_call(coadd_kernel, out_shape=jax.ShapeDtypeStruct((64, pixels),...  2.41 us
    pallas_call x1, Pallas kernels, body(): pl.pallas_call(weight_kernel, out_shape=(jax.ShapeDtypeStruct((count, pix...  2.29 us
    pallas_call x1, Pallas kernels, body(): pl.pallas_call(final_kernel, out_shape=(jax.ShapeDtypeStruct((TERMS, 32,...  1.68 us
  transfers between devices with their start and end apart: 15, of which 7 were waited for; matrix products, arithmetic and copies ran while one was open for 0% of the time, Pallas kernels for 18%

profile of v2, /device:TPU:1, one launch (start us, length us, event | category | flops | bytes accessed | tf_op | source)
XLA Modules:
  0.0 79.8 jit_solution(1105093959867957456)
XLA Ops:
  0.7 0.1 stack.23.place
  0.8 1.0 %copy-done.2 = bf16[2,10,7808]{2,0,1:T(2,128)(2,1)S(1)} copy-done((bf16[2,10,7808]{2,0,1:T(2,128)(2,1)S(1)}, bf16[2,10,7808]{2,0,1:T(2,128)(2,1)}, u32[]{:S(2)}) %copy-start.2) | copy-done | bytes 312344
  1.7 0.7 prep.1
  2.4 0.0 copy-start
  2.4 1.4 %copy-done = bf16[96,7808]{1,0:T(8,128)(2,1)S(1)} copy-done((bf16[96,7808]{1,0:T(8,128)(2,1)S(1)}, bf16[96,7808]{1,0:T(8,128)(2,1)}, u32[]{:S(2)}) %copy-start) | copy-done | bytes 1499160
  3.8 1.4 %copy-done.1 = bf16[96,7808]{1,0:T(8,128)(2,1)S(1)} copy-done((bf16[96,7808]{1,0:T(8,128)(2,1)S(1)}, bf16[96,7808]{1,0:T(8,128)(2,1)}, u32[]{:S(2)}) %copy-start.1) | copy-done | bytes 1499160
  5.2 0.8 copy-done.3
  5.9 0.7 copy-done.4
  6.6 2.3 %weight.1 = (bf16[96,7808]{1,0:T(8,128)(2,1)S(1)}, bf16[112,7808]{1,0:T(8,128)(2,1)S(1)}) custom-call(s32[5]{0:T(128)S(1)} %stack.23.place, bf16[96,7808]{1,0:T(8,128)(2,1)S(1)} %copy-done, bf16[96,7808]{1,0:T(8,128)(2,1)S(1)} %copy-done.1, s32[61,96]{1,0:T(8,128)S(1)} %bitcast.10, s32[1,96]{1,0:T(1,128)S(1)} %bitcast.11), custom_call_target="tpu_custom_call" | custom-call | tf_op jit(solution)/shard_map/weight/pallas_call | solution.py:295
  8.9 1.5 %collective-permute-start.6 = (bf16[112,7808]{1,0:T(8,128)(2,1)S(1)}, bf16[112,7808]{1,0:T(8,128)(2,1)S(1)}, u32[]{:S(2)}, u32[]{:S(2)}) collective-permute-start(bf16[112,7808]{1,0:T(8,128)(2,1)S(1)} %get-tuple-element.14), channel_id=1, source_target_pairs={{0,1},{1,0},{2,3},{3,2},{4,5},{5,4},{6,7},{7,6},{8,9},{9,8},{10,11... | collective-permute-start | bytes 5246984 | tf_op jit(solution)/shard_map/ppermute | solution.py:31
  10.4 2.8 %collective-permute-start = (bf16[1,10,16,512]{3,2,1,0:T(8,128)(2,1)S(1)}, bf16[1,10,16,512]{3,2,1,0:T(8,128)(2,1)S(1)}, u32[]{:S(2)}, u32[]{:S(2)}) collective-permute-start(bf16[1,10,16,512]{3,2,1,0:T(8,128)(2,1)S(1)} %prep.1), channel_id=1, source_target_pairs={{0,64},{1,65},{2,66},{3,67},{4,68},{5,69},{6,70},{7,71},{8,72},{9,... | collective-permute-start | bytes 491528 | tf_op jit(solution)/shard_map/ppermute | solution.py:31
  13.2 4.4 %collective-permute-done = bf16[1,10,16,512]{3,2,1,0:T(8,128)(2,1)S(1)} collective-permute-done((bf16[1,10,16,512]{3,2,1,0:T(8,128)(2,1)S(1)}, bf16[1,10,16,512]{3,2,1,0:T(8,128)(2,1)S(1)}, u32[]{:S(2)}, u32[]{:S(2)}) %collective-permute-start) | collective-permute-done | bytes 163872 | tf_op jit(solution)/shard_map/ppermute | solution.py:31
  17.7 1.4 %collective-permute-start.1 = (bf16[2,10,16,512]{3,2,1,0:T(8,128)(2,1)S(1)}, bf16[2,10,16,512]{3,2,1,0:T(8,128)(2,1)S(1)}, u32[]{:S(2)}, u32[]{:S(2)}) collective-permute-start(bf16[2,10,16,512]{3,2,1,0:T(8,128)(2,1)S(1)} %pad_maximum_fusion.own), channel_id=1, source_target_pairs={{0,16},{1,5},{2,18},{3,7},{4,20},{5,9},{6,22},{7,11},{8,24},{9,13}... | collective-permute-start | bytes 983048 | tf_op jit(solution)/shard_map/ppermute | solution.py:31
  19.1 1.5 %collective-permute-start.2 = (bf16[2,10,16,512]{3,2,1,0:T(8,128)(2,1)S(1)}, bf16[2,10,16,512]{3,2,1,0:T(8,128)(2,1)S(1)}, u32[]{:S(2)}, u32[]{:S(2)}) collective-permute-start(bf16[2,10,16,512]{3,2,1,0:T(8,128)(2,1)S(1)} %pad_maximum_fusion.own), channel_id=1, source_target_pairs={{0,48},{1,13},{2,50},{3,15},{4,52},{5,1},{6,54},{7,3},{8,56},{9,5}... | collective-permute-start | bytes 983048 | tf_op jit(solution)/shard_map/ppermute | solution.py:31
  20.6 1.6 %collective-permute-start.3 = (bf16[2,10,16,512]{3,2,1,0:T(8,128)(2,1)S(1)}, bf16[2,10,16,512]{3,2,1,0:T(8,128)(2,1)S(1)}, u32[]{:S(2)}, u32[]{:S(2)}) collective-permute-start(bf16[2,10,16,512]{3,2,1,0:T(8,128)(2,1)S(1)} %pad_maximum_fusion.own), channel_id=1, source_target_pairs={{0,32},{1,9},{2,34},{3,11},{4,36},{5,13},{6,38},{7,15},{8,40},{9,1... | collective-permute-start | bytes 983048 | tf_op jit(solution)/shard_map/ppermute | solution.py:31
  22.2 0.0 collective-permute-done.6.other_names.other
  22.2 2.4 %coadd.1.mine = bf16[64,7808]{1,0:T(8,128)(2,1)S(1)} custom-call(s32[5]{0:T(128)S(1)} %stack.23.place, s32[1,96]{1,0:T(1,128)S(1)} %bitcast.12, bf16[112,7808]{1,0:T(8,128)(2,1)S(1)} %collective-permute-done.6.other_names.other, bf16[96,7808]{1,0:T(8,128)(2,1)S(1)} %get-tuple-element.15.own, bf16[112,7808]{1,0:T(8,128)(2,1)S(1)} %collective-permute-done.6.other_names.other), custom_call_target="tpu_custom_call" | custom-call | tf_op jit(solution)/shard_map/coadd/pallas_call | solution.py:320
  24.6 1.3 %collective-permute-start.7 = (bf16[64,7808]{1,0:T(8,128)(2,1)S(1)}, bf16[64,7808]{1,0:T(8,128)(2,1)S(1)}, u32[]{:S(2)}, u32[]{:S(2)}) collective-permute-start(bf16[64,7808]{1,0:T(8,128)(2,1)S(1)} %coadd.1.mine), channel_id=1, source_target_pairs={{0,2},{1,3},{2,0},{3,1},{4,6},{5,7},{6,4},{7,5},{8,10},{9,11},{10,... | collective-permute-start | bytes 2998280 | tf_op jit(solution)/shard_map/ppermute | solution.py:31
  25.9 0.0 collective-permute-done.1.up
  25.9 2.3 %collective-permute-done.2.down = bf16[2,10,16,512]{3,2,1,0:T(8,128)(2,1)S(1)} collective-permute-done((bf16[2,10,16,512]{3,2,1,0:T(8,128)(2,1)S(1)}, bf16[2,10,16,512]{3,2,1,0:T(8,128)(2,1)S(1)}, u32[]{:S(2)}, u32[]{:S(2)}) %collective-permute-start.2) | collective-permute-done | bytes 327712 | tf_op jit(solution)/shard_map/ppermute | solution.py:31
  28.2 1.8 %collective-permute-done.3.far = bf16[2,10,16,512]{3,2,1,0:T(8,128)(2,1)S(1)} collective-permute-done((bf16[2,10,16,512]{3,2,1,0:T(8,128)(2,1)S(1)}, bf16[2,10,16,512]{3,2,1,0:T(8,128)(2,1)S(1)}, u32[]{:S(2)}, u32[]{:S(2)}) %collective-permute-start.3) | collective-permute-done | bytes 327712 | tf_op jit(solution)/shard_map/ppermute | solution.py:31
  30.0 0.5 join.1.own
  30.5 1.4 %collective-permute-start.4 = (bf16[16,5,16,512]{3,2,1,0:T(8,128)(2,1)S(1)}, bf16[16,5,16,512]{3,2,1,0:T(8,128)(2,1)S(1)}, u32[]{:S(2)}, u32[]{:S(2)}) collective-permute-start(bf16[16,5,16,512]{3,2,1,0:T(8,128)(2,1)S(1)} %join.1.own), channel_id=1, source_target_pairs={{0,4},{1,17},{2,6},{3,19},{4,8},{5,21},{6,10},{7,23},{8,12},{9,25}... | collective-permute-start | bytes 3932168 | tf_op jit(solution)/shard_map/ppermute | solution.py:31
  31.9 2.2 %collective-permute-start.5 = (bf16[16,5,16,512]{3,2,1,0:T(8,128)(2,1)S(1)}, bf16[16,5,16,512]{3,2,1,0:T(8,128)(2,1)S(1)}, u32[]{:S(2)}, u32[]{:S(2)}) collective-permute-start(bf16[16,5,16,512]{3,2,1,0:T(8,128)(2,1)S(1)} %join.1.own), channel_id=1, source_target_pairs={{0,12},{1,49},{2,14},{3,51},{4,0},{5,53},{6,2},{7,55},{8,4},{9,57}... | collective-permute-start | bytes 3932168 | tf_op jit(solution)/shard_map/ppermute | solution.py:31
  34.1 2.4 %collective-permute-start.8 = (bf16[64,7808]{1,0:T(8,128)(2,1)S(1)}, bf16[64,7808]{1,0:T(8,128)(2,1)S(1)}, u32[]{:S(2)}, u32[]{:S(2)}) collective-permute-start(bf16[64,7808]{1,0:T(8,128)(2,1)S(1)} %coadd.1.mine), channel_id=1, source_target_pairs={{0,1},{1,0},{2,3},{3,2},{4,5},{5,4},{6,7},{7,6},{8,9},{9,8},{10,11... | collective-permute-start | bytes 2998280 | tf_op jit(solution)/shard_map/ppermute | solution.py:31
  36.6 9.3 %collective-permute-done.7.direct = bf16[64,7808]{1,0:T(8,128)(2,1)S(1)} collective-permute-done((bf16[64,7808]{1,0:T(8,128)(2,1)S(1)}, bf16[64,7808]{1,0:T(8,128)(2,1)S(1)}, u32[]{:S(2)}, u32[]{:S(2)}) %collective-permute-start.7) | collective-permute-done | bytes 999456 | tf_op jit(solution)/shard_map/ppermute | solution.py:31
  45.9 3.3 %collective-permute-start.9 = (bf16[64,7808]{1,0:T(8,128)(2,1)S(1)}, bf16[64,7808]{1,0:T(8,128)(2,1)S(1)}, u32[]{:S(2)}, u32[]{:S(2)}) collective-permute-start(bf16[64,7808]{1,0:T(8,128)(2,1)S(1)} %collective-permute-done.7.direct), channel_id=1, source_target_pairs={{0,1},{1,0},{2,3},{3,2},{4,5},{5,4},{6,7},{7,6},{8,9},{9,8},{10,11... | collective-permute-start | bytes 2998280 | tf_op jit(solution)/shard_map/ppermute | solution.py:31
  49.2 0.1 collective-permute-done.4.up
  49.4 1.6 %collective-permute-start.10 = (bf16[8,5,16,512]{3,2,1,0:T(8,128)(2,1)S(1)}, bf16[8,5,16,512]{3,2,1,0:T(8,128)(2,1)S(1)}, u32[]{:S(2)}, u32[]{:S(2)}) collective-permute-start(bf16[8,5,16,512]{3,2,1,0:T(8,128)(2,1)S(1)} %slice.8), channel_id=1, source_target_pairs={{0,4},{1,17},{2,6},{3,19},{4,8},{5,21},{6,10},{7,23},{8,12},{9,25}... | collective-permute-start | bytes 1966088 | tf_op jit(solution)/shard_map/ppermute | solution.py:31
  51.0 0.0 collective-permute-done.5.down
  51.0 1.3 %collective-permute-start.11 = (bf16[8,5,16,512]{3,2,1,0:T(8,128)(2,1)S(1)}, bf16[8,5,16,512]{3,2,1,0:T(8,128)(2,1)S(1)}, u32[]{:S(2)}, u32[]{:S(2)}) collective-permute-start(bf16[8,5,16,512]{3,2,1,0:T(8,128)(2,1)S(1)} %slice.9), channel_id=1, source_target_pairs={{0,12},{1,49},{2,14},{3,51},{4,0},{5,53},{6,2},{7,55},{8,4},{9,57}... | collective-permute-start | bytes 1966088 | tf_op jit(solution)/shard_map/ppermute | solution.py:31
  52.4 0.0 collective-permute-done.8.over
  52.4 0.0 collective-permute-done.9.swapped
  52.4 11.8 %first_fit.1.first = f32[4,3,3,8,128]{4,3,2,1,0:T(8,128)S(1)} custom-call(s32[5]{0:T(128)S(1)} %stack.23.place, bf16[16,5,16,512]{3,2,1,0:T(8,128)(2,1)S(1)} %join.1.own, bf16[16,5,16,512]{3,2,1,0:T(8,128)(2,1)S(1)} %collective-permute-done.4.up, bf16[16,5,16,512]{3,2,1,0:T(8,128)(2,1)S(1)} %collective-permute-done.5.down, bf16[64,7808]{1,0:T(8,128)(2,1)S(1)} %coadd.1.mine, ...), custom_call_target="tpu_custom_call" | custom-call | tf_op jit(solution)/shard_map/first_fit/pallas_call | solution.py:351
  64.2 0.0 copy-start.6
  64.2 0.0 copy-start.5
  64.2 0.0 collective-permute-done.10.far_a
  64.2 0.0 collective-permute-done.11.far_b
  64.2 5.7 %last_fit.1 = (f32[4,3,8,128]{3,2,1,0:T(8,128)S(1)}, f32[4,3,8,128]{3,2,1,0:T(8,128)S(1)}, f32[4,3,8,128]{3,2,1,0:T(8,128)S(1)}, f32[4,3,8,128]{3,2,1,0:T(8,128)S(1)}) custom-call(s32[5]{0:T(128)S(1)} %stack.23.place, f32[4,3,3,8,128]{4,3,2,1,0:T(8,128)S(1)} %first_fit.1.first, bf16[8,5,16,512]{3,2,1,0:T(8,128)(2,1)S(1)} %collective-permute-done.10.far_a, ...), custom_call_target="tpu_custom_call" | custom-call | tf_op jit(solution)/shard_map/last_fit/pallas_call | solution.py:360
  69.9 3.3 %collective-permute-start.12 = (f32[4,3,8,128]{3,2,1,0:T(8,128)S(1)}, f32[4,3,8,128]{3,2,1,0:T(8,128)S(1)}, u32[]{:S(2)}, u32[]{:S(2)}) collective-permute-start(f32[4,3,8,128]{3,2,1,0:T(8,128)S(1)} %get-tuple-element.17), channel_id=1, source_target_pairs={{0,1},{1,0},{2,3},{3,2},{4,5},{5,4},{6,7},{7,6},{8,9},{9,8},{10,11... | collective-permute-start | bytes 147464 | tf_op jit(solution)/shard_map/ppermute | solution.py:31
  73.2 1.2 %collective-permute-start.13 = (f32[4,3,8,128]{3,2,1,0:T(8,128)S(1)}, f32[4,3,8,128]{3,2,1,0:T(8,128)S(1)}, u32[]{:S(2)}, u32[]{:S(2)}) collective-permute-start(f32[4,3,8,128]{3,2,1,0:T(8,128)S(1)} %get-tuple-element.18), channel_id=1, source_target_pairs={{0,2},{1,3},{2,0},{3,1},{4,6},{5,7},{6,4},{7,5},{8,10},{9,11},{10,... | collective-permute-start | bytes 147464 | tf_op jit(solution)/shard_map/ppermute | solution.py:31
  74.4 0.5 collective-permute-start.14
  74.9 0.0 copy-done.6
  74.9 0.1 reshape_tile.3.classes
  75.0 0.0 collective-permute-done.12.part_1
  75.0 1.1 %collective-permute-done.13.part_2 = f32[4,3,8,128]{3,2,1,0:T(8,128)S(1)} collective-permute-done((f32[4,3,8,128]{3,2,1,0:T(8,128)S(1)}, f32[4,3,8,128]{3,2,1,0:T(8,128)S(1)}, u32[]{:S(2)}, u32[]{:S(2)}) %collective-permute-start.13) | collective-permute-done | bytes 49184 | tf_op jit(solution)/shard_map/ppermute | solution.py:31
  76.2 2.0 %collective-permute-done.14.part_3 = f32[4,3,8,128]{3,2,1,0:T(8,128)S(1)} collective-permute-done((f32[4,3,8,128]{3,2,1,0:T(8,128)S(1)}, f32[4,3,8,128]{3,2,1,0:T(8,128)S(1)}, u32[]{:S(2)}, u32[]{:S(2)}) %collective-permute-start.14) | collective-permute-done | bytes 49184 | tf_op jit(solution)/shard_map/ppermute | solution.py:31
  78.2 1.7 %final.1 = (f32[10,32,128]{2,1,0:T(8,128)}, f32[32,128]{1,0:T(8,128)}, f32[1,32]{1,0:T(1,128)}) custom-call(s32[5]{0:T(128)S(1)} %stack.23.place, s32[3]{0:T(128)S(1)} %copy-done.5, s32[1,128]{1,0:T(1,128)S(1)} %reshape_tile.3.classes, f32[4,3,8,128]{3,2,1,0:T(8,128)S(1)} %get-tuple-element.16.part_0, f32[4,3,8,128]{3,2,1,0:T(8,128)S(1)} %collective-permute-done.12.part_1, ...), custom_call_target="tpu_custom_call" | custom-call | tf_op jit(solution)/shard_map/final/pallas_call | solution.py:376
  (9 shorter events, 0.1 us)
Async XLA Ops:
  0.8 1.0 %copy-start.2 = (bf16[2,10,7808]{2,0,1:T(2,128)(2,1)S(1)}, bf16[2,10,7808]{2,0,1:T(2,128)(2,1)}, u32[]{:S(2)}) copy-start(bf16[2,10,7808]{2,0,1:T(2,128)(2,1)} %param.11) | copy-start | bytes 936964
  2.4 1.4 %copy-start = (bf16[96,7808]{1,0:T(8,128)(2,1)S(1)}, bf16[96,7808]{1,0:T(8,128)(2,1)}, u32[]{:S(2)}) copy-start(bf16[96,7808]{1,0:T(8,128)(2,1)} %flux) | copy-start | bytes 4497412
  3.8 1.4 %copy-start.1 = (bf16[96,7808]{1,0:T(8,128)(2,1)S(1)}, bf16[96,7808]{1,0:T(8,128)(2,1)}, u32[]{:S(2)}) copy-start(bf16[96,7808]{1,0:T(8,128)(2,1)} %ivar.1) | copy-start | bytes 4497412
  5.2 0.8 copy-start.3
  5.9 0.7 copy-start.4
  8.9 13.3 %collective-permute-start.6 = (bf16[112,7808]{1,0:T(8,128)(2,1)S(1)}, bf16[112,7808]{1,0:T(8,128)(2,1)S(1)}, u32[]{:S(2)}, u32[]{:S(2)}) collective-permute-start(bf16[112,7808]{1,0:T(8,128)(2,1)S(1)} %get-tuple-element.14), channel_id=1, source_target_pairs={{0,1},{1,0},{2,3},{3,2},{4,5},{5,4},{6,7},{7,6},{8,9},{9,8},{10,11... | collective-permute-start | bytes 5246984 | tf_op jit(solution)/shard_map/ppermute | solution.py:31
  10.4 7.3 %collective-permute-start = (bf16[1,10,16,512]{3,2,1,0:T(8,128)(2,1)S(1)}, bf16[1,10,16,512]{3,2,1,0:T(8,128)(2,1)S(1)}, u32[]{:S(2)}, u32[]{:S(2)}) collective-permute-start(bf16[1,10,16,512]{3,2,1,0:T(8,128)(2,1)S(1)} %prep.1), channel_id=1, source_target_pairs={{0,64},{1,65},{2,66},{3,67},{4,68},{5,69},{6,70},{7,71},{8,72},{9,... | collective-permute-start | bytes 491528 | tf_op jit(solution)/shard_map/ppermute | solution.py:31
  17.7 8.2 %collective-permute-start.1 = (bf16[2,10,16,512]{3,2,1,0:T(8,128)(2,1)S(1)}, bf16[2,10,16,512]{3,2,1,0:T(8,128)(2,1)S(1)}, u32[]{:S(2)}, u32[]{:S(2)}) collective-permute-start(bf16[2,10,16,512]{3,2,1,0:T(8,128)(2,1)S(1)} %pad_maximum_fusion.own), channel_id=1, source_target_pairs={{0,16},{1,5},{2,18},{3,7},{4,20},{5,9},{6,22},{7,11},{8,24},{9,13}... | collective-permute-start | bytes 983048 | tf_op jit(solution)/shard_map/ppermute | solution.py:31
  19.1 9.1 %collective-permute-start.2 = (bf16[2,10,16,512]{3,2,1,0:T(8,128)(2,1)S(1)}, bf16[2,10,16,512]{3,2,1,0:T(8,128)(2,1)S(1)}, u32[]{:S(2)}, u32[]{:S(2)}) collective-permute-start(bf16[2,10,16,512]{3,2,1,0:T(8,128)(2,1)S(1)} %pad_maximum_fusion.own), channel_id=1, source_target_pairs={{0,48},{1,13},{2,50},{3,15},{4,52},{5,1},{6,54},{7,3},{8,56},{9,5}... | collective-permute-start | bytes 983048 | tf_op jit(solution)/shard_map/ppermute | solution.py:31
  20.6 9.4 %collective-permute-start.3 = (bf16[2,10,16,512]{3,2,1,0:T(8,128)(2,1)S(1)}, bf16[2,10,16,512]{3,2,1,0:T(8,128)(2,1)S(1)}, u32[]{:S(2)}, u32[]{:S(2)}) collective-permute-start(bf16[2,10,16,512]{3,2,1,0:T(8,128)(2,1)S(1)} %pad_maximum_fusion.own), channel_id=1, source_target_pairs={{0,32},{1,9},{2,34},{3,11},{4,36},{5,13},{6,38},{7,15},{8,40},{9,1... | collective-permute-start | bytes 983048 | tf_op jit(solution)/shard_map/ppermute | solution.py:31
  24.6 21.3 %collective-permute-start.7 = (bf16[64,7808]{1,0:T(8,128)(2,1)S(1)}, bf16[64,7808]{1,0:T(8,128)(2,1)S(1)}, u32[]{:S(2)}, u32[]{:S(2)}) collective-permute-start(bf16[64,7808]{1,0:T(8,128)(2,1)S(1)} %coadd.1.mine), channel_id=1, source_target_pairs={{0,2},{1,3},{2,0},{3,1},{4,6},{5,7},{6,4},{7,5},{8,10},{9,11},{10,... | collective-permute-start | bytes 2998280 | tf_op jit(solution)/shard_map/ppermute | solution.py:31
  30.5 18.8 %collective-permute-start.4 = (bf16[16,5,16,512]{3,2,1,0:T(8,128)(2,1)S(1)}, bf16[16,5,16,512]{3,2,1,0:T(8,128)(2,1)S(1)}, u32[]{:S(2)}, u32[]{:S(2)}) collective-permute-start(bf16[16,5,16,512]{3,2,1,0:T(8,128)(2,1)S(1)} %join.1.own), channel_id=1, source_target_pairs={{0,4},{1,17},{2,6},{3,19},{4,8},{5,21},{6,10},{7,23},{8,12},{9,25}... | collective-permute-start | bytes 3932168 | tf_op jit(solution)/shard_map/ppermute | solution.py:31
  31.9 19.0 %collective-permute-start.5 = (bf16[16,5,16,512]{3,2,1,0:T(8,128)(2,1)S(1)}, bf16[16,5,16,512]{3,2,1,0:T(8,128)(2,1)S(1)}, u32[]{:S(2)}, u32[]{:S(2)}) collective-permute-start(bf16[16,5,16,512]{3,2,1,0:T(8,128)(2,1)S(1)} %join.1.own), channel_id=1, source_target_pairs={{0,12},{1,49},{2,14},{3,51},{4,0},{5,53},{6,2},{7,55},{8,4},{9,57}... | collective-permute-start | bytes 3932168 | tf_op jit(solution)/shard_map/ppermute | solution.py:31
  34.1 18.2 %collective-permute-start.8 = (bf16[64,7808]{1,0:T(8,128)(2,1)S(1)}, bf16[64,7808]{1,0:T(8,128)(2,1)S(1)}, u32[]{:S(2)}, u32[]{:S(2)}) collective-permute-start(bf16[64,7808]{1,0:T(8,128)(2,1)S(1)} %coadd.1.mine), channel_id=1, source_target_pairs={{0,1},{1,0},{2,3},{3,2},{4,5},{5,4},{6,7},{7,6},{8,9},{9,8},{10,11... | collective-permute-start | bytes 2998280 | tf_op jit(solution)/shard_map/ppermute | solution.py:31
  45.9 6.5 %collective-permute-start.9 = (bf16[64,7808]{1,0:T(8,128)(2,1)S(1)}, bf16[64,7808]{1,0:T(8,128)(2,1)S(1)}, u32[]{:S(2)}, u32[]{:S(2)}) collective-permute-start(bf16[64,7808]{1,0:T(8,128)(2,1)S(1)} %collective-permute-done.7.direct), channel_id=1, source_target_pairs={{0,1},{1,0},{2,3},{3,2},{4,5},{5,4},{6,7},{7,6},{8,9},{9,8},{10,11... | collective-permute-start | bytes 2998280 | tf_op jit(solution)/shard_map/ppermute | solution.py:31
  49.4 14.8 %collective-permute-start.10 = (bf16[8,5,16,512]{3,2,1,0:T(8,128)(2,1)S(1)}, bf16[8,5,16,512]{3,2,1,0:T(8,128)(2,1)S(1)}, u32[]{:S(2)}, u32[]{:S(2)}) collective-permute-start(bf16[8,5,16,512]{3,2,1,0:T(8,128)(2,1)S(1)} %slice.8), channel_id=1, source_target_pairs={{0,4},{1,17},{2,6},{3,19},{4,8},{5,21},{6,10},{7,23},{8,12},{9,25}... | collective-permute-start | bytes 1966088 | tf_op jit(solution)/shard_map/ppermute | solution.py:31
  51.0 13.2 %collective-permute-start.11 = (bf16[8,5,16,512]{3,2,1,0:T(8,128)(2,1)S(1)}, bf16[8,5,16,512]{3,2,1,0:T(8,128)(2,1)S(1)}, u32[]{:S(2)}, u32[]{:S(2)}) collective-permute-start(bf16[8,5,16,512]{3,2,1,0:T(8,128)(2,1)S(1)} %slice.9), channel_id=1, source_target_pairs={{0,12},{1,49},{2,14},{3,51},{4,0},{5,53},{6,2},{7,55},{8,4},{9,57}... | collective-permute-start | bytes 1966088 | tf_op jit(solution)/shard_map/ppermute | solution.py:31
  64.2 10.8 %copy-start.6 = (s32[32]{0:T(128)S(1)}, s32[32]{0:T(128)}, u32[]{:S(2)}) copy-start(s32[32]{0:T(128)} %param.13) | copy-start | bytes 388
  64.2 14.0 %copy-start.5 = (s32[3]{0:T(128)S(1)}, s32[3]{0:T(128)}, u32[]{:S(2)}) copy-start(s32[3]{0:T(128)} %counts.1) | copy-start | bytes 40
  69.9 5.2 %collective-permute-start.12 = (f32[4,3,8,128]{3,2,1,0:T(8,128)S(1)}, f32[4,3,8,128]{3,2,1,0:T(8,128)S(1)}, u32[]{:S(2)}, u32[]{:S(2)}) collective-permute-start(f32[4,3,8,128]{3,2,1,0:T(8,128)S(1)} %get-tuple-element.17), channel_id=1, source_target_pairs={{0,1},{1,0},{2,3},{3,2},{4,5},{5,4},{6,7},{7,6},{8,9},{9,8},{10,11... | collective-permute-start | bytes 147464 | tf_op jit(solution)/shard_map/ppermute | solution.py:31
  73.2 3.0 %collective-permute-start.13 = (f32[4,3,8,128]{3,2,1,0:T(8,128)S(1)}, f32[4,3,8,128]{3,2,1,0:T(8,128)S(1)}, u32[]{:S(2)}, u32[]{:S(2)}) collective-permute-start(f32[4,3,8,128]{3,2,1,0:T(8,128)S(1)} %get-tuple-element.18), channel_id=1, source_target_pairs={{0,2},{1,3},{2,0},{3,1},{4,6},{5,7},{6,4},{7,5},{8,10},{9,11},{10,... | collective-permute-start | bytes 147464 | tf_op jit(solution)/shard_map/ppermute | solution.py:31
  74.4 3.7 %collective-permute-start.14 = (f32[4,3,8,128]{3,2,1,0:T(8,128)S(1)}, f32[4,3,8,128]{3,2,1,0:T(8,128)S(1)}, u32[]{:S(2)}, u32[]{:S(2)}) collective-permute-start(f32[4,3,8,128]{3,2,1,0:T(8,128)S(1)} %get-tuple-element.19), channel_id=1, source_target_pairs={{0,3},{1,2},{2,1},{3,0},{4,7},{5,6},{6,5},{7,4},{8,11},{9,10},{10,... | collective-permute-start | bytes 147464 | tf_op jit(solution)/shard_map/ppermute | solution.py:31

commit v3 on v2

--- a/solution.py
+++ b/solution.py
@@ -113,7 +113,9 @@
             [p[:, 2 * m : 2 * m + 2].reshape(p.shape[0] * 2 * SLICES, WIDTH) for p in (own, up, down, far)], axis=0
         )
         turned = jnp.dot(order, block, preferred_element_type=jnp.float32).astype(jnp.bfloat16)
-        out[:, m] = turned.reshape(SLICES, 16, WIDTH)
+        for block in range(out.shape[0]):
+            h, at = block // 4, block % 4 * 128
+            out[block, m] = turned[h * 16 : h * 16 + 16, at : at + 128]
 
 
 def solve(entries, right):
@@ -148,9 +150,9 @@
     pixels = mine.shape[1]
     contract = (((1,), (1,)), ((), ()))
 
-    def one_slice(h, segment, at, width, first):
-        static = isinstance(h, int)
-        lanes = pl.ds(h * WIDTH if static else pl.multiple_of(h * WIDTH, WIDTH), width)
+    for at in range(0, pixels // 128, WIDTH // 128):
+        taken = range(at, min(at + WIDTH // 128, pixels // 128))
+        lanes = pl.ds(at * 128, len(taken) * 128)
         near = jnp.concatenate([mine[:, lanes], direct[:, lanes]], axis=0)
         far = jnp.concatenate(
             [over[32:64, lanes], over[0:32, lanes], swapped[32:64, lanes], swapped[0:32, lanes]], axis=0
@@ -158,7 +160,10 @@
         ivar = jnp.where(core == 0, near, far)
         wflux = jnp.where(core == 0, far, near)
         for b, refs in enumerate(blocks):
-            evens = [refs[segment][at, m, :, 0:width] for m in range(HALVES)]
+            evens = []
+            for m in range(HALVES):
+                pieces = [refs[0][t, m] if t < refs[0].shape[0] else refs[1][t - refs[0].shape[0], m] for t in taken]
+                evens.append(jnp.concatenate(pieces, axis=1))
             odds = [jnp.concatenate([e[8:16], e[0:8]], axis=0) for e in evens]
             products = jnp.concatenate(
                 [evens[m] * (odds[n] if cross else evens[n]) for m, n, cross in combos()], axis=0
@@ -167,26 +172,12 @@
             project = lax.dot_general(
                 jnp.concatenate(evens, axis=0), wflux, contract, preferred_element_type=jnp.float32
             )
-            if first:
+            if at == 0:
                 total[b, 0 : COMBOS * 16] = normal
                 total[b, COMBOS * 16 : ROWS] = project
             else:
                 total[b, 0 : COMBOS * 16] += normal
                 total[b, COMBOS * 16 : ROWS] += project
-
-    full = pixels // WIDTH
-    segments = len(blocks[0])
-    per = SLICES // segments
-    one_slice(0, 0, 0, WIDTH, True)
-    for segment in range(segments):
-
-        def step(h, carry, segment=segment):
-            one_slice(h, segment, h - segment * per, WIDTH, False)
-            return carry
-
-        lax.fori_loop(max(1, segment * per), min(full, (segment + 1) * per), step, 0)
-    if pixels > full * WIDTH:
-        one_slice(full, full // per, full % per, pixels - full * WIDTH, False)
 
     entries = {}
     for (k, l), at in entry_rows().items():
@@ -267,6 +258,10 @@
                 gains[...] = turned[k * 32 : (k + 1) * 32]
 
 
+def cost(micros):
+    return pl.CostEstimate(flops=0, bytes_accessed=int(micros * 3.0e6), transcendentals=0)
+
+
 def body(flux, ivar, pixel_mask, exposure_target, basis, trial_counts, target_class):
     pixels = flux.shape[1]
     tmpl, spec, core = (lax.axis_index(a) for a in AXES)
@@ -282,11 +277,12 @@
         out_specs=vmem,
         scratch_shapes=[pltpu.VMEM((TERMS * SLICES, WIDTH), jnp.float32)],
         compiler_params=params,
+        cost_estimate=cost(0.7),
         name="prep",
     )(place, jnp.transpose(basis, (1, 0, 2)))
-    pair = jnp.concatenate([trial, send(trial, x_hi=1)], axis=0)
-
-    trial, flux = lax.optimization_barrier((trial, flux))
+    other = send(trial, x_hi=1)
+    pair = jnp.concatenate([trial, other], axis=0)
+
     count = flux.shape[0]
     height = 32
     steps = count // height
@@ -309,11 +305,11 @@
         out_specs=(spectra, pl.BlockSpec((height, pixels), lambda i: (i, 0))),
         scratch_shapes=[pltpu.VMEM((count, pixel_mask.shape[1]), jnp.float32)],
         compiler_params=params,
+        cost_estimate=cost(2.3),
         name="weight",
     )(place, flux, ivar, pixel_mask.T, owners)
+    outgoing, _ = lax.optimization_barrier((outgoing, other))
     incoming = send(outgoing, core=1)
-
-    near = [pair] + [send(pair, along=0, step=s) for s in (1, -1, 2)]
 
     chunk = 2048
     rows = pl.BlockSpec((count, chunk), lambda i: (0, i))
@@ -330,23 +326,28 @@
         ],
         out_specs=pl.BlockSpec((64, chunk), lambda i: (0, i)),
         compiler_params=params,
+        cost_estimate=cost(2.4),
         name="coadd",
     )(place, owners, incoming, keep, incoming)
     direct = send(mine, x_lo=1)
     over = send(mine, core=1)
     swapped = send(direct, core=1)
 
+    near = [pair] + [send(pair, along=0, step=s) for s in (1, -1, 2)]
+
     eight = pl.pallas_call(
         join_kernel,
-        out_shape=jax.ShapeDtypeStruct((SLICES, HALVES, 16, WIDTH), jnp.bfloat16),
+        out_shape=jax.ShapeDtypeStruct((pixels // 128, HALVES, 16, 128), jnp.bfloat16),
         in_specs=[vmem] * 4,
         out_specs=vmem,
         compiler_params=params,
+        cost_estimate=cost(0.5),
         name="join",
     )(*near)
     up, down = (send(eight, along=1, step=s) for s in (1, -1))
-    far_a = send(up[: SLICES // 2], along=1, step=1)
-    far_b = send(down[SLICES // 2 :], along=1, step=-1)
+    cut = pixels // 256
+    far_a = send(up[:cut], along=1, step=1)
+    far_b = send(down[cut:], along=1, step=-1)
 
     first = pl.pallas_call(
         first_fit_kernel,
@@ -355,6 +356,7 @@
         out_specs=vmem,
         scratch_shapes=[pltpu.VMEM((3, ROWS, 128), jnp.float32)],
         compiler_params=params,
+        cost_estimate=cost(12),
         name="first_fit",
     )(place, eight, up, down, mine, direct, over, swapped)
     parts = pl.pallas_call(
@@ -364,6 +366,7 @@
         out_specs=(vmem,) * 4,
         scratch_shapes=[pltpu.VMEM((1, ROWS, 128), jnp.float32)],
         compiler_params=params,
+        cost_estimate=cost(6),
         name="last_fit",
     )(place, first, far_a, far_b, mine, direct, over, swapped)
 
@@ -383,6 +386,7 @@
         in_specs=[smem, smem] + [vmem] * 5,
         out_specs=(vmem,) * 3,
         compiler_params=params,
+        cost_estimate=cost(2),
         name="final",
     )(place, trial_counts, jnp.tile(target_class, 4).reshape(1, 128), *parts)
     return coefs, gains, best.reshape(32)

time: 80.1 us -> 71.3 us (0.89)
  Pallas kernels: 25 us -> 19.5 us
  starting transfers between devices: 27.5 us -> 24.4 us
    pallas_call x1, Pallas kernels: 11.8 us -> 8.56 us  [body(): pl.pallas_call(first_fit_kernel, out_shape=jax.ShapeDtypeStruct((4, 3, 3,...]
    ppermute x15, starting transfers between devices: 27.5 us -> 24.4 us  [send(): return lax.ppermute(value, AXES, [(d, moved(d, **how)) for d in range(128)])]
    pallas_call x1, Pallas kernels: 5.66 us -> 3.44 us  [body(): pl.pallas_call(last_fit_kernel, out_shape=(jax.ShapeDtypeStruct((4, 3, 8,...]
  transfers between devices with their start and end apart: 15 -> 15, of which waited for: 7 -> 7; matrix products, arithmetic and copies ran while one was open for 0% -> 0% of each run, Pallas kernels for 18% -> 19%
where the time goes in v3:
time: 71.3 us; the launch traced here: 71.1 us
  starting transfers between devices  24.4 us (34%)
  waiting for transfers between devices  20.9 us (29%)
  Pallas kernels  19.5 us (27%)
  local copies, waits for them, and re-layouts  5.44 us (8%)
  between operations  0.79 us (1%)
    ppermute x15, starting transfers between devices, send(): return lax.ppermute(value, AXES, [(d, moved(d, **how)) for d in range(128)])  24.4 us
    ppermute x15, waiting for transfers between devices, send(): return lax.ppermute(value, AXES, [(d, moved(d, **how)) for d in range(128)])  20.9 us
    pallas_call x1, Pallas kernels, body(): pl.pallas_call(first_fit_kernel, out_shape=jax.ShapeDtypeStruct((4, 3, 3,...  8.56 us
    unnamed x14, local copies, waits for them, and re-layouts  5.16 us
    pallas_call x1, Pallas kernels, body(): pl.pallas_call(last_fit_kernel, out_shape=(jax.ShapeDtypeStruct((4, 3, 8,...  3.44 us
    pallas_call x1, Pallas kernels, body(): pl.pallas_call(coadd_kernel, out_shape=jax.ShapeDtypeStruct((64, pixels),...  2.41 us
    pallas_call x1, Pallas kernels, body(): pl.pallas_call(weight_kernel, out_shape=(jax.ShapeDtypeStruct((count, pix...  2.29 us
    pallas_call x1, Pallas kernels, body(): pl.pallas_call(final_kernel, out_shape=(jax.ShapeDtypeStruct((TERMS, 32,...  1.68 us
  transfers between devices with their start and end apart: 15, of which 7 were waited for; matrix products, arithmetic and copies ran while one was open for 0% of the time, Pallas kernels for 19%

profile of v3, /device:TPU:1, one launch (start us, length us, event | category | flops | bytes accessed | tf_op | source)
XLA Modules:
  0.0 71.1 jit_solution(2641608490606238726)
XLA Ops:
  0.7 0.1 stack.23.place
  0.8 1.0 %copy-done.2 = bf16[2,10,7808]{2,0,1:T(2,128)(2,1)S(1)} copy-done((bf16[2,10,7808]{2,0,1:T(2,128)(2,1)S(1)}, bf16[2,10,7808]{2,0,1:T(2,128)(2,1)}, u32[]{:S(2)}) %copy-start.2) | copy-done | bytes 312344
  1.7 0.7 prep.1
  2.4 3.7 %collective-permute-start = (bf16[1,10,16,512]{3,2,1,0:T(8,128)(2,1)S(1)}, bf16[1,10,16,512]{3,2,1,0:T(8,128)(2,1)S(1)}, u32[]{:S(2)}, u32[]{:S(2)}) collective-permute-start(bf16[1,10,16,512]{3,2,1,0:T(8,128)(2,1)S(1)} %prep.1), channel_id=1, source_target_pairs={{0,64},{1,65},{2,66},{3,67},{4,68},{5,69},{6,70},{7,71},{8,72},{9,... | collective-permute-start | bytes 491528 | tf_op jit(solution)/shard_map/ppermute | solution.py:31
  6.0 1.4 %copy-done = bf16[96,7808]{1,0:T(8,128)(2,1)S(1)} copy-done((bf16[96,7808]{1,0:T(8,128)(2,1)S(1)}, bf16[96,7808]{1,0:T(8,128)(2,1)}, u32[]{:S(2)}) %copy-start) | copy-done | bytes 1499160
  7.4 1.4 %copy-done.1 = bf16[96,7808]{1,0:T(8,128)(2,1)S(1)} copy-done((bf16[96,7808]{1,0:T(8,128)(2,1)S(1)}, bf16[96,7808]{1,0:T(8,128)(2,1)}, u32[]{:S(2)}) %copy-start.1) | copy-done | bytes 1499160
  8.8 0.8 %copy-done.3 = s32[96,61]{0,1:T(8,128)S(1)} copy-done((s32[96,61]{0,1:T(8,128)S(1)}, s32[96,61]{0,1:T(8,128)}, u32[]{:S(2)}) %copy-start.3) | copy-done | bytes 23448
  9.6 0.7 copy-done.4
  10.2 2.3 %weight.1 = (bf16[96,7808]{1,0:T(8,128)(2,1)S(1)}, bf16[112,7808]{1,0:T(8,128)(2,1)S(1)}) custom-call(s32[5]{0:T(128)S(1)} %stack.23.place, bf16[96,7808]{1,0:T(8,128)(2,1)S(1)} %copy-done, bf16[96,7808]{1,0:T(8,128)(2,1)S(1)} %copy-done.1, s32[61,96]{1,0:T(8,128)S(1)} %bitcast.10, s32[1,96]{1,0:T(1,128)S(1)} %bitcast.11), custom_call_target="tpu_custom_call" | custom-call | bytes 6899999 | tf_op jit(solution)/shard_map/weight/pallas_call | solution.py:291
  12.5 0.0 collective-permute-done
  12.5 1.0 %collective-permute-start.6 = (bf16[112,7808]{1,0:T(8,128)(2,1)S(1)}, bf16[112,7808]{1,0:T(8,128)(2,1)S(1)}, u32[]{:S(2)}, u32[]{:S(2)}) collective-permute-start(bf16[112,7808]{1,0:T(8,128)(2,1)S(1)} %get-tuple-element.14), channel_id=1, source_target_pairs={{0,1},{1,0},{2,3},{3,2},{4,5},{5,4},{6,7},{7,6},{8,9},{9,8},{10,11... | collective-permute-start | bytes 5246984 | tf_op jit(solution)/shard_map/ppermute | solution.py:31
  13.6 1.4 %collective-permute-start.1 = (bf16[2,10,16,512]{3,2,1,0:T(8,128)(2,1)S(1)}, bf16[2,10,16,512]{3,2,1,0:T(8,128)(2,1)S(1)}, u32[]{:S(2)}, u32[]{:S(2)}) collective-permute-start(bf16[2,10,16,512]{3,2,1,0:T(8,128)(2,1)S(1)} %pad_maximum_fusion.own), channel_id=1, source_target_pairs={{0,16},{1,5},{2,18},{3,7},{4,20},{5,9},{6,22},{7,11},{8,24},{9,13}... | collective-permute-start | bytes 983048 | tf_op jit(solution)/shard_map/ppermute | solution.py:31
  15.0 1.5 %collective-permute-start.2 = (bf16[2,10,16,512]{3,2,1,0:T(8,128)(2,1)S(1)}, bf16[2,10,16,512]{3,2,1,0:T(8,128)(2,1)S(1)}, u32[]{:S(2)}, u32[]{:S(2)}) collective-permute-start(bf16[2,10,16,512]{3,2,1,0:T(8,128)(2,1)S(1)} %pad_maximum_fusion.own), channel_id=1, source_target_pairs={{0,48},{1,13},{2,50},{3,15},{4,52},{5,1},{6,54},{7,3},{8,56},{9,5}... | collective-permute-start | bytes 983048 | tf_op jit(solution)/shard_map/ppermute | solution.py:31
  16.5 1.6 %collective-permute-start.3 = (bf16[2,10,16,512]{3,2,1,0:T(8,128)(2,1)S(1)}, bf16[2,10,16,512]{3,2,1,0:T(8,128)(2,1)S(1)}, u32[]{:S(2)}, u32[]{:S(2)}) collective-permute-start(bf16[2,10,16,512]{3,2,1,0:T(8,128)(2,1)S(1)} %pad_maximum_fusion.own), channel_id=1, source_target_pairs={{0,32},{1,9},{2,34},{3,11},{4,36},{5,13},{6,38},{7,15},{8,40},{9,1... | collective-permute-start | bytes 983048 | tf_op jit(solution)/shard_map/ppermute | solution.py:31
  18.0 0.0 collective-permute-done.6.other_names.other
  18.0 2.4 %coadd.1.mine = bf16[64,7808]{1,0:T(8,128)(2,1)S(1)} custom-call(s32[5]{0:T(128)S(1)} %stack.23.place, s32[1,96]{1,0:T(1,128)S(1)} %bitcast.12, bf16[112,7808]{1,0:T(8,128)(2,1)S(1)} %collective-permute-done.6.other_names.other, bf16[96,7808]{1,0:T(8,128)(2,1)S(1)} %get-tuple-element.15.own, bf16[112,7808]{1,0:T(8,128)(2,1)S(1)} %collective-permute-done.6.other_names.other), custom_call_target="tpu_custom_call" | custom-call | bytes 7200000 | tf_op jit(solution)/shard_map/coadd/pallas_call | solution.py:316
  20.5 0.4 collective-permute-start.7
  20.8 0.3 collective-permute-done.1.up
  21.2 2.9 %collective-permute-done.2.down = bf16[2,10,16,512]{3,2,1,0:T(8,128)(2,1)S(1)} collective-permute-done((bf16[2,10,16,512]{3,2,1,0:T(8,128)(2,1)S(1)}, bf16[2,10,16,512]{3,2,1,0:T(8,128)(2,1)S(1)}, u32[]{:S(2)}, u32[]{:S(2)}) %collective-permute-start.2) | collective-permute-done | bytes 327712 | tf_op jit(solution)/shard_map/ppermute | solution.py:31
  24.0 1.8 %collective-permute-done.3.far = bf16[2,10,16,512]{3,2,1,0:T(8,128)(2,1)S(1)} collective-permute-done((bf16[2,10,16,512]{3,2,1,0:T(8,128)(2,1)S(1)}, bf16[2,10,16,512]{3,2,1,0:T(8,128)(2,1)S(1)}, u32[]{:S(2)}, u32[]{:S(2)}) %collective-permute-start.3) | collective-permute-done | bytes 327712 | tf_op jit(solution)/shard_map/ppermute | solution.py:31
  25.8 0.5 join.1.own
  26.4 3.5 %collective-permute-start.5 = (bf16[61,5,16,128]{3,2,1,0:T(8,128)(2,1)S(1)}, bf16[61,5,16,128]{3,2,1,0:T(8,128)(2,1)S(1)}, u32[]{:S(2)}, u32[]{:S(2)}) collective-permute-start(bf16[61,5,16,128]{3,2,1,0:T(8,128)(2,1)S(1)} %join.1.own), channel_id=1, source_target_pairs={{0,12},{1,49},{2,14},{3,51},{4,0},{5,53},{6,2},{7,55},{8,4},{9,57}... | collective-permute-start | bytes 3747848 | tf_op jit(solution)/shard_map/ppermute | solution.py:31
  29.9 0.0 collective-permute-start.4
  29.9 1.5 %collective-permute-start.8 = (bf16[64,7808]{1,0:T(8,128)(2,1)S(1)}, bf16[64,7808]{1,0:T(8,128)(2,1)S(1)}, u32[]{:S(2)}, u32[]{:S(2)}) collective-permute-start(bf16[64,7808]{1,0:T(8,128)(2,1)S(1)} %coadd.1.mine), channel_id=1, source_target_pairs={{0,1},{1,0},{2,3},{3,2},{4,5},{5,4},{6,7},{7,6},{8,9},{9,8},{10,11... | collective-permute-start | bytes 2998280 | tf_op jit(solution)/shard_map/ppermute | solution.py:31
  31.3 11.2 %collective-permute-done.7.direct = bf16[64,7808]{1,0:T(8,128)(2,1)S(1)} collective-permute-done((bf16[64,7808]{1,0:T(8,128)(2,1)S(1)}, bf16[64,7808]{1,0:T(8,128)(2,1)S(1)}, u32[]{:S(2)}, u32[]{:S(2)}) %collective-permute-start.7) | collective-permute-done | bytes 999456 | tf_op jit(solution)/shard_map/ppermute | solution.py:31
  42.6 2.5 %collective-permute-start.9 = (bf16[64,7808]{1,0:T(8,128)(2,1)S(1)}, bf16[64,7808]{1,0:T(8,128)(2,1)S(1)}, u32[]{:S(2)}, u32[]{:S(2)}) collective-permute-start(bf16[64,7808]{1,0:T(8,128)(2,1)S(1)} %collective-permute-done.7.direct), channel_id=1, source_target_pairs={{0,1},{1,0},{2,3},{3,2},{4,5},{5,4},{6,7},{7,6},{8,9},{9,8},{10,11... | collective-permute-start | bytes 2998280 | tf_op jit(solution)/shard_map/ppermute | solution.py:31
  45.1 0.0 collective-permute-done.5.down
  45.1 0.1 slice.9
  45.1 3.2 %collective-permute-start.11 = (bf16[31,5,16,128]{3,2,1,0:T(8,128)(2,1)S(1)}, bf16[31,5,16,128]{3,2,1,0:T(8,128)(2,1)S(1)}, u32[]{:S(2)}, u32[]{:S(2)}) collective-permute-start(bf16[31,5,16,128]{3,2,1,0:T(8,128)(2,1)S(1)} %slice.9), channel_id=1, source_target_pairs={{0,12},{1,49},{2,14},{3,51},{4,0},{5,53},{6,2},{7,55},{8,4},{9,57}... | collective-permute-start | bytes 1904648 | tf_op jit(solution)/shard_map/ppermute | solution.py:31
  48.3 0.0 collective-permute-done.4.up
  48.3 0.1 slice.8
  48.4 0.3 collective-permute-start.10
  48.6 0.0 collective-permute-done.8.over
  48.6 0.0 collective-permute-done.9.swapped
  48.7 8.6 %first_fit.1.first = f32[4,3,3,8,128]{4,3,2,1,0:T(8,128)S(1)} custom-call(s32[5]{0:T(128)S(1)} %stack.23.place, bf16[61,5,16,128]{3,2,1,0:T(8,128)(2,1)S(1)} %join.1.own, bf16[61,5,16,128]{3,2,1,0:T(8,128)(2,1)S(1)} %collective-permute-done.4.up, bf16[61,5,16,128]{3,2,1,0:T(8,128)(2,1)S(1)} %collective-permute-done.5.down, bf16[64,7808]{1,0:T(8,128)(2,1)S(1)} %coadd.1.mine, ...), custom_call_target="tpu_custom_call" | custom-call | bytes 36000000 | tf_op jit(solution)/shard_map/first_fit/pallas_call | solution.py:352
  57.2 0.0 copy-start.6
  57.2 0.0 copy-start.5
  57.2 1.9 %collective-permute-done.10.far_a = bf16[30,5,16,128]{3,2,1,0:T(8,128)(2,1)S(1)} collective-permute-done((bf16[30,5,16,128]{3,2,1,0:T(8,128)(2,1)S(1)}, bf16[30,5,16,128]{3,2,1,0:T(8,128)(2,1)S(1)}, u32[]{:S(2)}, u32[]{:S(2)}) %collective-permute-start.10) | collective-permute-done | bytes 614432 | tf_op jit(solution)/shard_map/ppermute | solution.py:31
  59.1 0.0 collective-permute-done.11.far_b
  59.1 3.4 %last_fit.1 = (f32[4,3,8,128]{3,2,1,0:T(8,128)S(1)}, f32[4,3,8,128]{3,2,1,0:T(8,128)S(1)}, f32[4,3,8,128]{3,2,1,0:T(8,128)S(1)}, f32[4,3,8,128]{3,2,1,0:T(8,128)S(1)}) custom-call(s32[5]{0:T(128)S(1)} %stack.23.place, f32[4,3,3,8,128]{4,3,2,1,0:T(8,128)S(1)} %first_fit.1.first, bf16[30,5,16,128]{3,2,1,0:T(8,128)(2,1)S(1)} %collective-permute-done.10.far_a, ...), custom_call_target="tpu_custom_call" | custom-call | bytes 18000000 | tf_op jit(solution)/shard_map/last_fit/pallas_call | solution.py:362
  62.6 2.3 %collective-permute-start.12 = (f32[4,3,8,128]{3,2,1,0:T(8,128)S(1)}, f32[4,3,8,128]{3,2,1,0:T(8,128)S(1)}, u32[]{:S(2)}, u32[]{:S(2)}) collective-permute-start(f32[4,3,8,128]{3,2,1,0:T(8,128)S(1)} %get-tuple-element.17), channel_id=1, source_target_pairs={{0,1},{1,0},{2,3},{3,2},{4,5},{5,4},{6,7},{7,6},{8,9},{9,8},{10,11... | collective-permute-start | bytes 147464 | tf_op jit(solution)/shard_map/ppermute | solution.py:31
  64.8 0.3 collective-permute-start.13
  65.2 1.4 %collective-permute-start.14 = (f32[4,3,8,128]{3,2,1,0:T(8,128)S(1)}, f32[4,3,8,128]{3,2,1,0:T(8,128)S(1)}, u32[]{:S(2)}, u32[]{:S(2)}) collective-permute-start(f32[4,3,8,128]{3,2,1,0:T(8,128)S(1)} %get-tuple-element.19), channel_id=1, source_target_pairs={{0,3},{1,2},{2,1},{3,0},{4,7},{5,6},{6,5},{7,4},{8,11},{9,10},{10,... | collective-permute-start | bytes 147464 | tf_op jit(solution)/shard_map/ppermute | solution.py:31
  66.6 0.1 reshape_tile.3.classes
  66.6 0.0 collective-permute-done.12.part_1
  66.6 1.1 %collective-permute-done.13.part_2 = f32[4,3,8,128]{3,2,1,0:T(8,128)S(1)} collective-permute-done((f32[4,3,8,128]{3,2,1,0:T(8,128)S(1)}, f32[4,3,8,128]{3,2,1,0:T(8,128)S(1)}, u32[]{:S(2)}, u32[]{:S(2)}) %collective-permute-start.13) | collective-permute-done | bytes 49184 | tf_op jit(solution)/shard_map/ppermute | solution.py:31
  67.8 1.6 %collective-permute-done.14.part_3 = f32[4,3,8,128]{3,2,1,0:T(8,128)S(1)} collective-permute-done((f32[4,3,8,128]{3,2,1,0:T(8,128)S(1)}, f32[4,3,8,128]{3,2,1,0:T(8,128)S(1)}, u32[]{:S(2)}, u32[]{:S(2)}) %collective-permute-start.14) | collective-permute-done | bytes 49184 | tf_op jit(solution)/shard_map/ppermute | solution.py:31
  69.4 1.7 %final.1 = (f32[10,32,128]{2,1,0:T(8,128)}, f32[32,128]{1,0:T(8,128)}, f32[1,32]{1,0:T(1,128)}) custom-call(s32[5]{0:T(128)S(1)} %stack.23.place, s32[3]{0:T(128)S(1)} %copy-done.5, s32[1,128]{1,0:T(1,128)S(1)} %reshape_tile.3.classes, f32[4,3,8,128]{3,2,1,0:T(8,128)S(1)} %get-tuple-element.16.part_0, f32[4,3,8,128]{3,2,1,0:T(8,128)S(1)} %collective-permute-done.12.part_1, ...), custom_call_target="tpu_custom_call" | custom-call | bytes 6000000 | tf_op jit(solution)/shard_map/final/pallas_call | solution.py:379
  (9 shorter events, 0.0 us)
Async XLA Ops:
  0.8 1.0 %copy-start.2 = (bf16[2,10,7808]{2,0,1:T(2,128)(2,1)S(1)}, bf16[2,10,7808]{2,0,1:T(2,128)(2,1)}, u32[]{:S(2)}) copy-start(bf16[2,10,7808]{2,0,1:T(2,128)(2,1)} %param.11) | copy-start | bytes 936964
  2.4 10.1 %collective-permute-start = (bf16[1,10,16,512]{3,2,1,0:T(8,128)(2,1)S(1)}, bf16[1,10,16,512]{3,2,1,0:T(8,128)(2,1)S(1)}, u32[]{:S(2)}, u32[]{:S(2)}) collective-permute-start(bf16[1,10,16,512]{3,2,1,0:T(8,128)(2,1)S(1)} %prep.1), channel_id=1, source_target_pairs={{0,64},{1,65},{2,66},{3,67},{4,68},{5,69},{6,70},{7,71},{8,72},{9,... | collective-permute-start | bytes 491528 | tf_op jit(solution)/shard_map/ppermute | solution.py:31
  6.0 1.4 %copy-start = (bf16[96,7808]{1,0:T(8,128)(2,1)S(1)}, bf16[96,7808]{1,0:T(8,128)(2,1)}, u32[]{:S(2)}) copy-start(bf16[96,7808]{1,0:T(8,128)(2,1)} %flux.1) | copy-start | bytes 4497412
  7.4 1.4 %copy-start.1 = (bf16[96,7808]{1,0:T(8,128)(2,1)S(1)}, bf16[96,7808]{1,0:T(8,128)(2,1)}, u32[]{:S(2)}) copy-start(bf16[96,7808]{1,0:T(8,128)(2,1)} %ivar.1) | copy-start | bytes 4497412
  8.8 0.8 %copy-start.3 = (s32[96,61]{0,1:T(8,128)S(1)}, s32[96,61]{0,1:T(8,128)}, u32[]{:S(2)}) copy-start(s32[96,61]{0,1:T(8,128)} %param.9) | copy-start | bytes 70276
  9.6 0.7 copy-start.4
  12.5 5.5 %collective-permute-start.6 = (bf16[112,7808]{1,0:T(8,128)(2,1)S(1)}, bf16[112,7808]{1,0:T(8,128)(2,1)S(1)}, u32[]{:S(2)}, u32[]{:S(2)}) collective-permute-start(bf16[112,7808]{1,0:T(8,128)(2,1)S(1)} %get-tuple-element.14), channel_id=1, source_target_pairs={{0,1},{1,0},{2,3},{3,2},{4,5},{5,4},{6,7},{7,6},{8,9},{9,8},{10,11... | collective-permute-start | bytes 5246984 | tf_op jit(solution)/shard_map/ppermute | solution.py:31
  13.6 7.6 %collective-permute-start.1 = (bf16[2,10,16,512]{3,2,1,0:T(8,128)(2,1)S(1)}, bf16[2,10,16,512]{3,2,1,0:T(8,128)(2,1)S(1)}, u32[]{:S(2)}, u32[]{:S(2)}) collective-permute-start(bf16[2,10,16,512]{3,2,1,0:T(8,128)(2,1)S(1)} %pad_maximum_fusion.own), channel_id=1, source_target_pairs={{0,16},{1,5},{2,18},{3,7},{4,20},{5,9},{6,22},{7,11},{8,24},{9,13}... | collective-permute-start | bytes 983048 | tf_op jit(solution)/shard_map/ppermute | solution.py:31
  15.0 9.1 %collective-permute-start.2 = (bf16[2,10,16,512]{3,2,1,0:T(8,128)(2,1)S(1)}, bf16[2,10,16,512]{3,2,1,0:T(8,128)(2,1)S(1)}, u32[]{:S(2)}, u32[]{:S(2)}) collective-permute-start(bf16[2,10,16,512]{3,2,1,0:T(8,128)(2,1)S(1)} %pad_maximum_fusion.own), channel_id=1, source_target_pairs={{0,48},{1,13},{2,50},{3,15},{4,52},{5,1},{6,54},{7,3},{8,56},{9,5}... | collective-permute-start | bytes 983048 | tf_op jit(solution)/shard_map/ppermute | solution.py:31
  16.5 9.4 %collective-permute-start.3 = (bf16[2,10,16,512]{3,2,1,0:T(8,128)(2,1)S(1)}, bf16[2,10,16,512]{3,2,1,0:T(8,128)(2,1)S(1)}, u32[]{:S(2)}, u32[]{:S(2)}) collective-permute-start(bf16[2,10,16,512]{3,2,1,0:T(8,128)(2,1)S(1)} %pad_maximum_fusion.own), channel_id=1, source_target_pairs={{0,32},{1,9},{2,34},{3,11},{4,36},{5,13},{6,38},{7,15},{8,40},{9,1... | collective-permute-start | bytes 983048 | tf_op jit(solution)/shard_map/ppermute | solution.py:31
  20.5 22.1 %collective-permute-start.7 = (bf16[64,7808]{1,0:T(8,128)(2,1)S(1)}, bf16[64,7808]{1,0:T(8,128)(2,1)S(1)}, u32[]{:S(2)}, u32[]{:S(2)}) collective-permute-start(bf16[64,7808]{1,0:T(8,128)(2,1)S(1)} %coadd.1.mine), channel_id=1, source_target_pairs={{0,2},{1,3},{2,0},{3,1},{4,6},{5,7},{6,4},{7,5},{8,10},{9,11},{10,... | collective-permute-start | bytes 2998280 | tf_op jit(solution)/shard_map/ppermute | solution.py:31
  26.4 18.7 %collective-permute-start.5 = (bf16[61,5,16,128]{3,2,1,0:T(8,128)(2,1)S(1)}, bf16[61,5,16,128]{3,2,1,0:T(8,128)(2,1)S(1)}, u32[]{:S(2)}, u32[]{:S(2)}) collective-permute-start(bf16[61,5,16,128]{3,2,1,0:T(8,128)(2,1)S(1)} %join.1.own), channel_id=1, source_target_pairs={{0,12},{1,49},{2,14},{3,51},{4,0},{5,53},{6,2},{7,55},{8,4},{9,57}... | collective-permute-start | bytes 3747848 | tf_op jit(solution)/shard_map/ppermute | solution.py:31
  29.9 18.4 %collective-permute-start.4 = (bf16[61,5,16,128]{3,2,1,0:T(8,128)(2,1)S(1)}, bf16[61,5,16,128]{3,2,1,0:T(8,128)(2,1)S(1)}, u32[]{:S(2)}, u32[]{:S(2)}) collective-permute-start(bf16[61,5,16,128]{3,2,1,0:T(8,128)(2,1)S(1)} %join.1.own), channel_id=1, source_target_pairs={{0,4},{1,17},{2,6},{3,19},{4,8},{5,21},{6,10},{7,23},{8,12},{9,25}... | collective-permute-start | bytes 3747848 | tf_op jit(solution)/shard_map/ppermute | solution.py:31
  29.9 18.7 %collective-permute-start.8 = (bf16[64,7808]{1,0:T(8,128)(2,1)S(1)}, bf16[64,7808]{1,0:T(8,128)(2,1)S(1)}, u32[]{:S(2)}, u32[]{:S(2)}) collective-permute-start(bf16[64,7808]{1,0:T(8,128)(2,1)S(1)} %coadd.1.mine), channel_id=1, source_target_pairs={{0,1},{1,0},{2,3},{3,2},{4,5},{5,4},{6,7},{7,6},{8,9},{9,8},{10,11... | collective-permute-start | bytes 2998280 | tf_op jit(solution)/shard_map/ppermute | solution.py:31
  42.6 6.0 %collective-permute-start.9 = (bf16[64,7808]{1,0:T(8,128)(2,1)S(1)}, bf16[64,7808]{1,0:T(8,128)(2,1)S(1)}, u32[]{:S(2)}, u32[]{:S(2)}) collective-permute-start(bf16[64,7808]{1,0:T(8,128)(2,1)S(1)} %collective-permute-done.7.direct), channel_id=1, source_target_pairs={{0,1},{1,0},{2,3},{3,2},{4,5},{5,4},{6,7},{7,6},{8,9},{9,8},{10,11... | collective-permute-start | bytes 2998280 | tf_op jit(solution)/shard_map/ppermute | solution.py:31
  45.1 14.0 %collective-permute-start.11 = (bf16[31,5,16,128]{3,2,1,0:T(8,128)(2,1)S(1)}, bf16[31,5,16,128]{3,2,1,0:T(8,128)(2,1)S(1)}, u32[]{:S(2)}, u32[]{:S(2)}) collective-permute-start(bf16[31,5,16,128]{3,2,1,0:T(8,128)(2,1)S(1)} %slice.9), channel_id=1, source_target_pairs={{0,12},{1,49},{2,14},{3,51},{4,0},{5,53},{6,2},{7,55},{8,4},{9,57}... | collective-permute-start | bytes 1904648 | tf_op jit(solution)/shard_map/ppermute | solution.py:31
  48.4 10.8 %collective-permute-start.10 = (bf16[30,5,16,128]{3,2,1,0:T(8,128)(2,1)S(1)}, bf16[30,5,16,128]{3,2,1,0:T(8,128)(2,1)S(1)}, u32[]{:S(2)}, u32[]{:S(2)}) collective-permute-start(bf16[30,5,16,128]{3,2,1,0:T(8,128)(2,1)S(1)} %slice.8), channel_id=1, source_target_pairs={{0,4},{1,17},{2,6},{3,19},{4,8},{5,21},{6,10},{7,23},{8,12},{9,25}... | collective-permute-start | bytes 1843208 | tf_op jit(solution)/shard_map/ppermute | solution.py:31
  57.2 9.3 %copy-start.6 = (s32[32]{0:T(128)S(1)}, s32[32]{0:T(128)}, u32[]{:S(2)}) copy-start(s32[32]{0:T(128)} %param.13) | copy-start | bytes 388
  57.2 12.1 %copy-start.5 = (s32[3]{0:T(128)S(1)}, s32[3]{0:T(128)}, u32[]{:S(2)}) copy-start(s32[3]{0:T(128)} %counts.1) | copy-start | bytes 40
  62.6 4.1 %collective-permute-start.12 = (f32[4,3,8,128]{3,2,1,0:T(8,128)S(1)}, f32[4,3,8,128]{3,2,1,0:T(8,128)S(1)}, u32[]{:S(2)}, u32[]{:S(2)}) collective-permute-start(f32[4,3,8,128]{3,2,1,0:T(8,128)S(1)} %get-tuple-element.17), channel_id=1, source_target_pairs={{0,1},{1,0},{2,3},{3,2},{4,5},{5,4},{6,7},{7,6},{8,9},{9,8},{10,11... | collective-permute-start | bytes 147464 | tf_op jit(solution)/shard_map/ppermute | solution.py:31
  64.8 3.0 %collective-permute-start.13 = (f32[4,3,8,128]{3,2,1,0:T(8,128)S(1)}, f32[4,3,8,128]{3,2,1,0:T(8,128)S(1)}, u32[]{:S(2)}, u32[]{:S(2)}) collective-permute-start(f32[4,3,8,128]{3,2,1,0:T(8,128)S(1)} %get-tuple-element.18), channel_id=1, source_target_pairs={{0,2},{1,3},{2,0},{3,1},{4,6},{5,7},{6,4},{7,5},{8,10},{9,11},{10,... | collective-permute-start | bytes 147464 | tf_op jit(solution)/shard_map/ppermute | solution.py:31
  65.2 4.2 %collective-permute-start.14 = (f32[4,3,8,128]{3,2,1,0:T(8,128)S(1)}, f32[4,3,8,128]{3,2,1,0:T(8,128)S(1)}, u32[]{:S(2)}, u32[]{:S(2)}) collective-permute-start(f32[4,3,8,128]{3,2,1,0:T(8,128)S(1)} %get-tuple-element.19), channel_id=1, source_target_pairs={{0,3},{1,2},{2,1},{3,0},{4,7},{5,6},{6,5},{7,4},{8,11},{9,10},{10,... | collective-permute-start | bytes 147464 | tf_op jit(solution)/shard_map/ppermute | solution.py:31

commit v4 on v3

v4 whole, which is shorter than its diff:
```python
import jax
import jax.numpy as jnp
import numpy as np
from jax import lax
from jax.experimental import pallas as pl
from jax.experimental.pallas import tpu as pltpu
from jax.sharding import PartitionSpec as P

AXES = ("tmpl", "spec", "expo")
SIDES = (2, 4, 4, 2, 2)
TERMS = 10
HALVES = TERMS // 2
SLICES = 16
WIDTH = 512
COMBOS = 30
ROWS = COMBOS * 16 + TERMS * 8
VMEM = 24 * 1024 * 1024


def moved(device, core=0, x_hi=0, x=0, along=None, step=0):
    h, z, y, lo, c = (int(v) for v in np.unravel_index(device, SIDES))
    if along is not None:
        if (c == 0) == (along == 0):
            z = (z + step) % 4
        else:
            y = (y + step) % 4
    h, lo = divmod((2 * h + lo + (x if c == 0 else -x)) % 4, 2)
    return int(np.ravel_multi_index((h ^ x_hi, z, y, lo, c ^ core), SIDES))


def send(value, **how):
    return lax.ppermute(value, AXES, [(d, moved(d, **how)) for d in range(128)])


def combos():
    out = [(m, n, 0) for m in range(HALVES) for n in range(m + 1, HALVES)]
    out += [(m, n, 1) for m in range(HALVES) for n in range(m + 1, HALVES)]
    out += [(m, m, 0) for m in range(HALVES)]
    out += [(m, m, 1) for m in range(HALVES)]
    return out


def entry_rows():
    where = {}
    for i, (m, n, crossed) in enumerate(combos()):
        for half in range(2):
            k, l = 2 * m + half, 2 * n + (half ^ crossed)
            where.setdefault((min(k, l), max(k, l)), i * 16 + half * 8)
    return where


def prep_kernel(place, basis, out, rows):
    core = place[0]
    pixels = basis.shape[2]
    tail = pixels - (SLICES - 1) * WIDTH
    rows[...] = jnp.zeros_like(rows)
    for k in range(TERMS):
        both = basis[k].astype(jnp.float32)
        mine = jnp.where(core == 0, both[0:1], both[1:2])
        for h in range(SLICES):
            width = WIDTH if h < SLICES - 1 else tail
            rows[k * SLICES + h : k * SLICES + h + 1, :width] = mine[:, h * WIDTH : h * WIDTH + width]
    out[...] = rows[...].astype(jnp.bfloat16).reshape(out.shape)


def weight_kernel(place, flux, ivar, mask, owner, keep, out, flux_in, ivar_in, mask_in, owner_in, sems):
    core = place[0]
    count, pixels = flux_in.shape
    height = 32
    copies = [(mask, mask_in), (owner, owner_in)]
    for at in range(0, count, height):
        copies += [(a.at[pl.ds(at, height), :], b.at[pl.ds(at, height), :]) for a, b in ((ivar, ivar_in), (flux, flux_in))]
    copies = [pltpu.make_async_copy(a, b, sems.at[i]) for i, (a, b) in enumerate(copies)]
    for copy in copies:
        copy.start()
    copies[0].wait()
    copies[1].wait()
    good = mask_in[...].astype(jnp.float32).T
    names = owner_in[...].astype(jnp.float32)
    out[count : count + 16, :] = jnp.zeros((16, pixels), jnp.bfloat16)
    out[count : count + 16, 0:count] = jnp.broadcast_to(names, (16, count)).astype(jnp.bfloat16)
    for i, at in enumerate(range(0, count, height)):
        copies[2 + 2 * i].wait()
        copies[3 + 2 * i].wait()
        for b in range(good.shape[1]):
            here = slice(at, at + height), slice(b * 128, (b + 1) * 128)
            flag = jnp.broadcast_to(good[at : at + height, b : b + 1], (height, 128)).astype(jnp.bfloat16)
            masked = (ivar_in[here] * flag).astype(jnp.float32)
            fluxes = masked * flux_in[here].astype(jnp.float32)
            keep[here] = jnp.where(core == 0, masked, fluxes).astype(jnp.bfloat16)
            out[here] = jnp.where(core == 0, fluxes, masked).astype(jnp.bfloat16)


def coadd_kernel(place, names, own, other, coadd):
    core = place[0]
    count, pixels = own.shape
    row = lax.broadcasted_iota(jnp.int32, (64, count), 0)
    wanted = jnp.where(row < 32, row + core * 32, row - core * 32).astype(jnp.float32)
    near = (names[...].astype(jnp.float32) == wanted).astype(jnp.float32)
    far = (other[count : count + 16, 0:count][0:1].astype(jnp.float32) == wanted).astype(jnp.float32)
    select = jnp.concatenate([near, far], axis=1).astype(jnp.bfloat16)
    for at in range(0, pixels, WIDTH):
        lanes = slice(at, min(at + WIDTH, pixels))
        spectra = jnp.concatenate([own[:, lanes], other[0:count, lanes]], axis=0)
        coadd[:, lanes] = jnp.dot(select, spectra, preferred_element_type=jnp.float32).astype(jnp.bfloat16)


def join_kernel(own, up, down, far, *halves):
    side = SLICES * 16
    row = lax.broadcasted_iota(jnp.int32, (side, side), 0)
    col = lax.broadcasted_iota(jnp.int32, (side, side), 1)
    same = ((row // 16) == (col % 16)) & ((row % 8) == (col // 32)) & ((row // 8) % 2 == (col // 16) % 2)
    order = same.astype(jnp.float32).astype(jnp.bfloat16)
    for m in range(HALVES):
        block = jnp.concatenate(
            [p[:, 2 * m : 2 * m + 2].reshape(p.shape[0] * 2 * SLICES, WIDTH) for p in (own, up, down, far)], axis=0
        )
        turned = jnp.dot(order, block, preferred_element_type=jnp.float32).astype(jnp.bfloat16)
        cut = halves[0].shape[0]
        for block in range(cut + halves[1].shape[0]):
            h, at = block // 4, block % 4 * 128
            out, place = (halves[0], block) if block < cut else (halves[1], block - cut)
            out[place, m] = turned[h * 16 : h * 16 + 16, at : at + 128]


def solve(entries, right):
    lower, scaled, inverse = {}, {}, []
    for j in range(TERMS):
        pivot = entries[j, j]
        for e in range(j):
            pivot = pivot - lower[j, e] * scaled[j, e]
        inverse.append(1.0 / pivot)
        for i in range(j + 1, TERMS):
            value = entries[j, i]
            for e in range(j):
                value = value - lower[i, e] * scaled[j, e]
            scaled[i, j] = value
            lower[i, j] = value * inverse[j]
    forward = []
    for i in range(TERMS):
        value = right[i]
        for e in range(i):
            value = value - lower[i, e] * forward[e]
        forward.append(value)
    answer = [None] * TERMS
    for i in reversed(range(TERMS)):
        value = forward[i] * inverse[i]
        for e in range(i + 1, TERMS):
            value = value - lower[e, i] * answer[e]
        answer[i] = value
    return answer


def fit_blocks(blocks, pixels, stacks, total):
    for at in range(0, pixels // 128, WIDTH // 128):
        taken = range(at, min(at + WIDTH // 128, pixels // 128))
        ivar, wflux = stacks(slice(at * 128, (at + len(taken)) * 128))
        for b, refs in enumerate(blocks):
            evens = []
            for m in range(HALVES):
                pieces = [refs[0][t, m] if t < refs[0].shape[0] else refs[1][t - refs[0].shape[0], m] for t in taken]
                evens.append(jnp.concatenate(pieces, axis=1))
            odds = [jnp.concatenate([e[8:16], e[0:8]], axis=0) for e in evens]
            products = jnp.concatenate(
                [evens[m] * (odds[n] if cross else evens[n]) for m, n, cross in combos()], axis=0
            )
            normal = jnp.dot(products, ivar, preferred_element_type=jnp.float32)
            project = jnp.dot(jnp.concatenate(evens, axis=0), wflux, preferred_element_type=jnp.float32)
            if at == 0:
                total[b, 0 : COMBOS * 16] = normal
                total[b, COMBOS * 16 : ROWS] = project
            else:
                total[b, 0 : COMBOS * 16] += normal
                total[b, COMBOS * 16 : ROWS] += project

    entries = {}
    for (k, l), at in entry_rows().items():
        value = total[:, at : at + 8, :]
        entries[k, l] = value + 1.0 if k == l else value
    right = [total[:, COMBOS * 16 + k * 8 : COMBOS * 16 + k * 8 + 8, :] for k in range(TERMS)]
    answer = solve(entries, right)
    gain = right[0] * answer[0]
    for k in range(1, TERMS):
        gain = gain + right[k] * answer[k]
    values = answer + [gain / TERMS, jnp.zeros_like(gain)]
    lane = lax.broadcasted_iota(jnp.int32, values[0].shape, 2) // 32
    packed = []
    for group in range(4):
        packed.append([])
        for q in range(3):
            out = None
            for k in range(4):
                shift = (k - group) % 4 * 32
                value = values[4 * q + k]
                value = pltpu.roll(value, shift, 2) if shift else value
                out = value if out is None else jnp.where(lane == k, value, out)
            packed[-1].append(out)
    return packed


def own_fit_kernel(place, own_a, own_b, mine, direct_a, direct_b, over, swapped_a, swapped_b, out, ivar, wflux, total):
    core = place[0]

    def stacks(span):
        near = jnp.concatenate([mine[:, span], direct_a[:, span], direct_b[:, span]], axis=0)
        far = jnp.concatenate([over[32:64, span], over[0:32, span], swapped_b[:, span], swapped_a[:, span]], axis=0)
        both = jnp.where(core == 0, near, far).T, jnp.where(core == 0, far, near).T
        ivar[span, :], wflux[span, :] = both
        return both

    packed = fit_blocks([[own_a, own_b]], mine.shape[1], stacks, total)
    for group in range(4):
        for q in range(3):
            out[group, :, q] = packed[group][q]


def near_fit_kernel(up_a, up_b, down_a, down_b, ivar, wflux, out, total):
    packed = fit_blocks([[up_a, up_b], [down_a, down_b]], ivar.shape[0], lambda span: (ivar[span, :], wflux[span, :]), total)
    for group in range(4):
        for q in range(3):
            out[group, :, q] = packed[group][q]


def far_fit_kernel(own, near, far_a, far_b, ivar, wflux, *rest):
    outs, total = rest[:4], rest[4]
    packed = fit_blocks([[far_a, far_b]], ivar.shape[0], lambda span: (ivar[span, :], wflux[span, :]), total)
    for group in range(4):
        outs[group][0:1] = own[group]
        outs[group][1:3] = near[group]
        for q in range(3):
            outs[group][3:4, q] = packed[group][q]


def final_kernel(place, counts, classes, part_0, part_1, part_2, part_3, coefs, gains, best):
    core, lo, hi, z, y = (place[i] for i in range(5))

    def shift(n):
        return jnp.where(n == 1, 3, jnp.where(n == 2, 1, jnp.where(n == 3, 2, 0)))

    def trial_of(i):
        group, b, t = i // 32, (i // 8) % 4, i % 8
        source_core = core ^ (group % 2)
        source_x = (2 * hi + lo + jnp.where(group < 2, 0, jnp.where(core == 0, 1, 3))) % 4
        near, far = shift(t // 2), shift(b)
        z_of = (z + jnp.where(source_core == 0, near, far)) % 4
        y_of = (y + jnp.where(source_core == 0, far, near)) % 4
        return (source_x // 2 ^ (t % 2)) * 64 + z_of * 16 + y_of * 4 + source_x % 2 * 2 + source_core

    trial = trial_of(lax.broadcasted_iota(jnp.int32, (128, 128), 0))
    lane = lax.broadcasted_iota(jnp.int32, (128, 128), 1)
    to_lane = (trial == lane).astype(jnp.float32).astype(jnp.bfloat16)
    end_0 = counts[0]
    end_1 = end_0 + counts[1]
    end_2 = end_1 + counts[2]
    trial_class = sum((trial >= end).astype(jnp.int32) for end in (end_0, end_1, end_2))
    stack = []
    for q in range(3):
        rows = jnp.concatenate([p[:, q].reshape(32, 128) for p in (part_0, part_1, part_2, part_3)], axis=0)
        if q == 2:
            drop = (lane // 32 == 2) & (trial_class != classes[...])
            rows = jnp.where(drop, 0.0, rows)
            best[...] = jnp.max(rows, axis=0, keepdims=True)[:, 64:96]
        rest = rows.T
        for _ in range(3):
            part = rest.astype(jnp.bfloat16)
            stack.append(part)
            rest = rest - part.astype(jnp.float32)
    turned = jnp.dot(jnp.concatenate(stack, axis=0), to_lane, preferred_element_type=jnp.float32)
    for k in range(TERMS + 1):
        at = k // 4 * 384 + k % 4 * 32
        value = turned[at : at + 32] + (turned[at + 128 : at + 160] + turned[at + 256 : at + 288])
        if k < TERMS:
            coefs[k] = value
        else:
            gains[...] = value


def cost(micros):
    return pl.CostEstimate(flops=int(micros * 1e9), bytes_accessed=int(micros * 3.0e6), transcendentals=0)


def body(flux, ivar, pixel_mask, exposure_target, basis, trial_counts, target_class):
    pixels = flux.shape[1]
    tmpl, spec, core = (lax.axis_index(a) for a in AXES)
    place = jnp.stack([core, spec % 2, tmpl // 4, tmpl % 4, spec // 2]).astype(jnp.int32)
    smem = pl.BlockSpec(memory_space=pltpu.SMEM)
    vmem = pl.BlockSpec(memory_space=pltpu.VMEM)
    params = pltpu.CompilerParams(vmem_limit_bytes=VMEM)

    trial = pl.pallas_call(
        prep_kernel,
        out_shape=jax.ShapeDtypeStruct((1, TERMS, SLICES, WIDTH), jnp.bfloat16),
        in_specs=[smem, vmem],
        out_specs=vmem,
        scratch_shapes=[pltpu.VMEM((TERMS * SLICES, WIDTH), jnp.float32)],
        compiler_params=params,
        cost_estimate=cost(0.7),
        name="prep",
    )(place, jnp.transpose(basis, (1, 0, 2)))
    other = send(trial, x_hi=1)
    pair = jnp.concatenate([trial, other], axis=0)

    count = flux.shape[0]
    owners = exposure_target.reshape(1, count)
    views = (flux, ivar, pixel_mask.T, owners)
    keep, outgoing = pl.pallas_call(
        weight_kernel,
        out_shape=(
            jax.ShapeDtypeStruct((count, pixels), jnp.bfloat16),
            jax.ShapeDtypeStruct((count + 16, pixels), jnp.bfloat16),
        ),
        in_specs=[smem] + [pl.BlockSpec(memory_space=pltpu.HBM)] * 4,
        out_specs=(vmem,) * 2,
        scratch_shapes=[pltpu.VMEM(v.shape, v.dtype) for v in views] + [pltpu.SemaphoreType.DMA((8,))],
        compiler_params=params,
        cost_estimate=cost(2.3),
        name="weight",
    )(place, *(pltpu.with_memory_space_constraint(v, pltpu.HBM) for v in views))
    outgoing, _ = lax.optimization_barrier((outgoing, other))
    incoming = send(outgoing, core=1)

    mine = pl.pallas_call(
        coadd_kernel,
        out_shape=jax.ShapeDtypeStruct((64, pixels), jnp.bfloat16),
        in_specs=[smem] + [vmem] * 3,
        out_specs=vmem,
        compiler_params=params,
        cost_estimate=cost(2.4),
        name="coadd",
    )(place, owners, keep, incoming)
    direct = send(mine[:32], x=1), send(mine[32:], x=-1)
    late, _ = lax.optimization_barrier((mine, direct[0]))
    over = send(late, core=1)
    swapped = [send(v, core=1) for v in direct]

    near = [pair] + [send(pair, along=0, step=s) for s in (1, -1, 2)]

    near[0], mine = lax.optimization_barrier((near[0], mine))
    cut = pixels // 256
    eight = pl.pallas_call(
        join_kernel,
        out_shape=tuple(jax.ShapeDtypeStruct((n, HALVES, 16, 128), jnp.bfloat16) for n in (cut, pixels // 128 - cut)),
        in_specs=[vmem] * 4,
        out_specs=(vmem,) * 2,
        compiler_params=params,
        cost_estimate=cost(0.5),
        name="join",
    )(*near)
    up_a, down_b = send(eight[0], along=1, step=1), send(eight[1], along=1, step=-1)
    up_b, down_a = send(eight[1], along=1, step=1), send(eight[0], along=1, step=-1)
    far = send(up_a, along=1, step=1), send(down_b, along=1, step=-1)

    def fit(kernel, operands, shapes, count, micros, name):
        return pl.pallas_call(
            kernel,
            out_shape=shapes,
            in_specs=[smem if v is place else vmem for v in operands],
            out_specs=(vmem,) * len(shapes),
            scratch_shapes=[pltpu.VMEM((count, ROWS, 128), jnp.float32)],
            compiler_params=params,
            cost_estimate=cost(micros),
            name=name,
        )(*operands)

    stack = jax.ShapeDtypeStruct((pixels, 128), jnp.bfloat16)

    def packed(*sizes):
        return jax.ShapeDtypeStruct(sizes + (3, 8, 128), jnp.float32)

    own, *stacks = fit(
        own_fit_kernel, (place, *eight, mine, *direct, over, *swapped), (packed(4, 1), stack, stack), 1, 0, "own_fit"
    )
    (near,) = fit(near_fit_kernel, (up_a, up_b, down_a, down_b, *stacks), (packed(4, 2),), 2, 6, "near_fit")
    parts = fit(far_fit_kernel, (own, near, *far, *stacks), (packed(4),) * 4, 1, 3, "far_fit")

    parts = (
        parts[0],
        send(parts[1], core=1),
        send(parts[2], x=-1),
        send(parts[3], x=1, core=1),
    )
    coefs, gains, best = pl.pallas_call(
        final_kernel,
        out_shape=(
            jax.ShapeDtypeStruct((TERMS, 32, 128), jnp.float32),
            jax.ShapeDtypeStruct((32, 128), jnp.float32),
            jax.ShapeDtypeStruct((1, 32), jnp.float32),
        ),
        in_specs=[smem, smem] + [vmem] * 5,
        out_specs=(vmem,) * 3,
        compiler_params=params,
        cost_estimate=cost(2),
        name="final",
    )(place, trial_counts, jnp.tile(target_class, 4).reshape(1, 128), *parts)
    return coefs, gains, best.reshape(32)


def solution(mesh):
    rows = P(AXES, None)
    return jax.shard_map(
        body,
        mesh=mesh,
        in_specs=(rows, rows, rows, P(AXES), P(("tmpl", "spec"), None, None), P(), P(AXES)),
        out_specs=(P(None, AXES, None), P(AXES, None), P(AXES)),
        check_vma=False,
    )
```

time: 71.3 us -> 67.1 us (0.941)
  starting transfers between devices: 24.4 us -> 32.4 us
  waiting for transfers between devices: 20.9 us -> 13.3 us
  local copies, waits for them, and re-layouts: 5.44 us -> 1.22 us
  Pallas kernels: 19.5 us -> 18.4 us
    ppermute x15 -> x19, starting transfers between devices: 24.4 us -> 32.4 us  [send(): return lax.ppermute(value, AXES, [(d, moved(d, **how)) for d in range(128)])]
    ppermute x15 -> x19, waiting for transfers between devices: 20.9 us -> 13.3 us  [send(): return lax.ppermute(value, AXES, [(d, moved(d, **how)) for d in range(128)])]
    unnamed x14 -> x8, local copies, waits for them, and re-layouts: 5.16 us -> 0.98 us
    pallas_call x1, Pallas kernels: 2.41 us -> 1.29 us  [body(): pl.pallas_call(coadd_kernel, out_shape=jax.ShapeDtypeStruct((64, pixels),...]
    pallas_call x1, Pallas kernels: 2.29 us -> 3.08 us  [body(): pl.pallas_call(weight_kernel, out_shape=(jax.ShapeDtypeStruct((count, pix...]
    pallas_call x3 -> x4, Pallas kernels: 12.5 us -> 11.8 us  [the longest x3 11.3 us: fit(): pl.pallas_call(kernel, out_shape=shapes, in_specs=[smem if v is place els...]
  transfers between devices with their start and end apart: 15 -> 19, of which waited for: 7 -> 8; matrix products, arithmetic and copies ran while one was open for 0% -> 0% of each run, Pallas kernels for 19% -> 20%
where the time goes in v4:
time: 67.1 us; the launch traced here: 66.1 us
  starting transfers between devices  32.4 us (48%)
  Pallas kernels  18.4 us (27%)
  waiting for transfers between devices  13.3 us (20%)
  local copies, waits for them, and re-layouts  1.22 us (2%)
  between operations  0.76 us (1%)
    ppermute x19, starting transfers between devices, send(): return lax.ppermute(value, AXES, [(d, moved(d, **how)) for d in range(128)])  32.4 us
    ppermute x19, waiting for transfers between devices, send(): return lax.ppermute(value, AXES, [(d, moved(d, **how)) for d in range(128)])  13.3 us
    pallas_call x3, Pallas kernels, fit(): pl.pallas_call(kernel, out_shape=shapes, in_specs=[smem if v is place els...  11.3 us
    pallas_call x1, Pallas kernels, body(): pl.pallas_call(weight_kernel, out_shape=(jax.ShapeDtypeStruct((count, pix...  3.08 us
    pallas_call x1, Pallas kernels, body(): pl.pallas_call(final_kernel, out_shape=(jax.ShapeDtypeStruct((TERMS, 32,...  1.61 us
  transfers between devices with their start and end apart: 19, of which 8 were waited for; matrix products, arithmetic and copies ran while one was open for 0% of the time, Pallas kernels for 20%

profile of v4, /device:TPU:1, one launch (start us, length us, event | category | flops | bytes accessed | tf_op | source)
XLA Modules:
  0.0 66.1 jit_solution(2798201272389707842)
XLA Ops:
  0.7 0.1 stack.23.place
  0.8 1.0 %copy-done = bf16[2,10,7808]{2,0,1:T(2,128)(2,1)S(1)} copy-done((bf16[2,10,7808]{2,0,1:T(2,128)(2,1)S(1)}, bf16[2,10,7808]{2,0,1:T(2,128)(2,1)}, u32[]{:S(2)}) %copy-start) | copy-done | bytes 312344
  1.7 0.7 prep.1
  2.4 3.7 %collective-permute-start = (bf16[1,10,16,512]{3,2,1,0:T(8,128)(2,1)S(1)}, bf16[1,10,16,512]{3,2,1,0:T(8,128)(2,1)S(1)}, u32[]{:S(2)}, u32[]{:S(2)}) collective-permute-start(bf16[1,10,16,512]{3,2,1,0:T(8,128)(2,1)S(1)} %prep.1), channel_id=1, source_target_pairs={{0,64},{1,65},{2,66},{3,67},{4,68},{5,69},{6,70},{7,71},{8,72},{9,... | collective-permute-start | bytes 491528 | tf_op jit(solution)/shard_map/ppermute | solution.py:32
  6.0 3.1 %weight.1 = (bf16[96,7808]{1,0:T(8,128)(2,1)S(1)}, bf16[112,7808]{1,0:T(8,128)(2,1)S(1)}) custom-call(s32[5]{0:T(128)S(1)} %stack.23.place, bf16[96,7808]{1,0:T(8,128)(2,1)} %flux.1, bf16[96,7808]{1,0:T(8,128)(2,1)} %ivar.1, s32[61,96]{1,0:T(8,128)} %bitcast.12, s32[1,96]{1,0:T(1,128)} %bitcast.10), custom_call_target="tpu_custom_call" | custom-call | flops 2300000000 | bytes 6899999 | tf_op jit(solution)/shard_map/weight/pallas_call | solution.py:306
  9.1 0.4 collective-permute-done
  9.5 1.7 %collective-permute-start.1 = (bf16[112,7808]{1,0:T(8,128)(2,1)S(1)}, bf16[112,7808]{1,0:T(8,128)(2,1)S(1)}, u32[]{:S(2)}, u32[]{:S(2)}) collective-permute-start(bf16[112,7808]{1,0:T(8,128)(2,1)S(1)} %get-tuple-element.23), channel_id=1, source_target_pairs={{0,1},{1,0},{2,3},{3,2},{4,5},{5,4},{6,7},{7,6},{8,9},{9,8},{10,11... | collective-permute-start | bytes 5246984 | tf_op jit(solution)/shard_map/ppermute | solution.py:32
  11.2 1.6 %collective-permute-start.2 = (bf16[2,10,16,512]{3,2,1,0:T(8,128)(2,1)S(1)}, bf16[2,10,16,512]{3,2,1,0:T(8,128)(2,1)S(1)}, u32[]{:S(2)}, u32[]{:S(2)}) collective-permute-start(bf16[2,10,16,512]{3,2,1,0:T(8,128)(2,1)S(1)} %pad_maximum_fusion.own), channel_id=1, source_target_pairs={{0,16},{1,5},{2,18},{3,7},{4,20},{5,9},{6,22},{7,11},{8,24},{9,13}... | collective-permute-start | bytes 983048 | tf_op jit(solution)/shard_map/ppermute | solution.py:32
  12.8 1.5 %collective-permute-start.3 = (bf16[2,10,16,512]{3,2,1,0:T(8,128)(2,1)S(1)}, bf16[2,10,16,512]{3,2,1,0:T(8,128)(2,1)S(1)}, u32[]{:S(2)}, u32[]{:S(2)}) collective-permute-start(bf16[2,10,16,512]{3,2,1,0:T(8,128)(2,1)S(1)} %pad_maximum_fusion.own), channel_id=1, source_target_pairs={{0,48},{1,13},{2,50},{3,15},{4,52},{5,1},{6,54},{7,3},{8,56},{9,5}... | collective-permute-start | bytes 983048 | tf_op jit(solution)/shard_map/ppermute | solution.py:32
  14.3 1.6 %collective-permute-start.4 = (bf16[2,10,16,512]{3,2,1,0:T(8,128)(2,1)S(1)}, bf16[2,10,16,512]{3,2,1,0:T(8,128)(2,1)S(1)}, u32[]{:S(2)}, u32[]{:S(2)}) collective-permute-start(bf16[2,10,16,512]{3,2,1,0:T(8,128)(2,1)S(1)} %pad_maximum_fusion.own), channel_id=1, source_target_pairs={{0,32},{1,9},{2,34},{3,11},{4,36},{5,13},{6,38},{7,15},{8,40},{9,1... | collective-permute-start | bytes 983048 | tf_op jit(solution)/shard_map/ppermute | solution.py:32
  15.9 0.0 collective-permute-done.1.other
  15.9 1.3 %coadd.1.mine = bf16[64,7808]{1,0:T(8,128)(2,1)S(1)} custom-call(s32[5]{0:T(128)S(1)} %stack.23.place, s32[1,96]{1,0:T(1,128)S(1)} %bitcast.11, bf16[96,7808]{1,0:T(8,128)(2,1)S(1)} %get-tuple-element.21.own, bf16[112,7808]{1,0:T(8,128)(2,1)S(1)} %collective-permute-done.1.other), custom_call_target="tpu_custom_call" | custom-call | flops 2400000000 | bytes 7200000 | tf_op jit(solution)/shard_map/coadd/pallas_call | solution.py:322
  17.2 0.1 fusion
  17.3 2.5 %collective-permute-start.5 = (bf16[32,7808]{1,0:T(8,128)(2,1)S(1)}, bf16[32,7808]{1,0:T(8,128)(2,1)S(1)}, u32[]{:S(2)}, u32[]{:S(2)}) collective-permute-start(bf16[32,7808]{1,0:T(8,128)(2,1)S(1)} %get-tuple-element.40), channel_id=1, source_target_pairs={{0,2},{1,67},{2,64},{3,1},{4,6},{5,71},{6,68},{7,5},{8,10},{9,75},... | collective-permute-start | bytes 1499144 | tf_op jit(solution)/shard_map/ppermute | solution.py:32
  19.8 0.0 collective-permute-done.2.up
  19.8 2.0 %collective-permute-done.3.down = bf16[2,10,16,512]{3,2,1,0:T(8,128)(2,1)S(1)} collective-permute-done((bf16[2,10,16,512]{3,2,1,0:T(8,128)(2,1)S(1)}, bf16[2,10,16,512]{3,2,1,0:T(8,128)(2,1)S(1)}, u32[]{:S(2)}, u32[]{:S(2)}) %collective-permute-start.3) | collective-permute-done | bytes 327712 | tf_op jit(solution)/shard_map/ppermute | solution.py:32
  21.9 1.8 %collective-permute-done.4.far = bf16[2,10,16,512]{3,2,1,0:T(8,128)(2,1)S(1)} collective-permute-done((bf16[2,10,16,512]{3,2,1,0:T(8,128)(2,1)S(1)}, bf16[2,10,16,512]{3,2,1,0:T(8,128)(2,1)S(1)}, u32[]{:S(2)}, u32[]{:S(2)}) %collective-permute-start.4) | collective-permute-done | bytes 327712 | tf_op jit(solution)/shard_map/ppermute | solution.py:32
  23.7 0.5 join.1
  24.2 3.5 %collective-permute-start.13 = (bf16[31,5,16,128]{3,2,1,0:T(8,128)(2,1)S(1)}, bf16[31,5,16,128]{3,2,1,0:T(8,128)(2,1)S(1)}, u32[]{:S(2)}, u32[]{:S(2)}) collective-permute-start(bf16[31,5,16,128]{3,2,1,0:T(8,128)(2,1)S(1)} %get-tuple-element.26.own_b), channel_id=1, source_target_pairs={{0,12},{1,49},{2,14},{3,51},{4,0},{5,53},{6,2},{7,55},{8,4},{9,57}... | collective-permute-start | bytes 1904648 | tf_op jit(solution)/shard_map/ppermute | solution.py:32
  27.8 0.0 collective-permute-start.10
  27.8 1.2 %collective-permute-start.6 = (bf16[32,7808]{1,0:T(8,128)(2,1)S(1)}, bf16[32,7808]{1,0:T(8,128)(2,1)S(1)}, u32[]{:S(2)}, u32[]{:S(2)}) collective-permute-start(bf16[32,7808]{1,0:T(8,128)(2,1)S(1)} %get-tuple-element.39), channel_id=1, source_target_pairs={{0,66},{1,3},{2,0},{3,65},{4,70},{5,7},{6,4},{7,69},{8,74},{9,11},... | collective-permute-start | bytes 1499144 | tf_op jit(solution)/shard_map/ppermute | solution.py:32
  29.0 0.0 collective-permute-done.5.direct_a
  29.0 3.0 %collective-permute-start.7 = (bf16[64,7808]{1,0:T(8,128)(2,1)S(1)}, bf16[64,7808]{1,0:T(8,128)(2,1)S(1)}, u32[]{:S(2)}, u32[]{:S(2)}) collective-permute-start(bf16[64,7808]{1,0:T(8,128)(2,1)S(1)} %coadd.1.mine), channel_id=1, source_target_pairs={{0,1},{1,0},{2,3},{3,2},{4,5},{5,4},{6,7},{7,6},{8,9},{9,8},{10,11... | collective-permute-start | bytes 2998280 | tf_op jit(solution)/shard_map/ppermute | solution.py:32
  31.9 1.1 %collective-permute-start.11 = (bf16[31,5,16,128]{3,2,1,0:T(8,128)(2,1)S(1)}, bf16[31,5,16,128]{3,2,1,0:T(8,128)(2,1)S(1)}, u32[]{:S(2)}, u32[]{:S(2)}) collective-permute-start(bf16[31,5,16,128]{3,2,1,0:T(8,128)(2,1)S(1)} %get-tuple-element.26.own_b), channel_id=1, source_target_pairs={{0,4},{1,17},{2,6},{3,19},{4,8},{5,21},{6,10},{7,23},{8,12},{9,25}... | collective-permute-start | bytes 1904648 | tf_op jit(solution)/shard_map/ppermute | solution.py:32
  33.1 3.9 %collective-permute-done.6.direct_b = bf16[32,7808]{1,0:T(8,128)(2,1)S(1)} collective-permute-done((bf16[32,7808]{1,0:T(8,128)(2,1)S(1)}, bf16[32,7808]{1,0:T(8,128)(2,1)S(1)}, u32[]{:S(2)}, u32[]{:S(2)}) %collective-permute-start.6) | collective-permute-done | bytes 499744 | tf_op jit(solution)/shard_map/ppermute | solution.py:32
  37.0 2.7 %collective-permute-start.12 = (bf16[30,5,16,128]{3,2,1,0:T(8,128)(2,1)S(1)}, bf16[30,5,16,128]{3,2,1,0:T(8,128)(2,1)S(1)}, u32[]{:S(2)}, u32[]{:S(2)}) collective-permute-start(bf16[30,5,16,128]{3,2,1,0:T(8,128)(2,1)S(1)} %get-tuple-element.25.own_a), channel_id=1, source_target_pairs={{0,12},{1,49},{2,14},{3,51},{4,0},{5,53},{6,2},{7,55},{8,4},{9,57}... | collective-permute-start | bytes 1843208 | tf_op jit(solution)/shard_map/ppermute | solution.py:32
  39.7 0.0 collective-permute-done.10.up_a
  39.7 1.9 %collective-permute-start.8 = (bf16[32,7808]{1,0:T(8,128)(2,1)S(1)}, bf16[32,7808]{1,0:T(8,128)(2,1)S(1)}, u32[]{:S(2)}, u32[]{:S(2)}) collective-permute-start(bf16[32,7808]{1,0:T(8,128)(2,1)S(1)} %collective-permute-done.5.direct_a), channel_id=1, source_target_pairs={{0,1},{1,0},{2,3},{3,2},{4,5},{5,4},{6,7},{7,6},{8,9},{9,8},{10,11... | collective-permute-start | bytes 1499144 | tf_op jit(solution)/shard_map/ppermute | solution.py:32
  41.6 0.0 collective-permute-done.13.down_b
  41.6 0.1 collective-permute-start.9
  41.7 1.4 %collective-permute-done.8.swapped_a = bf16[32,7808]{1,0:T(8,128)(2,1)S(1)} collective-permute-done((bf16[32,7808]{1,0:T(8,128)(2,1)S(1)}, bf16[32,7808]{1,0:T(8,128)(2,1)S(1)}, u32[]{:S(2)}, u32[]{:S(2)}) %collective-permute-start.8) | collective-permute-done | bytes 499744 | tf_op jit(solution)/shard_map/ppermute | solution.py:32
  43.1 1.6 %collective-permute-start.15 = (bf16[31,5,16,128]{3,2,1,0:T(8,128)(2,1)S(1)}, bf16[31,5,16,128]{3,2,1,0:T(8,128)(2,1)S(1)}, u32[]{:S(2)}, u32[]{:S(2)}) collective-permute-start(bf16[31,5,16,128]{3,2,1,0:T(8,128)(2,1)S(1)} %collective-permute-done.13.down_b), channel_id=1, source_target_pairs={{0,12},{1,49},{2,14},{3,51},{4,0},{5,53},{6,2},{7,55},{8,4},{9,57}... | collective-permute-start | bytes 1904648 | tf_op jit(solution)/shard_map/ppermute | solution.py:32
  44.7 0.0 collective-permute-done.9.swapped_b
  44.7 0.3 collective-permute-start.14
  45.0 0.0 collective-permute-done.7.over
  45.0 3.4 %own_fit.1 = (f32[4,1,3,8,128]{4,3,2,1,0:T(8,128)S(1)}, bf16[7808,128]{1,0:T(8,128)(2,1)S(1)}, bf16[7808,128]{1,0:T(8,128)(2,1)S(1)}) custom-call(s32[5]{0:T(128)S(1)} %stack.23.place, bf16[30,5,16,128]{3,2,1,0:T(8,128)(2,1)S(1)} %get-tuple-element.25.own_a, bf16[31,5,16,128]{3,2,1,0:T(8,128)(2,1)S(1)} %get-tuple-element.26.own_b, ...), custom_call_target="tpu_custom_call" | custom-call | tf_op jit(solution)/shard_map/own_fit/pallas_call | solution.py:354
  48.4 0.0 collective-permute-done.11.up_b
  48.4 5.2 %near_fit.1.near = f32[4,2,3,8,128]{4,3,2,1,0:T(8,128)S(1)} custom-call(bf16[30,5,16,128]{3,2,1,0:T(8,128)(2,1)S(1)} %collective-permute-done.10.up_a, bf16[31,5,16,128]{3,2,1,0:T(8,128)(2,1)S(1)} %collective-permute-done.11.up_b, bf16[30,5,16,128]{3,2,1,0:T(8,128)(2,1)S(1)} %collective-permute-done.12.down_a, ...), custom_call_target="tpu_custom_call" | custom-call | flops 6000000000 | bytes 18000000 | tf_op jit(solution)/shard_map/near_fit/pallas_call | solution.py:354
  53.6 1.6 %collective-permute-done.14.far_a = bf16[30,5,16,128]{3,2,1,0:T(8,128)(2,1)S(1)} collective-permute-done((bf16[30,5,16,128]{3,2,1,0:T(8,128)(2,1)S(1)}, bf16[30,5,16,128]{3,2,1,0:T(8,128)(2,1)S(1)}, u32[]{:S(2)}, u32[]{:S(2)}) %collective-permute-start.14) | collective-permute-done | bytes 614432 | tf_op jit(solution)/shard_map/ppermute | solution.py:32
  55.2 0.0 collective-permute-done.15.far_b
  55.2 2.7 %far_fit.1 = (f32[4,3,8,128]{3,2,1,0:T(8,128)S(1)}, f32[4,3,8,128]{3,2,1,0:T(8,128)S(1)}, f32[4,3,8,128]{3,2,1,0:T(8,128)S(1)}, f32[4,3,8,128]{3,2,1,0:T(8,128)S(1)}) custom-call(f32[4,1,3,8,128]{4,3,2,1,0:T(8,128)S(1)} %get-tuple-element.29.own, f32[4,2,3,8,128]{4,3,2,1,0:T(8,128)S(1)} %near_fit.1.near, ...), custom_call_target="tpu_custom_call" | custom-call | flops 3000000000 | bytes 9000000 | tf_op jit(solution)/shard_map/far_fit/pallas_call | solution.py:354
  57.9 1.0 %collective-permute-start.16 = (f32[4,3,8,128]{3,2,1,0:T(8,128)S(1)}, f32[4,3,8,128]{3,2,1,0:T(8,128)S(1)}, u32[]{:S(2)}, u32[]{:S(2)}) collective-permute-start(f32[4,3,8,128]{3,2,1,0:T(8,128)S(1)} %get-tuple-element.33), channel_id=1, source_target_pairs={{0,1},{1,0},{2,3},{3,2},{4,5},{5,4},{6,7},{7,6},{8,9},{9,8},{10,11... | collective-permute-start | bytes 147464 | tf_op jit(solution)/shard_map/ppermute | solution.py:32
  58.9 0.9 %collective-permute-start.17 = (f32[4,3,8,128]{3,2,1,0:T(8,128)S(1)}, f32[4,3,8,128]{3,2,1,0:T(8,128)S(1)}, u32[]{:S(2)}, u32[]{:S(2)}) collective-permute-start(f32[4,3,8,128]{3,2,1,0:T(8,128)S(1)} %get-tuple-element.34), channel_id=1, source_target_pairs={{0,66},{1,3},{2,0},{3,65},{4,70},{5,7},{6,4},{7,69},{8,74},{9,11},... | collective-permute-start | bytes 147464 | tf_op jit(solution)/shard_map/ppermute | solution.py:32
  59.8 2.5 %collective-permute-start.18 = (f32[4,3,8,128]{3,2,1,0:T(8,128)S(1)}, f32[4,3,8,128]{3,2,1,0:T(8,128)S(1)}, u32[]{:S(2)}, u32[]{:S(2)}) collective-permute-start(f32[4,3,8,128]{3,2,1,0:T(8,128)S(1)} %get-tuple-element.35), channel_id=1, source_target_pairs={{0,3},{1,66},{2,65},{3,0},{4,7},{5,70},{6,69},{7,4},{8,11},{9,74},... | collective-permute-start | bytes 147464 | tf_op jit(solution)/shard_map/ppermute | solution.py:32
  62.4 0.1 reshape_tile.3.classes
  62.4 1.3 %collective-permute-done.17.part_2 = f32[4,3,8,128]{3,2,1,0:T(8,128)S(1)} collective-permute-done((f32[4,3,8,128]{3,2,1,0:T(8,128)S(1)}, f32[4,3,8,128]{3,2,1,0:T(8,128)S(1)}, u32[]{:S(2)}, u32[]{:S(2)}) %collective-permute-start.17) | collective-permute-done | bytes 49184 | tf_op jit(solution)/shard_map/ppermute | solution.py:32
  63.8 0.8 %collective-permute-done.18.part_3 = f32[4,3,8,128]{3,2,1,0:T(8,128)S(1)} collective-permute-done((f32[4,3,8,128]{3,2,1,0:T(8,128)S(1)}, f32[4,3,8,128]{3,2,1,0:T(8,128)S(1)}, u32[]{:S(2)}, u32[]{:S(2)}) %collective-permute-start.18) | collective-permute-done | bytes 49184 | tf_op jit(solution)/shard_map/ppermute | solution.py:32
  64.5 1.6 %final.1 = (f32[10,32,128]{2,1,0:T(8,128)}, f32[32,128]{1,0:T(8,128)}, f32[1,32]{1,0:T(1,128)}) custom-call(s32[5]{0:T(128)S(1)} %stack.23.place, s32[3]{0:T(128)S(1)} %copy-done.2, s32[1,128]{1,0:T(1,128)S(1)} %reshape_tile.3.classes, f32[4,3,8,128]{3,2,1,0:T(8,128)S(1)} %get-tuple-element.32.part_0, f32[4,3,8,128]{3,2,1,0:T(8,128)S(1)} %collective-permute-done.16.part_1, ...), custom_call_target="tpu_custom_call" | custom-call | flops 2000000000 | bytes 6000000 | tf_op jit(solution)/shard_map/final/pallas_call | solution.py:382
  (11 shorter events, 0.1 us)
Async XLA Ops:
  0.8 1.0 %copy-start = (bf16[2,10,7808]{2,0,1:T(2,128)(2,1)S(1)}, bf16[2,10,7808]{2,0,1:T(2,128)(2,1)}, u32[]{:S(2)}) copy-start(bf16[2,10,7808]{2,0,1:T(2,128)(2,1)} %param.11) | copy-start | bytes 936964
  2.4 7.1 %collective-permute-start = (bf16[1,10,16,512]{3,2,1,0:T(8,128)(2,1)S(1)}, bf16[1,10,16,512]{3,2,1,0:T(8,128)(2,1)S(1)}, u32[]{:S(2)}, u32[]{:S(2)}) collective-permute-start(bf16[1,10,16,512]{3,2,1,0:T(8,128)(2,1)S(1)} %prep.1), channel_id=1, source_target_pairs={{0,64},{1,65},{2,66},{3,67},{4,68},{5,69},{6,70},{7,71},{8,72},{9,... | collective-permute-start | bytes 491528 | tf_op jit(solution)/shard_map/ppermute | solution.py:32
  6.0 9.9 %copy-start.1 = (s32[96]{0:T(128)S(1)}, s32[96]{0:T(128)}, u32[]{:S(2)}) copy-start(s32[96]{0:T(128)} %param.10) | copy-start | bytes 1156
  9.5 6.4 %collective-permute-start.1 = (bf16[112,7808]{1,0:T(8,128)(2,1)S(1)}, bf16[112,7808]{1,0:T(8,128)(2,1)S(1)}, u32[]{:S(2)}, u32[]{:S(2)}) collective-permute-start(bf16[112,7808]{1,0:T(8,128)(2,1)S(1)} %get-tuple-element.23), channel_id=1, source_target_pairs={{0,1},{1,0},{2,3},{3,2},{4,5},{5,4},{6,7},{7,6},{8,9},{9,8},{10,11... | collective-permute-start | bytes 5246984 | tf_op jit(solution)/shard_map/ppermute | solution.py:32
  11.2 8.6 %collective-permute-start.2 = (bf16[2,10,16,512]{3,2,1,0:T(8,128)(2,1)S(1)}, bf16[2,10,16,512]{3,2,1,0:T(8,128)(2,1)S(1)}, u32[]{:S(2)}, u32[]{:S(2)}) collective-permute-start(bf16[2,10,16,512]{3,2,1,0:T(8,128)(2,1)S(1)} %pad_maximum_fusion.own), channel_id=1, source_target_pairs={{0,16},{1,5},{2,18},{3,7},{4,20},{5,9},{6,22},{7,11},{8,24},{9,13}... | collective-permute-start | bytes 983048 | tf_op jit(solution)/shard_map/ppermute | solution.py:32
  12.8 9.1 %collective-permute-start.3 = (bf16[2,10,16,512]{3,2,1,0:T(8,128)(2,1)S(1)}, bf16[2,10,16,512]{3,2,1,0:T(8,128)(2,1)S(1)}, u32[]{:S(2)}, u32[]{:S(2)}) collective-permute-start(bf16[2,10,16,512]{3,2,1,0:T(8,128)(2,1)S(1)} %pad_maximum_fusion.own), channel_id=1, source_target_pairs={{0,48},{1,13},{2,50},{3,15},{4,52},{5,1},{6,54},{7,3},{8,56},{9,5}... | collective-permute-start | bytes 983048 | tf_op jit(solution)/shard_map/ppermute | solution.py:32
  14.3 9.4 %collective-permute-start.4 = (bf16[2,10,16,512]{3,2,1,0:T(8,128)(2,1)S(1)}, bf16[2,10,16,512]{3,2,1,0:T(8,128)(2,1)S(1)}, u32[]{:S(2)}, u32[]{:S(2)}) collective-permute-start(bf16[2,10,16,512]{3,2,1,0:T(8,128)(2,1)S(1)} %pad_maximum_fusion.own), channel_id=1, source_target_pairs={{0,32},{1,9},{2,34},{3,11},{4,36},{5,13},{6,38},{7,15},{8,40},{9,1... | collective-permute-start | bytes 983048 | tf_op jit(solution)/shard_map/ppermute | solution.py:32
  17.3 11.7 %collective-permute-start.5 = (bf16[32,7808]{1,0:T(8,128)(2,1)S(1)}, bf16[32,7808]{1,0:T(8,128)(2,1)S(1)}, u32[]{:S(2)}, u32[]{:S(2)}) collective-permute-start(bf16[32,7808]{1,0:T(8,128)(2,1)S(1)} %get-tuple-element.40), channel_id=1, source_target_pairs={{0,2},{1,67},{2,64},{3,1},{4,6},{5,71},{6,68},{7,5},{8,10},{9,75},... | collective-permute-start | bytes 1499144 | tf_op jit(solution)/shard_map/ppermute | solution.py:32
  24.2 17.4 %collective-permute-start.13 = (bf16[31,5,16,128]{3,2,1,0:T(8,128)(2,1)S(1)}, bf16[31,5,16,128]{3,2,1,0:T(8,128)(2,1)S(1)}, u32[]{:S(2)}, u32[]{:S(2)}) collective-permute-start(bf16[31,5,16,128]{3,2,1,0:T(8,128)(2,1)S(1)} %get-tuple-element.26.own_b), channel_id=1, source_target_pairs={{0,12},{1,49},{2,14},{3,51},{4,0},{5,53},{6,2},{7,55},{8,4},{9,57}... | collective-permute-start | bytes 1904648 | tf_op jit(solution)/shard_map/ppermute | solution.py:32
  27.8 12.0 %collective-permute-start.10 = (bf16[30,5,16,128]{3,2,1,0:T(8,128)(2,1)S(1)}, bf16[30,5,16,128]{3,2,1,0:T(8,128)(2,1)S(1)}, u32[]{:S(2)}, u32[]{:S(2)}) collective-permute-start(bf16[30,5,16,128]{3,2,1,0:T(8,128)(2,1)S(1)} %get-tuple-element.25.own_a), channel_id=1, source_target_pairs={{0,4},{1,17},{2,6},{3,19},{4,8},{5,21},{6,10},{7,23},{8,12},{9,25}... | collective-permute-start | bytes 1843208 | tf_op jit(solution)/shard_map/ppermute | solution.py:32
  27.8 9.3 %collective-permute-start.6 = (bf16[32,7808]{1,0:T(8,128)(2,1)S(1)}, bf16[32,7808]{1,0:T(8,128)(2,1)S(1)}, u32[]{:S(2)}, u32[]{:S(2)}) collective-permute-start(bf16[32,7808]{1,0:T(8,128)(2,1)S(1)} %get-tuple-element.39), channel_id=1, source_target_pairs={{0,66},{1,3},{2,0},{3,65},{4,70},{5,7},{6,4},{7,69},{8,74},{9,11},... | collective-permute-start | bytes 1499144 | tf_op jit(solution)/shard_map/ppermute | solution.py:32
  29.0 16.0 %collective-permute-start.7 = (bf16[64,7808]{1,0:T(8,128)(2,1)S(1)}, bf16[64,7808]{1,0:T(8,128)(2,1)S(1)}, u32[]{:S(2)}, u32[]{:S(2)}) collective-permute-start(bf16[64,7808]{1,0:T(8,128)(2,1)S(1)} %coadd.1.mine), channel_id=1, source_target_pairs={{0,1},{1,0},{2,3},{3,2},{4,5},{5,4},{6,7},{7,6},{8,9},{9,8},{10,11... | collective-permute-start | bytes 2998280 | tf_op jit(solution)/shard_map/ppermute | solution.py:32
  31.9 16.4 %collective-permute-start.11 = (bf16[31,5,16,128]{3,2,1,0:T(8,128)(2,1)S(1)}, bf16[31,5,16,128]{3,2,1,0:T(8,128)(2,1)S(1)}, u32[]{:S(2)}, u32[]{:S(2)}) collective-permute-start(bf16[31,5,16,128]{3,2,1,0:T(8,128)(2,1)S(1)} %get-tuple-element.26.own_b), channel_id=1, source_target_pairs={{0,4},{1,17},{2,6},{3,19},{4,8},{5,21},{6,10},{7,23},{8,12},{9,25}... | collective-permute-start | bytes 1904648 | tf_op jit(solution)/shard_map/ppermute | solution.py:32
  37.0 11.3 %collective-permute-start.12 = (bf16[30,5,16,128]{3,2,1,0:T(8,128)(2,1)S(1)}, bf16[30,5,16,128]{3,2,1,0:T(8,128)(2,1)S(1)}, u32[]{:S(2)}, u32[]{:S(2)}) collective-permute-start(bf16[30,5,16,128]{3,2,1,0:T(8,128)(2,1)S(1)} %get-tuple-element.25.own_a), channel_id=1, source_target_pairs={{0,12},{1,49},{2,14},{3,51},{4,0},{5,53},{6,2},{7,55},{8,4},{9,57}... | collective-permute-start | bytes 1843208 | tf_op jit(solution)/shard_map/ppermute | solution.py:32
  39.7 3.4 %collective-permute-start.8 = (bf16[32,7808]{1,0:T(8,128)(2,1)S(1)}, bf16[32,7808]{1,0:T(8,128)(2,1)S(1)}, u32[]{:S(2)}, u32[]{:S(2)}) collective-permute-start(bf16[32,7808]{1,0:T(8,128)(2,1)S(1)} %collective-permute-done.5.direct_a), channel_id=1, source_target_pairs={{0,1},{1,0},{2,3},{3,2},{4,5},{5,4},{6,7},{7,6},{8,9},{9,8},{10,11... | collective-permute-start | bytes 1499144 | tf_op jit(solution)/shard_map/ppermute | solution.py:32
  41.6 3.1 %collective-permute-start.9 = (bf16[32,7808]{1,0:T(8,128)(2,1)S(1)}, bf16[32,7808]{1,0:T(8,128)(2,1)S(1)}, u32[]{:S(2)}, u32[]{:S(2)}) collective-permute-start(bf16[32,7808]{1,0:T(8,128)(2,1)S(1)} %collective-permute-done.6.direct_b), channel_id=1, source_target_pairs={{0,1},{1,0},{2,3},{3,2},{4,5},{5,4},{6,7},{7,6},{8,9},{9,8},{10,11... | collective-permute-start | bytes 1499144 | tf_op jit(solution)/shard_map/ppermute | solution.py:32
  43.1 12.1 %collective-permute-start.15 = (bf16[31,5,16,128]{3,2,1,0:T(8,128)(2,1)S(1)}, bf16[31,5,16,128]{3,2,1,0:T(8,128)(2,1)S(1)}, u32[]{:S(2)}, u32[]{:S(2)}) collective-permute-start(bf16[31,5,16,128]{3,2,1,0:T(8,128)(2,1)S(1)} %collective-permute-done.13.down_b), channel_id=1, source_target_pairs={{0,12},{1,49},{2,14},{3,51},{4,0},{5,53},{6,2},{7,55},{8,4},{9,57}... | collective-permute-start | bytes 1904648 | tf_op jit(solution)/shard_map/ppermute | solution.py:32
  44.7 10.5 %collective-permute-start.14 = (bf16[30,5,16,128]{3,2,1,0:T(8,128)(2,1)S(1)}, bf16[30,5,16,128]{3,2,1,0:T(8,128)(2,1)S(1)}, u32[]{:S(2)}, u32[]{:S(2)}) collective-permute-start(bf16[30,5,16,128]{3,2,1,0:T(8,128)(2,1)S(1)} %collective-permute-done.10.up_a), channel_id=1, source_target_pairs={{0,4},{1,17},{2,6},{3,19},{4,8},{5,21},{6,10},{7,23},{8,12},{9,25}... | collective-permute-start | bytes 1843208 | tf_op jit(solution)/shard_map/ppermute | solution.py:32
  55.2 7.2 %copy-start.3 = (s32[32]{0:T(128)S(1)}, s32[32]{0:T(128)}, u32[]{:S(2)}) copy-start(s32[32]{0:T(128)} %param.13) | copy-start | bytes 388
  55.2 9.4 %copy-start.2 = (s32[3]{0:T(128)S(1)}, s32[3]{0:T(128)}, u32[]{:S(2)}) copy-start(s32[3]{0:T(128)} %counts.1) | copy-start | bytes 40
  57.9 4.6 %collective-permute-start.16 = (f32[4,3,8,128]{3,2,1,0:T(8,128)S(1)}, f32[4,3,8,128]{3,2,1,0:T(8,128)S(1)}, u32[]{:S(2)}, u32[]{:S(2)}) collective-permute-start(f32[4,3,8,128]{3,2,1,0:T(8,128)S(1)} %get-tuple-element.33), channel_id=1, source_target_pairs={{0,1},{1,0},{2,3},{3,2},{4,5},{5,4},{6,7},{7,6},{8,9},{9,8},{10,11... | collective-permute-start | bytes 147464 | tf_op jit(solution)/shard_map/ppermute | solution.py:32
  58.9 4.9 %collective-permute-start.17 = (f32[4,3,8,128]{3,2,1,0:T(8,128)S(1)}, f32[4,3,8,128]{3,2,1,0:T(8,128)S(1)}, u32[]{:S(2)}, u32[]{:S(2)}) collective-permute-start(f32[4,3,8,128]{3,2,1,0:T(8,128)S(1)} %get-tuple-element.34), channel_id=1, source_target_pairs={{0,66},{1,3},{2,0},{3,65},{4,70},{5,7},{6,4},{7,69},{8,74},{9,11},... | collective-permute-start | bytes 147464 | tf_op jit(solution)/shard_map/ppermute | solution.py:32
  59.8 4.7 %collective-permute-start.18 = (f32[4,3,8,128]{3,2,1,0:T(8,128)S(1)}, f32[4,3,8,128]{3,2,1,0:T(8,128)S(1)}, u32[]{:S(2)}, u32[]{:S(2)}) collective-permute-start(f32[4,3,8,128]{3,2,1,0:T(8,128)S(1)} %get-tuple-element.35), channel_id=1, source_target_pairs={{0,3},{1,66},{2,65},{3,0},{4,7},{5,70},{6,69},{7,4},{8,11},{9,74},... | collective-permute-start | bytes 147464 | tf_op jit(solution)/shard_map/ppermute | solution.py:32

commit v5 on v4

--- a/solution.py
+++ b/solution.py
@@ -329,7 +329,7 @@
         name="coadd",
     )(place, owners, keep, incoming)
     direct = send(mine[:32], x=1), send(mine[32:], x=-1)
-    late, _ = lax.optimization_barrier((mine, direct[0]))
+    late, _ = lax.optimization_barrier((mine, direct))
     over = send(late, core=1)
     swapped = [send(v, core=1) for v in direct]
 

time: 67.1 us -> 65 us (0.969); the launches traced: 66.1 us -> 64.8 us
  starting transfers between devices: 32.4 us -> 26.7 us
  waiting for transfers between devices: 13.3 us -> 17.7 us
    ppermute x19, starting transfers between devices: 32.4 us -> 26.7 us  [send(): return lax.ppermute(value, AXES, [(d, moved(d, **how)) for d in range(128)])]
    ppermute x19, waiting for transfers between devices: 13.3 us -> 17.7 us  [send(): return lax.ppermute(value, AXES, [(d, moved(d, **how)) for d in range(128)])]
  transfers between devices with their start and end apart: 19 -> 19, of which waited for: 8 -> 10; matrix products, arithmetic and copies ran while one was open for 0% -> 0% of each run, Pallas kernels for 20% -> 21%
where the time goes in v5:
time: 65 us; the launch traced here: 64.8 us
  starting transfers between devices  26.7 us (41%)
  Pallas kernels  18.4 us (28%)
  waiting for transfers between devices  17.7 us (27%)
  local copies, waits for them, and re-layouts  1.22 us (2%)
  between operations  0.76 us (1%)
    ppermute x19, starting transfers between devices, send(): return lax.ppermute(value, AXES, [(d, moved(d, **how)) for d in range(128)])  26.7 us
    ppermute x19, waiting for transfers between devices, send(): return lax.ppermute(value, AXES, [(d, moved(d, **how)) for d in range(128)])  17.7 us
    pallas_call x3, Pallas kernels, fit(): pl.pallas_call(kernel, out_shape=shapes, in_specs=[smem if v is place els...  11.3 us
    pallas_call x1, Pallas kernels, body(): pl.pallas_call(weight_kernel, out_shape=(jax.ShapeDtypeStruct((count, pix...  3.08 us
    pallas_call x1, Pallas kernels, body(): pl.pallas_call(final_kernel, out_shape=(jax.ShapeDtypeStruct((TERMS, 32,...  1.61 us
  transfers between devices with their start and end apart: 19, of which 10 were waited for; matrix products, arithmetic and copies ran while one was open for 0% of the time, Pallas kernels for 21%

profile of v5, /device:TPU:1, one launch (start us, length us, event | category | flops | bytes accessed | tf_op | source)
XLA Modules:
  0.0 64.8 jit_solution(13669850172328139970)
XLA Ops:
  0.7 0.1 stack.23.place
  0.8 1.0 %copy-done = bf16[2,10,7808]{2,0,1:T(2,128)(2,1)S(1)} copy-done((bf16[2,10,7808]{2,0,1:T(2,128)(2,1)S(1)}, bf16[2,10,7808]{2,0,1:T(2,128)(2,1)}, u32[]{:S(2)}) %copy-start) | copy-done | bytes 312344
  1.7 0.7 %prep.1 = bf16[1,10,16,512]{3,2,1,0:T(8,128)(2,1)S(1)} custom-call(s32[5]{0:T(128)S(1)} %stack.23.place, bf16[10,2,7808]{2,1,0:T(2,128)(2,1)S(1)} %bitcast.9), custom_call_target="tpu_custom_call" | custom-call | flops 700000000 | bytes 2100000 | tf_op jit(solution)/shard_map/prep/pallas_call | solution.py:290
  2.4 3.7 %collective-permute-start = (bf16[1,10,16,512]{3,2,1,0:T(8,128)(2,1)S(1)}, bf16[1,10,16,512]{3,2,1,0:T(8,128)(2,1)S(1)}, u32[]{:S(2)}, u32[]{:S(2)}) collective-permute-start(bf16[1,10,16,512]{3,2,1,0:T(8,128)(2,1)S(1)} %prep.1), channel_id=1, source_target_pairs={{0,64},{1,65},{2,66},{3,67},{4,68},{5,69},{6,70},{7,71},{8,72},{9,... | collective-permute-start | bytes 491528 | tf_op jit(solution)/shard_map/ppermute | solution.py:32
  6.0 3.1 %weight.1 = (bf16[96,7808]{1,0:T(8,128)(2,1)S(1)}, bf16[112,7808]{1,0:T(8,128)(2,1)S(1)}) custom-call(s32[5]{0:T(128)S(1)} %stack.23.place, bf16[96,7808]{1,0:T(8,128)(2,1)} %flux.1, bf16[96,7808]{1,0:T(8,128)(2,1)} %ivar.1, s32[61,96]{1,0:T(8,128)} %bitcast.12, s32[1,96]{1,0:T(1,128)} %bitcast.10), custom_call_target="tpu_custom_call" | custom-call | flops 2300000000 | bytes 6899999 | tf_op jit(solution)/shard_map/weight/pallas_call | solution.py:306
  9.1 0.4 collective-permute-done
  9.5 1.7 %collective-permute-start.1 = (bf16[112,7808]{1,0:T(8,128)(2,1)S(1)}, bf16[112,7808]{1,0:T(8,128)(2,1)S(1)}, u32[]{:S(2)}, u32[]{:S(2)}) collective-permute-start(bf16[112,7808]{1,0:T(8,128)(2,1)S(1)} %get-tuple-element.23), channel_id=1, source_target_pairs={{0,1},{1,0},{2,3},{3,2},{4,5},{5,4},{6,7},{7,6},{8,9},{9,8},{10,11... | collective-permute-start | bytes 5246984 | tf_op jit(solution)/shard_map/ppermute | solution.py:32
  11.2 1.6 %collective-permute-start.2 = (bf16[2,10,16,512]{3,2,1,0:T(8,128)(2,1)S(1)}, bf16[2,10,16,512]{3,2,1,0:T(8,128)(2,1)S(1)}, u32[]{:S(2)}, u32[]{:S(2)}) collective-permute-start(bf16[2,10,16,512]{3,2,1,0:T(8,128)(2,1)S(1)} %pad_maximum_fusion.own), channel_id=1, source_target_pairs={{0,16},{1,5},{2,18},{3,7},{4,20},{5,9},{6,22},{7,11},{8,24},{9,13}... | collective-permute-start | bytes 983048 | tf_op jit(solution)/shard_map/ppermute | solution.py:32
  12.8 1.5 %collective-permute-start.3 = (bf16[2,10,16,512]{3,2,1,0:T(8,128)(2,1)S(1)}, bf16[2,10,16,512]{3,2,1,0:T(8,128)(2,1)S(1)}, u32[]{:S(2)}, u32[]{:S(2)}) collective-permute-start(bf16[2,10,16,512]{3,2,1,0:T(8,128)(2,1)S(1)} %pad_maximum_fusion.own), channel_id=1, source_target_pairs={{0,48},{1,13},{2,50},{3,15},{4,52},{5,1},{6,54},{7,3},{8,56},{9,5}... | collective-permute-start | bytes 983048 | tf_op jit(solution)/shard_map/ppermute | solution.py:32
  14.3 1.6 %collective-permute-start.4 = (bf16[2,10,16,512]{3,2,1,0:T(8,128)(2,1)S(1)}, bf16[2,10,16,512]{3,2,1,0:T(8,128)(2,1)S(1)}, u32[]{:S(2)}, u32[]{:S(2)}) collective-permute-start(bf16[2,10,16,512]{3,2,1,0:T(8,128)(2,1)S(1)} %pad_maximum_fusion.own), channel_id=1, source_target_pairs={{0,32},{1,9},{2,34},{3,11},{4,36},{5,13},{6,38},{7,15},{8,40},{9,1... | collective-permute-start | bytes 983048 | tf_op jit(solution)/shard_map/ppermute | solution.py:32
  15.9 0.0 collective-permute-done.1.other
  15.9 1.3 %coadd.1.mine = bf16[64,7808]{1,0:T(8,128)(2,1)S(1)} custom-call(s32[5]{0:T(128)S(1)} %stack.23.place, s32[1,96]{1,0:T(1,128)S(1)} %bitcast.11, bf16[96,7808]{1,0:T(8,128)(2,1)S(1)} %get-tuple-element.21.own, bf16[112,7808]{1,0:T(8,128)(2,1)S(1)} %collective-permute-done.1.other), custom_call_target="tpu_custom_call" | custom-call | flops 2400000000 | bytes 7200000 | tf_op jit(solution)/shard_map/coadd/pallas_call | solution.py:322
  17.2 0.1 fusion
  17.3 2.5 %collective-permute-start.5 = (bf16[32,7808]{1,0:T(8,128)(2,1)S(1)}, bf16[32,7808]{1,0:T(8,128)(2,1)S(1)}, u32[]{:S(2)}, u32[]{:S(2)}) collective-permute-start(bf16[32,7808]{1,0:T(8,128)(2,1)S(1)} %get-tuple-element.40), channel_id=1, source_target_pairs={{0,2},{1,67},{2,64},{3,1},{4,6},{5,71},{6,68},{7,5},{8,10},{9,75},... | collective-permute-start | bytes 1499144 | tf_op jit(solution)/shard_map/ppermute | solution.py:32
  19.8 0.0 collective-permute-start.6
  19.8 0.0 collective-permute-done.2.up
  19.8 2.0 %collective-permute-done.3.down = bf16[2,10,16,512]{3,2,1,0:T(8,128)(2,1)S(1)} collective-permute-done((bf16[2,10,16,512]{3,2,1,0:T(8,128)(2,1)S(1)}, bf16[2,10,16,512]{3,2,1,0:T(8,128)(2,1)S(1)}, u32[]{:S(2)}, u32[]{:S(2)}) %collective-permute-start.3) | collective-permute-done | bytes 327712 | tf_op jit(solution)/shard_map/ppermute | solution.py:32
  21.9 1.8 %collective-permute-done.4.far = bf16[2,10,16,512]{3,2,1,0:T(8,128)(2,1)S(1)} collective-permute-done((bf16[2,10,16,512]{3,2,1,0:T(8,128)(2,1)S(1)}, bf16[2,10,16,512]{3,2,1,0:T(8,128)(2,1)S(1)}, u32[]{:S(2)}, u32[]{:S(2)}) %collective-permute-start.4) | collective-permute-done | bytes 327712 | tf_op jit(solution)/shard_map/ppermute | solution.py:32
  23.7 0.5 join.1
  24.2 3.5 %collective-permute-start.13 = (bf16[31,5,16,128]{3,2,1,0:T(8,128)(2,1)S(1)}, bf16[31,5,16,128]{3,2,1,0:T(8,128)(2,1)S(1)}, u32[]{:S(2)}, u32[]{:S(2)}) collective-permute-start(bf16[31,5,16,128]{3,2,1,0:T(8,128)(2,1)S(1)} %get-tuple-element.26.own_b), channel_id=1, source_target_pairs={{0,12},{1,49},{2,14},{3,51},{4,0},{5,53},{6,2},{7,55},{8,4},{9,57}... | collective-permute-start | bytes 1904648 | tf_op jit(solution)/shard_map/ppermute | solution.py:32
  27.8 0.0 collective-permute-start.10
  27.8 0.8 %collective-permute-done.5.direct_a = bf16[32,7808]{1,0:T(8,128)(2,1)S(1)} collective-permute-done((bf16[32,7808]{1,0:T(8,128)(2,1)S(1)}, bf16[32,7808]{1,0:T(8,128)(2,1)S(1)}, u32[]{:S(2)}, u32[]{:S(2)}) %collective-permute-start.5) | collective-permute-done | bytes 499744 | tf_op jit(solution)/shard_map/ppermute | solution.py:32
  28.5 5.4 %collective-permute-done.6.direct_b = bf16[32,7808]{1,0:T(8,128)(2,1)S(1)} collective-permute-done((bf16[32,7808]{1,0:T(8,128)(2,1)S(1)}, bf16[32,7808]{1,0:T(8,128)(2,1)S(1)}, u32[]{:S(2)}, u32[]{:S(2)}) %collective-permute-start.6) | collective-permute-done | bytes 499744 | tf_op jit(solution)/shard_map/ppermute | solution.py:32
  34.0 0.0 collective-permute-start.7
  34.0 0.4 collective-permute-start.11
  34.4 2.2 %collective-permute-start.12 = (bf16[30,5,16,128]{3,2,1,0:T(8,128)(2,1)S(1)}, bf16[30,5,16,128]{3,2,1,0:T(8,128)(2,1)S(1)}, u32[]{:S(2)}, u32[]{:S(2)}) collective-permute-start(bf16[30,5,16,128]{3,2,1,0:T(8,128)(2,1)S(1)} %get-tuple-element.25.own_a), channel_id=1, source_target_pairs={{0,12},{1,49},{2,14},{3,51},{4,0},{5,53},{6,2},{7,55},{8,4},{9,57}... | collective-permute-start | bytes 1843208 | tf_op jit(solution)/shard_map/ppermute | solution.py:32
  36.6 1.6 %collective-permute-done.10.up_a = bf16[30,5,16,128]{3,2,1,0:T(8,128)(2,1)S(1)} collective-permute-done((bf16[30,5,16,128]{3,2,1,0:T(8,128)(2,1)S(1)}, bf16[30,5,16,128]{3,2,1,0:T(8,128)(2,1)S(1)}, u32[]{:S(2)}, u32[]{:S(2)}) %collective-permute-start.10) | collective-permute-done | bytes 614432 | tf_op jit(solution)/shard_map/ppermute | solution.py:32
  38.3 2.3 %collective-permute-start.8 = (bf16[32,7808]{1,0:T(8,128)(2,1)S(1)}, bf16[32,7808]{1,0:T(8,128)(2,1)S(1)}, u32[]{:S(2)}, u32[]{:S(2)}) collective-permute-start(bf16[32,7808]{1,0:T(8,128)(2,1)S(1)} %collective-permute-done.5.direct_a), channel_id=1, source_target_pairs={{0,1},{1,0},{2,3},{3,2},{4,5},{5,4},{6,7},{7,6},{8,9},{9,8},{10,11... | collective-permute-start | bytes 1499144 | tf_op jit(solution)/shard_map/ppermute | solution.py:32
  40.5 0.0 collective-permute-done.13.down_b
  40.5 0.0 collective-permute-start.9
  40.6 1.5 %collective-permute-done.8.swapped_a = bf16[32,7808]{1,0:T(8,128)(2,1)S(1)} collective-permute-done((bf16[32,7808]{1,0:T(8,128)(2,1)S(1)}, bf16[32,7808]{1,0:T(8,128)(2,1)S(1)}, u32[]{:S(2)}, u32[]{:S(2)}) %collective-permute-start.8) | collective-permute-done | bytes 499744 | tf_op jit(solution)/shard_map/ppermute | solution.py:32
  42.0 1.6 %collective-permute-start.15 = (bf16[31,5,16,128]{3,2,1,0:T(8,128)(2,1)S(1)}, bf16[31,5,16,128]{3,2,1,0:T(8,128)(2,1)S(1)}, u32[]{:S(2)}, u32[]{:S(2)}) collective-permute-start(bf16[31,5,16,128]{3,2,1,0:T(8,128)(2,1)S(1)} %collective-permute-done.13.down_b), channel_id=1, source_target_pairs={{0,12},{1,49},{2,14},{3,51},{4,0},{5,53},{6,2},{7,55},{8,4},{9,57}... | collective-permute-start | bytes 1904648 | tf_op jit(solution)/shard_map/ppermute | solution.py:32
  43.6 0.0 collective-permute-done.9.swapped_b
  43.6 0.3 collective-permute-start.14
  43.9 0.0 collective-permute-done.7.over
  43.9 3.4 %own_fit.1 = (f32[4,1,3,8,128]{4,3,2,1,0:T(8,128)S(1)}, bf16[7808,128]{1,0:T(8,128)(2,1)S(1)}, bf16[7808,128]{1,0:T(8,128)(2,1)S(1)}) custom-call(s32[5]{0:T(128)S(1)} %stack.23.place, bf16[30,5,16,128]{3,2,1,0:T(8,128)(2,1)S(1)} %get-tuple-element.25.own_a, bf16[31,5,16,128]{3,2,1,0:T(8,128)(2,1)S(1)} %get-tuple-element.26.own_b, ...), custom_call_target="tpu_custom_call" | custom-call | tf_op jit(solution)/shard_map/own_fit/pallas_call | solution.py:354
  47.3 0.0 collective-permute-done.11.up_b
  47.3 5.2 %near_fit.1.near = f32[4,2,3,8,128]{4,3,2,1,0:T(8,128)S(1)} custom-call(bf16[30,5,16,128]{3,2,1,0:T(8,128)(2,1)S(1)} %collective-permute-done.10.up_a, bf16[31,5,16,128]{3,2,1,0:T(8,128)(2,1)S(1)} %collective-permute-done.11.up_b, bf16[30,5,16,128]{3,2,1,0:T(8,128)(2,1)S(1)} %collective-permute-done.12.down_a, ...), custom_call_target="tpu_custom_call" | custom-call | flops 6000000000 | bytes 18000000 | tf_op jit(solution)/shard_map/near_fit/pallas_call | solution.py:354
  52.5 1.6 %collective-permute-done.14.far_a = bf16[30,5,16,128]{3,2,1,0:T(8,128)(2,1)S(1)} collective-permute-done((bf16[30,5,16,128]{3,2,1,0:T(8,128)(2,1)S(1)}, bf16[30,5,16,128]{3,2,1,0:T(8,128)(2,1)S(1)}, u32[]{:S(2)}, u32[]{:S(2)}) %collective-permute-start.14) | collective-permute-done | bytes 614432 | tf_op jit(solution)/shard_map/ppermute | solution.py:32
  54.1 0.0 collective-permute-done.15.far_b
  54.1 2.7 %far_fit.1 = (f32[4,3,8,128]{3,2,1,0:T(8,128)S(1)}, f32[4,3,8,128]{3,2,1,0:T(8,128)S(1)}, f32[4,3,8,128]{3,2,1,0:T(8,128)S(1)}, f32[4,3,8,128]{3,2,1,0:T(8,128)S(1)}) custom-call(f32[4,1,3,8,128]{4,3,2,1,0:T(8,128)S(1)} %get-tuple-element.29.own, f32[4,2,3,8,128]{4,3,2,1,0:T(8,128)S(1)} %near_fit.1.near, ...), custom_call_target="tpu_custom_call" | custom-call | flops 3000000000 | bytes 9000000 | tf_op jit(solution)/shard_map/far_fit/pallas_call | solution.py:354
  56.8 0.5 collective-permute-start.16
  57.3 1.2 %collective-permute-start.17 = (f32[4,3,8,128]{3,2,1,0:T(8,128)S(1)}, f32[4,3,8,128]{3,2,1,0:T(8,128)S(1)}, u32[]{:S(2)}, u32[]{:S(2)}) collective-permute-start(f32[4,3,8,128]{3,2,1,0:T(8,128)S(1)} %get-tuple-element.34), channel_id=1, source_target_pairs={{0,66},{1,3},{2,0},{3,65},{4,70},{5,7},{6,4},{7,69},{8,74},{9,11},... | collective-permute-start | bytes 147464 | tf_op jit(solution)/shard_map/ppermute | solution.py:32
  58.5 2.1 %collective-permute-start.18 = (f32[4,3,8,128]{3,2,1,0:T(8,128)S(1)}, f32[4,3,8,128]{3,2,1,0:T(8,128)S(1)}, u32[]{:S(2)}, u32[]{:S(2)}) collective-permute-start(f32[4,3,8,128]{3,2,1,0:T(8,128)S(1)} %get-tuple-element.35), channel_id=1, source_target_pairs={{0,3},{1,66},{2,65},{3,0},{4,7},{5,70},{6,69},{7,4},{8,11},{9,74},... | collective-permute-start | bytes 147464 | tf_op jit(solution)/shard_map/ppermute | solution.py:32
  60.6 0.1 reshape_tile.3.classes
  60.7 0.7 %collective-permute-done.17.part_2 = f32[4,3,8,128]{3,2,1,0:T(8,128)S(1)} collective-permute-done((f32[4,3,8,128]{3,2,1,0:T(8,128)S(1)}, f32[4,3,8,128]{3,2,1,0:T(8,128)S(1)}, u32[]{:S(2)}, u32[]{:S(2)}) %collective-permute-start.17) | collective-permute-done | bytes 49184 | tf_op jit(solution)/shard_map/ppermute | solution.py:32
  61.4 1.8 %collective-permute-done.18.part_3 = f32[4,3,8,128]{3,2,1,0:T(8,128)S(1)} collective-permute-done((f32[4,3,8,128]{3,2,1,0:T(8,128)S(1)}, f32[4,3,8,128]{3,2,1,0:T(8,128)S(1)}, u32[]{:S(2)}, u32[]{:S(2)}) %collective-permute-start.18) | collective-permute-done | bytes 49184 | tf_op jit(solution)/shard_map/ppermute | solution.py:32
  63.2 1.6 %final.1 = (f32[10,32,128]{2,1,0:T(8,128)}, f32[32,128]{1,0:T(8,128)}, f32[1,32]{1,0:T(1,128)}) custom-call(s32[5]{0:T(128)S(1)} %stack.23.place, s32[3]{0:T(128)S(1)} %copy-done.2, s32[1,128]{1,0:T(1,128)S(1)} %reshape_tile.3.classes, f32[4,3,8,128]{3,2,1,0:T(8,128)S(1)} %get-tuple-element.32.part_0, f32[4,3,8,128]{3,2,1,0:T(8,128)S(1)} %collective-permute-done.16.part_1, ...), custom_call_target="tpu_custom_call" | custom-call | flops 2000000000 | bytes 6000000 | tf_op jit(solution)/shard_map/final/pallas_call | solution.py:382
  (11 shorter events, 0.1 us)
Async XLA Ops:
  0.8 1.0 %copy-start = (bf16[2,10,7808]{2,0,1:T(2,128)(2,1)S(1)}, bf16[2,10,7808]{2,0,1:T(2,128)(2,1)}, u32[]{:S(2)}) copy-start(bf16[2,10,7808]{2,0,1:T(2,128)(2,1)} %param.11) | copy-start | bytes 936964
  2.4 7.1 %collective-permute-start = (bf16[1,10,16,512]{3,2,1,0:T(8,128)(2,1)S(1)}, bf16[1,10,16,512]{3,2,1,0:T(8,128)(2,1)S(1)}, u32[]{:S(2)}, u32[]{:S(2)}) collective-permute-start(bf16[1,10,16,512]{3,2,1,0:T(8,128)(2,1)S(1)} %prep.1), channel_id=1, source_target_pairs={{0,64},{1,65},{2,66},{3,67},{4,68},{5,69},{6,70},{7,71},{8,72},{9,... | collective-permute-start | bytes 491528 | tf_op jit(solution)/shard_map/ppermute | solution.py:32
  6.0 9.9 %copy-start.1 = (s32[96]{0:T(128)S(1)}, s32[96]{0:T(128)}, u32[]{:S(2)}) copy-start(s32[96]{0:T(128)} %param.10) | copy-start | bytes 1156
  9.5 6.4 %collective-permute-start.1 = (bf16[112,7808]{1,0:T(8,128)(2,1)S(1)}, bf16[112,7808]{1,0:T(8,128)(2,1)S(1)}, u32[]{:S(2)}, u32[]{:S(2)}) collective-permute-start(bf16[112,7808]{1,0:T(8,128)(2,1)S(1)} %get-tuple-element.23), channel_id=1, source_target_pairs={{0,1},{1,0},{2,3},{3,2},{4,5},{5,4},{6,7},{7,6},{8,9},{9,8},{10,11... | collective-permute-start | bytes 5246984 | tf_op jit(solution)/shard_map/ppermute | solution.py:32
  11.2 8.6 %collective-permute-start.2 = (bf16[2,10,16,512]{3,2,1,0:T(8,128)(2,1)S(1)}, bf16[2,10,16,512]{3,2,1,0:T(8,128)(2,1)S(1)}, u32[]{:S(2)}, u32[]{:S(2)}) collective-permute-start(bf16[2,10,16,512]{3,2,1,0:T(8,128)(2,1)S(1)} %pad_maximum_fusion.own), channel_id=1, source_target_pairs={{0,16},{1,5},{2,18},{3,7},{4,20},{5,9},{6,22},{7,11},{8,24},{9,13}... | collective-permute-start | bytes 983048 | tf_op jit(solution)/shard_map/ppermute | solution.py:32
  12.8 9.1 %collective-permute-start.3 = (bf16[2,10,16,512]{3,2,1,0:T(8,128)(2,1)S(1)}, bf16[2,10,16,512]{3,2,1,0:T(8,128)(2,1)S(1)}, u32[]{:S(2)}, u32[]{:S(2)}) collective-permute-start(bf16[2,10,16,512]{3,2,1,0:T(8,128)(2,1)S(1)} %pad_maximum_fusion.own), channel_id=1, source_target_pairs={{0,48},{1,13},{2,50},{3,15},{4,52},{5,1},{6,54},{7,3},{8,56},{9,5}... | collective-permute-start | bytes 983048 | tf_op jit(solution)/shard_map/ppermute | solution.py:32
  14.3 9.4 %collective-permute-start.4 = (bf16[2,10,16,512]{3,2,1,0:T(8,128)(2,1)S(1)}, bf16[2,10,16,512]{3,2,1,0:T(8,128)(2,1)S(1)}, u32[]{:S(2)}, u32[]{:S(2)}) collective-permute-start(bf16[2,10,16,512]{3,2,1,0:T(8,128)(2,1)S(1)} %pad_maximum_fusion.own), channel_id=1, source_target_pairs={{0,32},{1,9},{2,34},{3,11},{4,36},{5,13},{6,38},{7,15},{8,40},{9,1... | collective-permute-start | bytes 983048 | tf_op jit(solution)/shard_map/ppermute | solution.py:32
  17.3 11.2 %collective-permute-start.5 = (bf16[32,7808]{1,0:T(8,128)(2,1)S(1)}, bf16[32,7808]{1,0:T(8,128)(2,1)S(1)}, u32[]{:S(2)}, u32[]{:S(2)}) collective-permute-start(bf16[32,7808]{1,0:T(8,128)(2,1)S(1)} %get-tuple-element.40), channel_id=1, source_target_pairs={{0,2},{1,67},{2,64},{3,1},{4,6},{5,71},{6,68},{7,5},{8,10},{9,75},... | collective-permute-start | bytes 1499144 | tf_op jit(solution)/shard_map/ppermute | solution.py:32
  19.8 14.1 %collective-permute-start.6 = (bf16[32,7808]{1,0:T(8,128)(2,1)S(1)}, bf16[32,7808]{1,0:T(8,128)(2,1)S(1)}, u32[]{:S(2)}, u32[]{:S(2)}) collective-permute-start(bf16[32,7808]{1,0:T(8,128)(2,1)S(1)} %get-tuple-element.39), channel_id=1, source_target_pairs={{0,66},{1,3},{2,0},{3,65},{4,70},{5,7},{6,4},{7,69},{8,74},{9,11},... | collective-permute-start | bytes 1499144 | tf_op jit(solution)/shard_map/ppermute | solution.py:32
  24.2 16.3 %collective-permute-start.13 = (bf16[31,5,16,128]{3,2,1,0:T(8,128)(2,1)S(1)}, bf16[31,5,16,128]{3,2,1,0:T(8,128)(2,1)S(1)}, u32[]{:S(2)}, u32[]{:S(2)}) collective-permute-start(bf16[31,5,16,128]{3,2,1,0:T(8,128)(2,1)S(1)} %get-tuple-element.26.own_b), channel_id=1, source_target_pairs={{0,12},{1,49},{2,14},{3,51},{4,0},{5,53},{6,2},{7,55},{8,4},{9,57}... | collective-permute-start | bytes 1904648 | tf_op jit(solution)/shard_map/ppermute | solution.py:32
  27.8 10.5 %collective-permute-start.10 = (bf16[30,5,16,128]{3,2,1,0:T(8,128)(2,1)S(1)}, bf16[30,5,16,128]{3,2,1,0:T(8,128)(2,1)S(1)}, u32[]{:S(2)}, u32[]{:S(2)}) collective-permute-start(bf16[30,5,16,128]{3,2,1,0:T(8,128)(2,1)S(1)} %get-tuple-element.25.own_a), channel_id=1, source_target_pairs={{0,4},{1,17},{2,6},{3,19},{4,8},{5,21},{6,10},{7,23},{8,12},{9,25}... | collective-permute-start | bytes 1843208 | tf_op jit(solution)/shard_map/ppermute | solution.py:32
  34.0 10.0 %collective-permute-start.7 = (bf16[64,7808]{1,0:T(8,128)(2,1)S(1)}, bf16[64,7808]{1,0:T(8,128)(2,1)S(1)}, u32[]{:S(2)}, u32[]{:S(2)}) collective-permute-start(bf16[64,7808]{1,0:T(8,128)(2,1)S(1)} %coadd.1.mine), channel_id=1, source_target_pairs={{0,1},{1,0},{2,3},{3,2},{4,5},{5,4},{6,7},{7,6},{8,9},{9,8},{10,11... | collective-permute-start | bytes 2998280 | tf_op jit(solution)/shard_map/ppermute | solution.py:32
  34.0 13.3 %collective-permute-start.11 = (bf16[31,5,16,128]{3,2,1,0:T(8,128)(2,1)S(1)}, bf16[31,5,16,128]{3,2,1,0:T(8,128)(2,1)S(1)}, u32[]{:S(2)}, u32[]{:S(2)}) collective-permute-start(bf16[31,5,16,128]{3,2,1,0:T(8,128)(2,1)S(1)} %get-tuple-element.26.own_b), channel_id=1, source_target_pairs={{0,4},{1,17},{2,6},{3,19},{4,8},{5,21},{6,10},{7,23},{8,12},{9,25}... | collective-permute-start | bytes 1904648 | tf_op jit(solution)/shard_map/ppermute | solution.py:32
  34.4 12.9 %collective-permute-start.12 = (bf16[30,5,16,128]{3,2,1,0:T(8,128)(2,1)S(1)}, bf16[30,5,16,128]{3,2,1,0:T(8,128)(2,1)S(1)}, u32[]{:S(2)}, u32[]{:S(2)}) collective-permute-start(bf16[30,5,16,128]{3,2,1,0:T(8,128)(2,1)S(1)} %get-tuple-element.25.own_a), channel_id=1, source_target_pairs={{0,12},{1,49},{2,14},{3,51},{4,0},{5,53},{6,2},{7,55},{8,4},{9,57}... | collective-permute-start | bytes 1843208 | tf_op jit(solution)/shard_map/ppermute | solution.py:32
  38.3 3.8 %collective-permute-start.8 = (bf16[32,7808]{1,0:T(8,128)(2,1)S(1)}, bf16[32,7808]{1,0:T(8,128)(2,1)S(1)}, u32[]{:S(2)}, u32[]{:S(2)}) collective-permute-start(bf16[32,7808]{1,0:T(8,128)(2,1)S(1)} %collective-permute-done.5.direct_a), channel_id=1, source_target_pairs={{0,1},{1,0},{2,3},{3,2},{4,5},{5,4},{6,7},{7,6},{8,9},{9,8},{10,11... | collective-permute-start | bytes 1499144 | tf_op jit(solution)/shard_map/ppermute | solution.py:32
  40.5 3.1 %collective-permute-start.9 = (bf16[32,7808]{1,0:T(8,128)(2,1)S(1)}, bf16[32,7808]{1,0:T(8,128)(2,1)S(1)}, u32[]{:S(2)}, u32[]{:S(2)}) collective-permute-start(bf16[32,7808]{1,0:T(8,128)(2,1)S(1)} %collective-permute-done.6.direct_b), channel_id=1, source_target_pairs={{0,1},{1,0},{2,3},{3,2},{4,5},{5,4},{6,7},{7,6},{8,9},{9,8},{10,11... | collective-permute-start | bytes 1499144 | tf_op jit(solution)/shard_map/ppermute | solution.py:32
  42.0 12.1 %collective-permute-start.15 = (bf16[31,5,16,128]{3,2,1,0:T(8,128)(2,1)S(1)}, bf16[31,5,16,128]{3,2,1,0:T(8,128)(2,1)S(1)}, u32[]{:S(2)}, u32[]{:S(2)}) collective-permute-start(bf16[31,5,16,128]{3,2,1,0:T(8,128)(2,1)S(1)} %collective-permute-done.13.down_b), channel_id=1, source_target_pairs={{0,12},{1,49},{2,14},{3,51},{4,0},{5,53},{6,2},{7,55},{8,4},{9,57}... | collective-permute-start | bytes 1904648 | tf_op jit(solution)/shard_map/ppermute | solution.py:32
  43.6 10.5 %collective-permute-start.14 = (bf16[30,5,16,128]{3,2,1,0:T(8,128)(2,1)S(1)}, bf16[30,5,16,128]{3,2,1,0:T(8,128)(2,1)S(1)}, u32[]{:S(2)}, u32[]{:S(2)}) collective-permute-start(bf16[30,5,16,128]{3,2,1,0:T(8,128)(2,1)S(1)} %collective-permute-done.10.up_a), channel_id=1, source_target_pairs={{0,4},{1,17},{2,6},{3,19},{4,8},{5,21},{6,10},{7,23},{8,12},{9,25}... | collective-permute-start | bytes 1843208 | tf_op jit(solution)/shard_map/ppermute | solution.py:32
  54.1 6.5 %copy-start.3 = (s32[32]{0:T(128)S(1)}, s32[32]{0:T(128)}, u32[]{:S(2)}) copy-start(s32[32]{0:T(128)} %param.13) | copy-start | bytes 388
  54.1 9.1 %copy-start.2 = (s32[3]{0:T(128)S(1)}, s32[3]{0:T(128)}, u32[]{:S(2)}) copy-start(s32[3]{0:T(128)} %counts.1) | copy-start | bytes 40
  56.8 3.9 %collective-permute-start.16 = (f32[4,3,8,128]{3,2,1,0:T(8,128)S(1)}, f32[4,3,8,128]{3,2,1,0:T(8,128)S(1)}, u32[]{:S(2)}, u32[]{:S(2)}) collective-permute-start(f32[4,3,8,128]{3,2,1,0:T(8,128)S(1)} %get-tuple-element.33), channel_id=1, source_target_pairs={{0,1},{1,0},{2,3},{3,2},{4,5},{5,4},{6,7},{7,6},{8,9},{9,8},{10,11... | collective-permute-start | bytes 147464 | tf_op jit(solution)/shard_map/ppermute | solution.py:32
  57.3 4.2 %collective-permute-start.17 = (f32[4,3,8,128]{3,2,1,0:T(8,128)S(1)}, f32[4,3,8,128]{3,2,1,0:T(8,128)S(1)}, u32[]{:S(2)}, u32[]{:S(2)}) collective-permute-start(f32[4,3,8,128]{3,2,1,0:T(8,128)S(1)} %get-tuple-element.34), channel_id=1, source_target_pairs={{0,66},{1,3},{2,0},{3,65},{4,70},{5,7},{6,4},{7,69},{8,74},{9,11},... | collective-permute-start | bytes 147464 | tf_op jit(solution)/shard_map/ppermute | solution.py:32
  58.5 4.7 %collective-permute-start.18 = (f32[4,3,8,128]{3,2,1,0:T(8,128)S(1)}, f32[4,3,8,128]{3,2,1,0:T(8,128)S(1)}, u32[]{:S(2)}, u32[]{:S(2)}) collective-permute-start(f32[4,3,8,128]{3,2,1,0:T(8,128)S(1)} %get-tuple-element.35), channel_id=1, source_target_pairs={{0,3},{1,66},{2,65},{3,0},{4,7},{5,70},{6,69},{7,4},{8,11},{9,74},... | collective-permute-start | bytes 147464 | tf_op jit(solution)/shard_map/ppermute | solution.py:32

commit v6 on v5

--- a/solution.py
+++ b/solution.py
@@ -231,7 +231,7 @@
             outs[group][3:4, q] = packed[group][q]
 
 
-def final_kernel(place, counts, classes, part_0, part_1, part_2, part_3, coefs, gains, best):
+def trial_order(place, counts, classes, to_lane, drop):
     core, lo, hi, z, y = (place[i] for i in range(5))
 
     def shift(n):
@@ -248,24 +248,27 @@
 
     trial = trial_of(lax.broadcasted_iota(jnp.int32, (128, 128), 0))
     lane = lax.broadcasted_iota(jnp.int32, (128, 128), 1)
-    to_lane = (trial == lane).astype(jnp.float32).astype(jnp.bfloat16)
+    to_lane[...] = (trial == lane).astype(jnp.float32).astype(jnp.bfloat16)
     end_0 = counts[0]
     end_1 = end_0 + counts[1]
     end_2 = end_1 + counts[2]
     trial_class = sum((trial >= end).astype(jnp.int32) for end in (end_0, end_1, end_2))
+    drop[...] = ((lane // 32 == 2) & (trial_class != classes[...])).astype(jnp.float32)
+
+
+def final_kernel(to_lane, drop, part_0, part_1, part_2, part_3, coefs, gains, best):
     stack = []
     for q in range(3):
         rows = jnp.concatenate([p[:, q].reshape(32, 128) for p in (part_0, part_1, part_2, part_3)], axis=0)
         if q == 2:
-            drop = (lane // 32 == 2) & (trial_class != classes[...])
-            rows = jnp.where(drop, 0.0, rows)
+            rows = jnp.where(drop[...] > 0.0, 0.0, rows)
             best[...] = jnp.max(rows, axis=0, keepdims=True)[:, 64:96]
         rest = rows.T
         for _ in range(3):
             part = rest.astype(jnp.bfloat16)
             stack.append(part)
             rest = rest - part.astype(jnp.float32)
-    turned = jnp.dot(jnp.concatenate(stack, axis=0), to_lane, preferred_element_type=jnp.float32)
+    turned = jnp.dot(jnp.concatenate(stack, axis=0), to_lane[...], preferred_element_type=jnp.float32)
     for k in range(TERMS + 1):
         at = k // 4 * 384 + k % 4 * 32
         value = turned[at : at + 32] + (turned[at + 128 : at + 160] + turned[at + 256 : at + 288])
@@ -373,6 +376,15 @@
     (near,) = fit(near_fit_kernel, (up_a, up_b, down_a, down_b, *stacks), (packed(4, 2),), 2, 6, "near_fit")
     parts = fit(far_fit_kernel, (own, near, *far, *stacks), (packed(4),) * 4, 1, 3, "far_fit")
 
+    to_lane, drop = pl.pallas_call(
+        trial_order,
+        out_shape=(jax.ShapeDtypeStruct((128, 128), jnp.bfloat16), jax.ShapeDtypeStruct((128, 128), jnp.float32)),
+        in_specs=[smem, smem, vmem],
+        out_specs=(vmem,) * 2,
+        compiler_params=params,
+        cost_estimate=cost(0),
+        name="order",
+    )(place, trial_counts, jnp.tile(target_class, 4).reshape(1, 128))
     parts = (
         parts[0],
         send(parts[1], core=1),
@@ -386,12 +398,12 @@
             jax.ShapeDtypeStruct((32, 128), jnp.float32),
             jax.ShapeDtypeStruct((1, 32), jnp.float32),
         ),
-        in_specs=[smem, smem] + [vmem] * 5,
+        in_specs=[vmem] * 6,
         out_specs=(vmem,) * 3,
         compiler_params=params,
         cost_estimate=cost(2),
         name="final",
-    )(place, trial_counts, jnp.tile(target_class, 4).reshape(1, 128), *parts)
+    )(to_lane, drop, *parts)
     return coefs, gains, best.reshape(32)
 
 

time: 65 us -> 64.4 us (level)
  waiting for transfers between devices: 17.7 us -> 17 us
    ppermute x19, waiting for transfers between devices: 17.7 us -> 17 us  [send(): return lax.ppermute(value, AXES, [(d, moved(d, **how)) for d in range(128)])]
    pallas_call x0 -> x1, Pallas kernels: none -> 0.71 us  [body(): pl.pallas_call(trial_order, out_shape=(jax.ShapeDtypeStruct((128, 128), j...]
  transfers between devices with their start and end apart: 19 -> 19, of which waited for: 10 -> 9; matrix products, arithmetic and copies ran while one was open for 0% -> 0% of each run, Pallas kernels for 21% -> 22%
where the time goes in v6:
time: 64.4 us; the launch traced here: 64.2 us
  starting transfers between devices  26.7 us (41%)
  Pallas kernels  18.5 us (29%)
  waiting for transfers between devices  17 us (26%)
  local copies, waits for them, and re-layouts  1.22 us (2%)
  between operations  0.77 us (1%)
    ppermute x19, starting transfers between devices, send(): return lax.ppermute(value, AXES, [(d, moved(d, **how)) for d in range(128)])  26.7 us
    ppermute x19, waiting for transfers between devices, send(): return lax.ppermute(value, AXES, [(d, moved(d, **how)) for d in range(128)])  17 us
    pallas_call x3, Pallas kernels, fit(): pl.pallas_call(kernel, out_shape=shapes, in_specs=[smem if v is place els...  11.3 us
    pallas_call x1, Pallas kernels, body(): pl.pallas_call(weight_kernel, out_shape=(jax.ShapeDtypeStruct((count, pix...  3.08 us
  transfers between devices with their start and end apart: 19, of which 9 were waited for; matrix products, arithmetic and copies ran while one was open for 0% of the time, Pallas kernels for 22%

profile of v6, /device:TPU:1, one launch (start us, length us, event | category | flops | bytes accessed | tf_op | source)
XLA Modules:
  0.0 64.2 jit_solution(9673179366809030935)
XLA Ops:
  0.7 0.1 stack.23.place
  0.8 1.0 %copy-done = bf16[2,10,7808]{2,0,1:T(2,128)(2,1)S(1)} copy-done((bf16[2,10,7808]{2,0,1:T(2,128)(2,1)S(1)}, bf16[2,10,7808]{2,0,1:T(2,128)(2,1)}, u32[]{:S(2)}) %copy-start) | copy-done | bytes 312344
  1.7 0.7 %prep.1 = bf16[1,10,16,512]{3,2,1,0:T(8,128)(2,1)S(1)} custom-call(s32[5]{0:T(128)S(1)} %stack.23.place, bf16[10,2,7808]{2,1,0:T(2,128)(2,1)S(1)} %bitcast.9), custom_call_target="tpu_custom_call" | custom-call | flops 700000000 | bytes 2100000 | tf_op jit(solution)/shard_map/prep/pallas_call | solution.py:293
  2.4 3.7 %collective-permute-start = (bf16[1,10,16,512]{3,2,1,0:T(8,128)(2,1)S(1)}, bf16[1,10,16,512]{3,2,1,0:T(8,128)(2,1)S(1)}, u32[]{:S(2)}, u32[]{:S(2)}) collective-permute-start(bf16[1,10,16,512]{3,2,1,0:T(8,128)(2,1)S(1)} %prep.1), channel_id=1, source_target_pairs={{0,64},{1,65},{2,66},{3,67},{4,68},{5,69},{6,70},{7,71},{8,72},{9,... | collective-permute-start | bytes 491528 | tf_op jit(solution)/shard_map/ppermute | solution.py:32
  6.0 3.1 %weight.1 = (bf16[96,7808]{1,0:T(8,128)(2,1)S(1)}, bf16[112,7808]{1,0:T(8,128)(2,1)S(1)}) custom-call(s32[5]{0:T(128)S(1)} %stack.23.place, bf16[96,7808]{1,0:T(8,128)(2,1)} %flux.1, bf16[96,7808]{1,0:T(8,128)(2,1)} %ivar.1, s32[61,96]{1,0:T(8,128)} %bitcast.12, s32[1,96]{1,0:T(1,128)} %bitcast.10), custom_call_target="tpu_custom_call" | custom-call | flops 2300000000 | bytes 6899999 | tf_op jit(solution)/shard_map/weight/pallas_call | solution.py:309
  9.1 0.4 collective-permute-done
  9.5 1.7 %collective-permute-start.1 = (bf16[112,7808]{1,0:T(8,128)(2,1)S(1)}, bf16[112,7808]{1,0:T(8,128)(2,1)S(1)}, u32[]{:S(2)}, u32[]{:S(2)}) collective-permute-start(bf16[112,7808]{1,0:T(8,128)(2,1)S(1)} %get-tuple-element.27), channel_id=1, source_target_pairs={{0,1},{1,0},{2,3},{3,2},{4,5},{5,4},{6,7},{7,6},{8,9},{9,8},{10,11... | collective-permute-start | bytes 5246984 | tf_op jit(solution)/shard_map/ppermute | solution.py:32
  11.2 1.6 %collective-permute-start.2 = (bf16[2,10,16,512]{3,2,1,0:T(8,128)(2,1)S(1)}, bf16[2,10,16,512]{3,2,1,0:T(8,128)(2,1)S(1)}, u32[]{:S(2)}, u32[]{:S(2)}) collective-permute-start(bf16[2,10,16,512]{3,2,1,0:T(8,128)(2,1)S(1)} %pad_maximum_fusion.own), channel_id=1, source_target_pairs={{0,16},{1,5},{2,18},{3,7},{4,20},{5,9},{6,22},{7,11},{8,24},{9,13}... | collective-permute-start | bytes 983048 | tf_op jit(solution)/shard_map/ppermute | solution.py:32
  12.8 1.5 %collective-permute-start.3 = (bf16[2,10,16,512]{3,2,1,0:T(8,128)(2,1)S(1)}, bf16[2,10,16,512]{3,2,1,0:T(8,128)(2,1)S(1)}, u32[]{:S(2)}, u32[]{:S(2)}) collective-permute-start(bf16[2,10,16,512]{3,2,1,0:T(8,128)(2,1)S(1)} %pad_maximum_fusion.own), channel_id=1, source_target_pairs={{0,48},{1,13},{2,50},{3,15},{4,52},{5,1},{6,54},{7,3},{8,56},{9,5}... | collective-permute-start | bytes 983048 | tf_op jit(solution)/shard_map/ppermute | solution.py:32
  14.3 1.6 %collective-permute-start.4 = (bf16[2,10,16,512]{3,2,1,0:T(8,128)(2,1)S(1)}, bf16[2,10,16,512]{3,2,1,0:T(8,128)(2,1)S(1)}, u32[]{:S(2)}, u32[]{:S(2)}) collective-permute-start(bf16[2,10,16,512]{3,2,1,0:T(8,128)(2,1)S(1)} %pad_maximum_fusion.own), channel_id=1, source_target_pairs={{0,32},{1,9},{2,34},{3,11},{4,36},{5,13},{6,38},{7,15},{8,40},{9,1... | collective-permute-start | bytes 983048 | tf_op jit(solution)/shard_map/ppermute | solution.py:32
  15.9 0.0 collective-permute-done.1.other
  15.9 1.3 %coadd.1.mine = bf16[64,7808]{1,0:T(8,128)(2,1)S(1)} custom-call(s32[5]{0:T(128)S(1)} %stack.23.place, s32[1,96]{1,0:T(1,128)S(1)} %bitcast.11, bf16[96,7808]{1,0:T(8,128)(2,1)S(1)} %get-tuple-element.25.own, bf16[112,7808]{1,0:T(8,128)(2,1)S(1)} %collective-permute-done.1.other), custom_call_target="tpu_custom_call" | custom-call | flops 2400000000 | bytes 7200000 | tf_op jit(solution)/shard_map/coadd/pallas_call | solution.py:325
  17.2 0.1 fusion
  17.3 2.5 %collective-permute-start.5 = (bf16[32,7808]{1,0:T(8,128)(2,1)S(1)}, bf16[32,7808]{1,0:T(8,128)(2,1)S(1)}, u32[]{:S(2)}, u32[]{:S(2)}) collective-permute-start(bf16[32,7808]{1,0:T(8,128)(2,1)S(1)} %get-tuple-element.44), channel_id=1, source_target_pairs={{0,2},{1,67},{2,64},{3,1},{4,6},{5,71},{6,68},{7,5},{8,10},{9,75},... | collective-permute-start | bytes 1499144 | tf_op jit(solution)/shard_map/ppermute | solution.py:32
  19.8 0.0 collective-permute-start.6
  19.8 0.0 collective-permute-done.2.up
  19.8 2.0 %collective-permute-done.3.down = bf16[2,10,16,512]{3,2,1,0:T(8,128)(2,1)S(1)} collective-permute-done((bf16[2,10,16,512]{3,2,1,0:T(8,128)(2,1)S(1)}, bf16[2,10,16,512]{3,2,1,0:T(8,128)(2,1)S(1)}, u32[]{:S(2)}, u32[]{:S(2)}) %collective-permute-start.3) | collective-permute-done | bytes 327712 | tf_op jit(solution)/shard_map/ppermute | solution.py:32
  21.9 1.8 %collective-permute-done.4.far = bf16[2,10,16,512]{3,2,1,0:T(8,128)(2,1)S(1)} collective-permute-done((bf16[2,10,16,512]{3,2,1,0:T(8,128)(2,1)S(1)}, bf16[2,10,16,512]{3,2,1,0:T(8,128)(2,1)S(1)}, u32[]{:S(2)}, u32[]{:S(2)}) %collective-permute-start.4) | collective-permute-done | bytes 327712 | tf_op jit(solution)/shard_map/ppermute | solution.py:32
  23.7 0.5 join.1
  24.2 3.5 %collective-permute-start.13 = (bf16[31,5,16,128]{3,2,1,0:T(8,128)(2,1)S(1)}, bf16[31,5,16,128]{3,2,1,0:T(8,128)(2,1)S(1)}, u32[]{:S(2)}, u32[]{:S(2)}) collective-permute-start(bf16[31,5,16,128]{3,2,1,0:T(8,128)(2,1)S(1)} %get-tuple-element.30.own_b), channel_id=1, source_target_pairs={{0,12},{1,49},{2,14},{3,51},{4,0},{5,53},{6,2},{7,55},{8,4},{9,57}... | collective-permute-start | bytes 1904648 | tf_op jit(solution)/shard_map/ppermute | solution.py:32
  27.8 0.0 collective-permute-start.10
  27.8 0.8 %collective-permute-done.5.direct_a = bf16[32,7808]{1,0:T(8,128)(2,1)S(1)} collective-permute-done((bf16[32,7808]{1,0:T(8,128)(2,1)S(1)}, bf16[32,7808]{1,0:T(8,128)(2,1)S(1)}, u32[]{:S(2)}, u32[]{:S(2)}) %collective-permute-start.5) | collective-permute-done | bytes 499744 | tf_op jit(solution)/shard_map/ppermute | solution.py:32
  28.5 5.4 %collective-permute-done.6.direct_b = bf16[32,7808]{1,0:T(8,128)(2,1)S(1)} collective-permute-done((bf16[32,7808]{1,0:T(8,128)(2,1)S(1)}, bf16[32,7808]{1,0:T(8,128)(2,1)S(1)}, u32[]{:S(2)}, u32[]{:S(2)}) %collective-permute-start.6) | collective-permute-done | bytes 499744 | tf_op jit(solution)/shard_map/ppermute | solution.py:32
  34.0 0.0 collective-permute-start.7
  34.0 0.4 collective-permute-start.11
  34.4 2.2 %collective-permute-start.12 = (bf16[30,5,16,128]{3,2,1,0:T(8,128)(2,1)S(1)}, bf16[30,5,16,128]{3,2,1,0:T(8,128)(2,1)S(1)}, u32[]{:S(2)}, u32[]{:S(2)}) collective-permute-start(bf16[30,5,16,128]{3,2,1,0:T(8,128)(2,1)S(1)} %get-tuple-element.29.own_a), channel_id=1, source_target_pairs={{0,12},{1,49},{2,14},{3,51},{4,0},{5,53},{6,2},{7,55},{8,4},{9,57}... | collective-permute-start | bytes 1843208 | tf_op jit(solution)/shard_map/ppermute | solution.py:32
  36.6 1.6 %collective-permute-done.10.up_a = bf16[30,5,16,128]{3,2,1,0:T(8,128)(2,1)S(1)} collective-permute-done((bf16[30,5,16,128]{3,2,1,0:T(8,128)(2,1)S(1)}, bf16[30,5,16,128]{3,2,1,0:T(8,128)(2,1)S(1)}, u32[]{:S(2)}, u32[]{:S(2)}) %collective-permute-start.10) | collective-permute-done | bytes 614432 | tf_op jit(solution)/shard_map/ppermute | solution.py:32
  38.3 2.3 %collective-permute-start.8 = (bf16[32,7808]{1,0:T(8,128)(2,1)S(1)}, bf16[32,7808]{1,0:T(8,128)(2,1)S(1)}, u32[]{:S(2)}, u32[]{:S(2)}) collective-permute-start(bf16[32,7808]{1,0:T(8,128)(2,1)S(1)} %collective-permute-done.5.direct_a), channel_id=1, source_target_pairs={{0,1},{1,0},{2,3},{3,2},{4,5},{5,4},{6,7},{7,6},{8,9},{9,8},{10,11... | collective-permute-start | bytes 1499144 | tf_op jit(solution)/shard_map/ppermute | solution.py:32
  40.5 0.0 collective-permute-start.9
  40.6 1.5 %collective-permute-done.8.swapped_a = bf16[32,7808]{1,0:T(8,128)(2,1)S(1)} collective-permute-done((bf16[32,7808]{1,0:T(8,128)(2,1)S(1)}, bf16[32,7808]{1,0:T(8,128)(2,1)S(1)}, u32[]{:S(2)}, u32[]{:S(2)}) %collective-permute-start.8) | collective-permute-done | bytes 499744 | tf_op jit(solution)/shard_map/ppermute | solution.py:32
  42.0 1.6 %collective-permute-start.15 = (bf16[31,5,16,128]{3,2,1,0:T(8,128)(2,1)S(1)}, bf16[31,5,16,128]{3,2,1,0:T(8,128)(2,1)S(1)}, u32[]{:S(2)}, u32[]{:S(2)}) collective-permute-start(bf16[31,5,16,128]{3,2,1,0:T(8,128)(2,1)S(1)} %collective-permute-done.13.down_b), channel_id=1, source_target_pairs={{0,12},{1,49},{2,14},{3,51},{4,0},{5,53},{6,2},{7,55},{8,4},{9,57}... | collective-permute-start | bytes 1904648 | tf_op jit(solution)/shard_map/ppermute | solution.py:32
  43.6 0.0 collective-permute-done.9.swapped_b
  43.6 0.3 collective-permute-start.14
  43.9 0.0 collective-permute-done.7.over
  43.9 3.4 %own_fit.1 = (f32[4,1,3,8,128]{4,3,2,1,0:T(8,128)S(1)}, bf16[7808,128]{1,0:T(8,128)(2,1)S(1)}, bf16[7808,128]{1,0:T(8,128)(2,1)S(1)}) custom-call(s32[5]{0:T(128)S(1)} %stack.23.place, bf16[30,5,16,128]{3,2,1,0:T(8,128)(2,1)S(1)} %get-tuple-element.29.own_a, bf16[31,5,16,128]{3,2,1,0:T(8,128)(2,1)S(1)} %get-tuple-element.30.own_b, ...), custom_call_target="tpu_custom_call" | custom-call | tf_op jit(solution)/shard_map/own_fit/pallas_call | solution.py:357
  47.3 0.0 collective-permute-done.12.down_a
  47.3 5.2 %near_fit.1.near = f32[4,2,3,8,128]{4,3,2,1,0:T(8,128)S(1)} custom-call(bf16[30,5,16,128]{3,2,1,0:T(8,128)(2,1)S(1)} %collective-permute-done.10.up_a, bf16[31,5,16,128]{3,2,1,0:T(8,128)(2,1)S(1)} %collective-permute-done.11.up_b, bf16[30,5,16,128]{3,2,1,0:T(8,128)(2,1)S(1)} %collective-permute-done.12.down_a, ...), custom_call_target="tpu_custom_call" | custom-call | flops 6000000000 | bytes 18000000 | tf_op jit(solution)/shard_map/near_fit/pallas_call | solution.py:357
  52.5 1.6 %collective-permute-done.14.far_a = bf16[30,5,16,128]{3,2,1,0:T(8,128)(2,1)S(1)} collective-permute-done((bf16[30,5,16,128]{3,2,1,0:T(8,128)(2,1)S(1)}, bf16[30,5,16,128]{3,2,1,0:T(8,128)(2,1)S(1)}, u32[]{:S(2)}, u32[]{:S(2)}) %collective-permute-start.14) | collective-permute-done | bytes 614432 | tf_op jit(solution)/shard_map/ppermute | solution.py:32
  54.1 0.0 collective-permute-done.15.far_b
  54.1 2.7 %far_fit.1 = (f32[4,3,8,128]{3,2,1,0:T(8,128)S(1)}, f32[4,3,8,128]{3,2,1,0:T(8,128)S(1)}, f32[4,3,8,128]{3,2,1,0:T(8,128)S(1)}, f32[4,3,8,128]{3,2,1,0:T(8,128)S(1)}) custom-call(f32[4,1,3,8,128]{4,3,2,1,0:T(8,128)S(1)} %get-tuple-element.33.own, f32[4,2,3,8,128]{4,3,2,1,0:T(8,128)S(1)} %near_fit.1.near, ...), custom_call_target="tpu_custom_call" | custom-call | flops 3000000000 | bytes 9000000 | tf_op jit(solution)/shard_map/far_fit/pallas_call | solution.py:357
  56.8 0.5 collective-permute-start.16
  57.3 1.2 %collective-permute-start.17 = (f32[4,3,8,128]{3,2,1,0:T(8,128)S(1)}, f32[4,3,8,128]{3,2,1,0:T(8,128)S(1)}, u32[]{:S(2)}, u32[]{:S(2)}) collective-permute-start(f32[4,3,8,128]{3,2,1,0:T(8,128)S(1)} %get-tuple-element.38), channel_id=1, source_target_pairs={{0,66},{1,3},{2,0},{3,65},{4,70},{5,7},{6,4},{7,69},{8,74},{9,11},... | collective-permute-start | bytes 147464 | tf_op jit(solution)/shard_map/ppermute | solution.py:32
  58.5 2.1 %collective-permute-start.18 = (f32[4,3,8,128]{3,2,1,0:T(8,128)S(1)}, f32[4,3,8,128]{3,2,1,0:T(8,128)S(1)}, u32[]{:S(2)}, u32[]{:S(2)}) collective-permute-start(f32[4,3,8,128]{3,2,1,0:T(8,128)S(1)} %get-tuple-element.39), channel_id=1, source_target_pairs={{0,3},{1,66},{2,65},{3,0},{4,7},{5,70},{6,69},{7,4},{8,11},{9,74},... | collective-permute-start | bytes 147464 | tf_op jit(solution)/shard_map/ppermute | solution.py:32
  60.6 0.1 reshape_tile.3.classes
  60.7 0.7 %order.1 = (bf16[128,128]{1,0:T(8,128)(2,1)S(1)}, f32[128,128]{1,0:T(8,128)S(1)}) custom-call(s32[5]{0:T(128)S(1)} %stack.23.place, s32[3]{0:T(128)S(1)} %copy-done.2, s32[1,128]{1,0:T(1,128)S(1)} %reshape_tile.3.classes), custom_call_target="tpu_custom_call" | custom-call | tf_op jit(solution)/shard_map/order/pallas_call | solution.py:379
  61.4 0.0 collective-permute-done.17.part_2
  61.4 1.8 %collective-permute-done.18.part_3 = f32[4,3,8,128]{3,2,1,0:T(8,128)S(1)} collective-permute-done((f32[4,3,8,128]{3,2,1,0:T(8,128)S(1)}, f32[4,3,8,128]{3,2,1,0:T(8,128)S(1)}, u32[]{:S(2)}, u32[]{:S(2)}) %collective-permute-start.18) | collective-permute-done | bytes 49184 | tf_op jit(solution)/shard_map/ppermute | solution.py:32
  63.2 1.0 %final.1 = (f32[10,32,128]{2,1,0:T(8,128)}, f32[32,128]{1,0:T(8,128)}, f32[1,32]{1,0:T(1,128)}) custom-call(bf16[128,128]{1,0:T(8,128)(2,1)S(1)} %get-tuple-element.23.to_lane, f32[128,128]{1,0:T(8,128)S(1)} %get-tuple-element.24.drop, f32[4,3,8,128]{3,2,1,0:T(8,128)S(1)} %get-tuple-element.36.part_0, f32[4,3,8,128]{3,2,1,0:T(8,128)S(1)} %collective-permute-done.16.part_1, ...), custom_call_target="tpu_custom_call" | custom-call | flops 2000000000 | bytes 6000000 | tf_op jit(solution)/shard_map/final/pallas_call | solution.py:394
  (12 shorter events, 0.1 us)
Async XLA Ops:
  0.8 1.0 %copy-start = (bf16[2,10,7808]{2,0,1:T(2,128)(2,1)S(1)}, bf16[2,10,7808]{2,0,1:T(2,128)(2,1)}, u32[]{:S(2)}) copy-start(bf16[2,10,7808]{2,0,1:T(2,128)(2,1)} %param.11) | copy-start | bytes 936964
  2.4 7.1 %collective-permute-start = (bf16[1,10,16,512]{3,2,1,0:T(8,128)(2,1)S(1)}, bf16[1,10,16,512]{3,2,1,0:T(8,128)(2,1)S(1)}, u32[]{:S(2)}, u32[]{:S(2)}) collective-permute-start(bf16[1,10,16,512]{3,2,1,0:T(8,128)(2,1)S(1)} %prep.1), channel_id=1, source_target_pairs={{0,64},{1,65},{2,66},{3,67},{4,68},{5,69},{6,70},{7,71},{8,72},{9,... | collective-permute-start | bytes 491528 | tf_op jit(solution)/shard_map/ppermute | solution.py:32
  6.0 9.9 %copy-start.1 = (s32[96]{0:T(128)S(1)}, s32[96]{0:T(128)}, u32[]{:S(2)}) copy-start(s32[96]{0:T(128)} %param.10) | copy-start | bytes 1156
  9.5 6.4 %collective-permute-start.1 = (bf16[112,7808]{1,0:T(8,128)(2,1)S(1)}, bf16[112,7808]{1,0:T(8,128)(2,1)S(1)}, u32[]{:S(2)}, u32[]{:S(2)}) collective-permute-start(bf16[112,7808]{1,0:T(8,128)(2,1)S(1)} %get-tuple-element.27), channel_id=1, source_target_pairs={{0,1},{1,0},{2,3},{3,2},{4,5},{5,4},{6,7},{7,6},{8,9},{9,8},{10,11... | collective-permute-start | bytes 5246984 | tf_op jit(solution)/shard_map/ppermute | solution.py:32
  11.2 8.6 %collective-permute-start.2 = (bf16[2,10,16,512]{3,2,1,0:T(8,128)(2,1)S(1)}, bf16[2,10,16,512]{3,2,1,0:T(8,128)(2,1)S(1)}, u32[]{:S(2)}, u32[]{:S(2)}) collective-permute-start(bf16[2,10,16,512]{3,2,1,0:T(8,128)(2,1)S(1)} %pad_maximum_fusion.own), channel_id=1, source_target_pairs={{0,16},{1,5},{2,18},{3,7},{4,20},{5,9},{6,22},{7,11},{8,24},{9,13}... | collective-permute-start | bytes 983048 | tf_op jit(solution)/shard_map/ppermute | solution.py:32
  12.8 9.1 %collective-permute-start.3 = (bf16[2,10,16,512]{3,2,1,0:T(8,128)(2,1)S(1)}, bf16[2,10,16,512]{3,2,1,0:T(8,128)(2,1)S(1)}, u32[]{:S(2)}, u32[]{:S(2)}) collective-permute-start(bf16[2,10,16,512]{3,2,1,0:T(8,128)(2,1)S(1)} %pad_maximum_fusion.own), channel_id=1, source_target_pairs={{0,48},{1,13},{2,50},{3,15},{4,52},{5,1},{6,54},{7,3},{8,56},{9,5}... | collective-permute-start | bytes 983048 | tf_op jit(solution)/shard_map/ppermute | solution.py:32
  14.3 9.4 %collective-permute-start.4 = (bf16[2,10,16,512]{3,2,1,0:T(8,128)(2,1)S(1)}, bf16[2,10,16,512]{3,2,1,0:T(8,128)(2,1)S(1)}, u32[]{:S(2)}, u32[]{:S(2)}) collective-permute-start(bf16[2,10,16,512]{3,2,1,0:T(8,128)(2,1)S(1)} %pad_maximum_fusion.own), channel_id=1, source_target_pairs={{0,32},{1,9},{2,34},{3,11},{4,36},{5,13},{6,38},{7,15},{8,40},{9,1... | collective-permute-start | bytes 983048 | tf_op jit(solution)/shard_map/ppermute | solution.py:32
  17.3 11.2 %collective-permute-start.5 = (bf16[32,7808]{1,0:T(8,128)(2,1)S(1)}, bf16[32,7808]{1,0:T(8,128)(2,1)S(1)}, u32[]{:S(2)}, u32[]{:S(2)}) collective-permute-start(bf16[32,7808]{1,0:T(8,128)(2,1)S(1)} %get-tuple-element.44), channel_id=1, source_target_pairs={{0,2},{1,67},{2,64},{3,1},{4,6},{5,71},{6,68},{7,5},{8,10},{9,75},... | collective-permute-start | bytes 1499144 | tf_op jit(solution)/shard_map/ppermute | solution.py:32
  19.8 14.1 %collective-permute-start.6 = (bf16[32,7808]{1,0:T(8,128)(2,1)S(1)}, bf16[32,7808]{1,0:T(8,128)(2,1)S(1)}, u32[]{:S(2)}, u32[]{:S(2)}) collective-permute-start(bf16[32,7808]{1,0:T(8,128)(2,1)S(1)} %get-tuple-element.43), channel_id=1, source_target_pairs={{0,66},{1,3},{2,0},{3,65},{4,70},{5,7},{6,4},{7,69},{8,74},{9,11},... | collective-permute-start | bytes 1499144 | tf_op jit(solution)/shard_map/ppermute | solution.py:32
  24.2 16.3 %collective-permute-start.13 = (bf16[31,5,16,128]{3,2,1,0:T(8,128)(2,1)S(1)}, bf16[31,5,16,128]{3,2,1,0:T(8,128)(2,1)S(1)}, u32[]{:S(2)}, u32[]{:S(2)}) collective-permute-start(bf16[31,5,16,128]{3,2,1,0:T(8,128)(2,1)S(1)} %get-tuple-element.30.own_b), channel_id=1, source_target_pairs={{0,12},{1,49},{2,14},{3,51},{4,0},{5,53},{6,2},{7,55},{8,4},{9,57}... | collective-permute-start | bytes 1904648 | tf_op jit(solution)/shard_map/ppermute | solution.py:32
  27.8 10.5 %collective-permute-start.10 = (bf16[30,5,16,128]{3,2,1,0:T(8,128)(2,1)S(1)}, bf16[30,5,16,128]{3,2,1,0:T(8,128)(2,1)S(1)}, u32[]{:S(2)}, u32[]{:S(2)}) collective-permute-start(bf16[30,5,16,128]{3,2,1,0:T(8,128)(2,1)S(1)} %get-tuple-element.29.own_a), channel_id=1, source_target_pairs={{0,4},{1,17},{2,6},{3,19},{4,8},{5,21},{6,10},{7,23},{8,12},{9,25}... | collective-permute-start | bytes 1843208 | tf_op jit(solution)/shard_map/ppermute | solution.py:32
  34.0 10.0 %collective-permute-start.7 = (bf16[64,7808]{1,0:T(8,128)(2,1)S(1)}, bf16[64,7808]{1,0:T(8,128)(2,1)S(1)}, u32[]{:S(2)}, u32[]{:S(2)}) collective-permute-start(bf16[64,7808]{1,0:T(8,128)(2,1)S(1)} %coadd.1.mine), channel_id=1, source_target_pairs={{0,1},{1,0},{2,3},{3,2},{4,5},{5,4},{6,7},{7,6},{8,9},{9,8},{10,11... | collective-permute-start | bytes 2998280 | tf_op jit(solution)/shard_map/ppermute | solution.py:32
  34.0 13.3 %collective-permute-start.11 = (bf16[31,5,16,128]{3,2,1,0:T(8,128)(2,1)S(1)}, bf16[31,5,16,128]{3,2,1,0:T(8,128)(2,1)S(1)}, u32[]{:S(2)}, u32[]{:S(2)}) collective-permute-start(bf16[31,5,16,128]{3,2,1,0:T(8,128)(2,1)S(1)} %get-tuple-element.30.own_b), channel_id=1, source_target_pairs={{0,4},{1,17},{2,6},{3,19},{4,8},{5,21},{6,10},{7,23},{8,12},{9,25}... | collective-permute-start | bytes 1904648 | tf_op jit(solution)/shard_map/ppermute | solution.py:32
  34.4 12.9 %collective-permute-start.12 = (bf16[30,5,16,128]{3,2,1,0:T(8,128)(2,1)S(1)}, bf16[30,5,16,128]{3,2,1,0:T(8,128)(2,1)S(1)}, u32[]{:S(2)}, u32[]{:S(2)}) collective-permute-start(bf16[30,5,16,128]{3,2,1,0:T(8,128)(2,1)S(1)} %get-tuple-element.29.own_a), channel_id=1, source_target_pairs={{0,12},{1,49},{2,14},{3,51},{4,0},{5,53},{6,2},{7,55},{8,4},{9,57}... | collective-permute-start | bytes 1843208 | tf_op jit(solution)/shard_map/ppermute | solution.py:32
  38.3 3.8 %collective-permute-start.8 = (bf16[32,7808]{1,0:T(8,128)(2,1)S(1)}, bf16[32,7808]{1,0:T(8,128)(2,1)S(1)}, u32[]{:S(2)}, u32[]{:S(2)}) collective-permute-start(bf16[32,7808]{1,0:T(8,128)(2,1)S(1)} %collective-permute-done.5.direct_a), channel_id=1, source_target_pairs={{0,1},{1,0},{2,3},{3,2},{4,5},{5,4},{6,7},{7,6},{8,9},{9,8},{10,11... | collective-permute-start | bytes 1499144 | tf_op jit(solution)/shard_map/ppermute | solution.py:32
  40.5 3.1 %collective-permute-start.9 = (bf16[32,7808]{1,0:T(8,128)(2,1)S(1)}, bf16[32,7808]{1,0:T(8,128)(2,1)S(1)}, u32[]{:S(2)}, u32[]{:S(2)}) collective-permute-start(bf16[32,7808]{1,0:T(8,128)(2,1)S(1)} %collective-permute-done.6.direct_b), channel_id=1, source_target_pairs={{0,1},{1,0},{2,3},{3,2},{4,5},{5,4},{6,7},{7,6},{8,9},{9,8},{10,11... | collective-permute-start | bytes 1499144 | tf_op jit(solution)/shard_map/ppermute | solution.py:32
  42.0 12.1 %collective-permute-start.15 = (bf16[31,5,16,128]{3,2,1,0:T(8,128)(2,1)S(1)}, bf16[31,5,16,128]{3,2,1,0:T(8,128)(2,1)S(1)}, u32[]{:S(2)}, u32[]{:S(2)}) collective-permute-start(bf16[31,5,16,128]{3,2,1,0:T(8,128)(2,1)S(1)} %collective-permute-done.13.down_b), channel_id=1, source_target_pairs={{0,12},{1,49},{2,14},{3,51},{4,0},{5,53},{6,2},{7,55},{8,4},{9,57}... | collective-permute-start | bytes 1904648 | tf_op jit(solution)/shard_map/ppermute | solution.py:32
  43.6 10.5 %collective-permute-start.14 = (bf16[30,5,16,128]{3,2,1,0:T(8,128)(2,1)S(1)}, bf16[30,5,16,128]{3,2,1,0:T(8,128)(2,1)S(1)}, u32[]{:S(2)}, u32[]{:S(2)}) collective-permute-start(bf16[30,5,16,128]{3,2,1,0:T(8,128)(2,1)S(1)} %collective-permute-done.10.up_a), channel_id=1, source_target_pairs={{0,4},{1,17},{2,6},{3,19},{4,8},{5,21},{6,10},{7,23},{8,12},{9,25}... | collective-permute-start | bytes 1843208 | tf_op jit(solution)/shard_map/ppermute | solution.py:32
  54.1 6.5 %copy-start.3 = (s32[32]{0:T(128)S(1)}, s32[32]{0:T(128)}, u32[]{:S(2)}) copy-start(s32[32]{0:T(128)} %param.13) | copy-start | bytes 388
  54.1 6.6 %copy-start.2 = (s32[3]{0:T(128)S(1)}, s32[3]{0:T(128)}, u32[]{:S(2)}) copy-start(s32[3]{0:T(128)} %counts.1) | copy-start | bytes 40
  56.8 4.6 %collective-permute-start.16 = (f32[4,3,8,128]{3,2,1,0:T(8,128)S(1)}, f32[4,3,8,128]{3,2,1,0:T(8,128)S(1)}, u32[]{:S(2)}, u32[]{:S(2)}) collective-permute-start(f32[4,3,8,128]{3,2,1,0:T(8,128)S(1)} %get-tuple-element.37), channel_id=1, source_target_pairs={{0,1},{1,0},{2,3},{3,2},{4,5},{5,4},{6,7},{7,6},{8,9},{9,8},{10,11... | collective-permute-start | bytes 147464 | tf_op jit(solution)/shard_map/ppermute | solution.py:32
  57.3 4.2 %collective-permute-start.17 = (f32[4,3,8,128]{3,2,1,0:T(8,128)S(1)}, f32[4,3,8,128]{3,2,1,0:T(8,128)S(1)}, u32[]{:S(2)}, u32[]{:S(2)}) collective-permute-start(f32[4,3,8,128]{3,2,1,0:T(8,128)S(1)} %get-tuple-element.38), channel_id=1, source_target_pairs={{0,66},{1,3},{2,0},{3,65},{4,70},{5,7},{6,4},{7,69},{8,74},{9,11},... | collective-permute-start | bytes 147464 | tf_op jit(solution)/shard_map/ppermute | solution.py:32
  58.5 4.7 %collective-permute-start.18 = (f32[4,3,8,128]{3,2,1,0:T(8,128)S(1)}, f32[4,3,8,128]{3,2,1,0:T(8,128)S(1)}, u32[]{:S(2)}, u32[]{:S(2)}) collective-permute-start(f32[4,3,8,128]{3,2,1,0:T(8,128)S(1)} %get-tuple-element.39), channel_id=1, source_target_pairs={{0,3},{1,66},{2,65},{3,0},{4,7},{5,70},{6,69},{7,4},{8,11},{9,74},... | collective-permute-start | bytes 147464 | tf_op jit(solution)/shard_map/ppermute | solution.py:32

commit v7 on v6

--- a/solution.py
+++ b/solution.py
@@ -151,10 +151,10 @@
     return answer
 
 
-def fit_blocks(blocks, pixels, stacks, total):
-    for at in range(0, pixels // 128, WIDTH // 128):
-        taken = range(at, min(at + WIDTH // 128, pixels // 128))
-        ivar, wflux = stacks(slice(at * 128, (at + len(taken)) * 128))
+def add_up(blocks, begin, count, stacks, total, fresh):
+    for at in range(0, count, WIDTH // 128):
+        taken = range(at, min(at + WIDTH // 128, count))
+        ivar, wflux = stacks(slice((begin + at) * 128, (begin + at + len(taken)) * 128))
         for b, refs in enumerate(blocks):
             evens = []
             for m in range(HALVES):
@@ -166,13 +166,15 @@
             )
             normal = jnp.dot(products, ivar, preferred_element_type=jnp.float32)
             project = jnp.dot(jnp.concatenate(evens, axis=0), wflux, preferred_element_type=jnp.float32)
-            if at == 0:
+            if fresh and at == 0:
                 total[b, 0 : COMBOS * 16] = normal
                 total[b, COMBOS * 16 : ROWS] = project
             else:
                 total[b, 0 : COMBOS * 16] += normal
                 total[b, COMBOS * 16 : ROWS] += project
 
+
+def solve_all(total):
     entries = {}
     for (k, l), at in entry_rows().items():
         value = total[:, at : at + 8, :]
@@ -208,22 +210,32 @@
         ivar[span, :], wflux[span, :] = both
         return both
 
-    packed = fit_blocks([[own_a, own_b]], mine.shape[1], stacks, total)
+    add_up([[own_a, own_b]], 0, mine.shape[1] // 128, stacks, total, True)
+    packed = solve_all(total)
     for group in range(4):
         for q in range(3):
             out[group, :, q] = packed[group][q]
 
 
 def near_fit_kernel(up_a, up_b, down_a, down_b, ivar, wflux, out, total):
-    packed = fit_blocks([[up_a, up_b], [down_a, down_b]], ivar.shape[0], lambda span: (ivar[span, :], wflux[span, :]), total)
+    whole = ivar.shape[0] // 128
+    add_up([[up_a, up_b], [down_a, down_b]], 0, whole, lambda span: (ivar[span, :], wflux[span, :]), total, True)
+    packed = solve_all(total)
     for group in range(4):
         for q in range(3):
             out[group, :, q] = packed[group][q]
 
 
-def far_fit_kernel(own, near, far_a, far_b, ivar, wflux, *rest):
+def half_fit_kernel(_, far_b, ivar, wflux, total):
+    count = far_b.shape[0]
+    add_up([[far_b]], ivar.shape[0] // 128 - count, count, lambda span: (ivar[span, :], wflux[span, :]), total, True)
+
+
+def far_fit_kernel(own, near, half, far_a, ivar, wflux, *rest):
     outs, total = rest[:4], rest[4]
-    packed = fit_blocks([[far_a, far_b]], ivar.shape[0], lambda span: (ivar[span, :], wflux[span, :]), total)
+    total[...] = half[...]
+    add_up([[far_a]], 0, far_a.shape[0], lambda span: (ivar[span, :], wflux[span, :]), total, False)
+    packed = solve_all(total)
     for group in range(4):
         outs[group][0:1] = own[group]
         outs[group][1:3] = near[group]
@@ -374,7 +386,16 @@
         own_fit_kernel, (place, *eight, mine, *direct, over, *swapped), (packed(4, 1), stack, stack), 1, 0, "own_fit"
     )
     (near,) = fit(near_fit_kernel, (up_a, up_b, down_a, down_b, *stacks), (packed(4, 2),), 2, 6, "near_fit")
-    parts = fit(far_fit_kernel, (own, near, *far, *stacks), (packed(4),) * 4, 1, 3, "far_fit")
+    half = pl.pallas_call(
+        half_fit_kernel,
+        out_shape=jax.ShapeDtypeStruct((1, ROWS, 128), jnp.float32),
+        in_specs=[pl.BlockSpec(memory_space=pl.ANY)] + [vmem] * 3,
+        out_specs=vmem,
+        compiler_params=params,
+        cost_estimate=cost(0),
+        name="half_fit",
+    )(near, far[1], *stacks)
+    parts = fit(far_fit_kernel, (own, near, half, far[0], *stacks), (packed(4),) * 4, 1, 3, "far_fit")
 
     to_lane, drop = pl.pallas_call(
         trial_order,

time: 64.4 us -> 61.6 us (0.957)
  waiting for transfers between devices: 17 us -> 14.6 us
    ppermute x19, waiting for transfers between devices: 17 us -> 14.6 us  [send(): return lax.ppermute(value, AXES, [(d, moved(d, **how)) for d in range(128)])]
    pallas_call x0 -> x1, Pallas kernels: none -> 1.37 us  [body(): pl.pallas_call(half_fit_kernel, out_shape=jax.ShapeDtypeStruct((1, ROWS,...]
    pallas_call x3, Pallas kernels: 11.3 us -> 10.1 us  [fit(): pl.pallas_call(kernel, out_shape=shapes, in_specs=[smem if v is place els...]
  transfers between devices with their start and end apart: 19 -> 19, of which waited for: 9 -> 10; matrix products, arithmetic and copies ran while one was open for 0% -> 0% of each run, Pallas kernels for 22% -> 25%
where the time goes in v7:
time: 61.6 us; the launch traced here: 61.4 us
  starting transfers between devices  26.1 us (42%)
  Pallas kernels  18.7 us (30%)
  waiting for transfers between devices  14.6 us (24%)
  local copies, waits for them, and re-layouts  1.23 us (2%)
  between operations  0.79 us (1%)
    ppermute x19, starting transfers between devices, send(): return lax.ppermute(value, AXES, [(d, moved(d, **how)) for d in range(128)])  26.1 us
    ppermute x19, waiting for transfers between devices, send(): return lax.ppermute(value, AXES, [(d, moved(d, **how)) for d in range(128)])  14.6 us
    pallas_call x3, Pallas kernels, fit(): pl.pallas_call(kernel, out_shape=shapes, in_specs=[smem if v is place els...  10.1 us
    pallas_call x1, Pallas kernels, body(): pl.pallas_call(weight_kernel, out_shape=(jax.ShapeDtypeStruct((count, pix...  3.08 us
    pallas_call x1, Pallas kernels, body(): pl.pallas_call(half_fit_kernel, out_shape=jax.ShapeDtypeStruct((1, ROWS,...  1.37 us
    pallas_call x1, Pallas kernels, body(): pl.pallas_call(coadd_kernel, out_shape=jax.ShapeDtypeStruct((64, pixels),...  1.29 us
  transfers between devices with their start and end apart: 19, of which 10 were waited for; matrix products, arithmetic and copies ran while one was open for 0% of the time, Pallas kernels for 25%

profile of v7, /device:TPU:1, one launch (start us, length us, event | category | flops | bytes accessed | tf_op | source)
XLA Modules:
  0.0 61.4 jit_solution(8539966819219374521)
XLA Ops:
  0.7 0.1 stack.23.place
  0.8 1.0 %copy-done = bf16[2,10,7808]{2,0,1:T(2,128)(2,1)S(1)} copy-done((bf16[2,10,7808]{2,0,1:T(2,128)(2,1)S(1)}, bf16[2,10,7808]{2,0,1:T(2,128)(2,1)}, u32[]{:S(2)}) %copy-start) | copy-done | bytes 312344
  1.7 0.7 %prep.1 = bf16[1,10,16,512]{3,2,1,0:T(8,128)(2,1)S(1)} custom-call(s32[5]{0:T(128)S(1)} %stack.23.place, bf16[10,2,7808]{2,1,0:T(2,128)(2,1)S(1)} %bitcast.9), custom_call_target="tpu_custom_call" | custom-call | flops 700000000 | bytes 2100000 | tf_op jit(solution)/shard_map/prep/pallas_call | solution.py:305
  2.4 3.7 %collective-permute-start = (bf16[1,10,16,512]{3,2,1,0:T(8,128)(2,1)S(1)}, bf16[1,10,16,512]{3,2,1,0:T(8,128)(2,1)S(1)}, u32[]{:S(2)}, u32[]{:S(2)}) collective-permute-start(bf16[1,10,16,512]{3,2,1,0:T(8,128)(2,1)S(1)} %prep.1), channel_id=1, source_target_pairs={{0,64},{1,65},{2,66},{3,67},{4,68},{5,69},{6,70},{7,71},{8,72},{9,... | collective-permute-start | bytes 491528 | tf_op jit(solution)/shard_map/ppermute | solution.py:32
  6.0 3.1 %weight.1 = (bf16[96,7808]{1,0:T(8,128)(2,1)S(1)}, bf16[112,7808]{1,0:T(8,128)(2,1)S(1)}) custom-call(s32[5]{0:T(128)S(1)} %stack.23.place, bf16[96,7808]{1,0:T(8,128)(2,1)} %flux.1, bf16[96,7808]{1,0:T(8,128)(2,1)} %ivar.1, s32[61,96]{1,0:T(8,128)} %bitcast.12, s32[1,96]{1,0:T(1,128)} %bitcast.10), custom_call_target="tpu_custom_call" | custom-call | flops 2300000000 | bytes 6899999 | tf_op jit(solution)/shard_map/weight/pallas_call | solution.py:321
  9.1 0.4 collective-permute-done
  9.5 1.7 %collective-permute-start.1 = (bf16[112,7808]{1,0:T(8,128)(2,1)S(1)}, bf16[112,7808]{1,0:T(8,128)(2,1)S(1)}, u32[]{:S(2)}, u32[]{:S(2)}) collective-permute-start(bf16[112,7808]{1,0:T(8,128)(2,1)S(1)} %get-tuple-element.27), channel_id=1, source_target_pairs={{0,1},{1,0},{2,3},{3,2},{4,5},{5,4},{6,7},{7,6},{8,9},{9,8},{10,11... | collective-permute-start | bytes 5246984 | tf_op jit(solution)/shard_map/ppermute | solution.py:32
  11.2 1.6 %collective-permute-start.2 = (bf16[2,10,16,512]{3,2,1,0:T(8,128)(2,1)S(1)}, bf16[2,10,16,512]{3,2,1,0:T(8,128)(2,1)S(1)}, u32[]{:S(2)}, u32[]{:S(2)}) collective-permute-start(bf16[2,10,16,512]{3,2,1,0:T(8,128)(2,1)S(1)} %pad_maximum_fusion.own), channel_id=1, source_target_pairs={{0,16},{1,5},{2,18},{3,7},{4,20},{5,9},{6,22},{7,11},{8,24},{9,13}... | collective-permute-start | bytes 983048 | tf_op jit(solution)/shard_map/ppermute | solution.py:32
  12.8 1.5 %collective-permute-start.3 = (bf16[2,10,16,512]{3,2,1,0:T(8,128)(2,1)S(1)}, bf16[2,10,16,512]{3,2,1,0:T(8,128)(2,1)S(1)}, u32[]{:S(2)}, u32[]{:S(2)}) collective-permute-start(bf16[2,10,16,512]{3,2,1,0:T(8,128)(2,1)S(1)} %pad_maximum_fusion.own), channel_id=1, source_target_pairs={{0,48},{1,13},{2,50},{3,15},{4,52},{5,1},{6,54},{7,3},{8,56},{9,5}... | collective-permute-start | bytes 983048 | tf_op jit(solution)/shard_map/ppermute | solution.py:32
  14.3 1.6 %collective-permute-start.4 = (bf16[2,10,16,512]{3,2,1,0:T(8,128)(2,1)S(1)}, bf16[2,10,16,512]{3,2,1,0:T(8,128)(2,1)S(1)}, u32[]{:S(2)}, u32[]{:S(2)}) collective-permute-start(bf16[2,10,16,512]{3,2,1,0:T(8,128)(2,1)S(1)} %pad_maximum_fusion.own), channel_id=1, source_target_pairs={{0,32},{1,9},{2,34},{3,11},{4,36},{5,13},{6,38},{7,15},{8,40},{9,1... | collective-permute-start | bytes 983048 | tf_op jit(solution)/shard_map/ppermute | solution.py:32
  15.9 0.0 collective-permute-done.1.other
  15.9 1.3 %coadd.1.mine = bf16[64,7808]{1,0:T(8,128)(2,1)S(1)} custom-call(s32[5]{0:T(128)S(1)} %stack.23.place, s32[1,96]{1,0:T(1,128)S(1)} %bitcast.11, bf16[96,7808]{1,0:T(8,128)(2,1)S(1)} %get-tuple-element.25.own, bf16[112,7808]{1,0:T(8,128)(2,1)S(1)} %collective-permute-done.1.other), custom_call_target="tpu_custom_call" | custom-call | flops 2400000000 | bytes 7200000 | tf_op jit(solution)/shard_map/coadd/pallas_call | solution.py:337
  17.2 0.1 fusion
  17.3 2.5 %collective-permute-start.5 = (bf16[32,7808]{1,0:T(8,128)(2,1)S(1)}, bf16[32,7808]{1,0:T(8,128)(2,1)S(1)}, u32[]{:S(2)}, u32[]{:S(2)}) collective-permute-start(bf16[32,7808]{1,0:T(8,128)(2,1)S(1)} %get-tuple-element.44), channel_id=1, source_target_pairs={{0,2},{1,67},{2,64},{3,1},{4,6},{5,71},{6,68},{7,5},{8,10},{9,75},... | collective-permute-start | bytes 1499144 | tf_op jit(solution)/shard_map/ppermute | solution.py:32
  19.8 0.0 collective-permute-start.6
  19.8 2.0 %collective-permute-done.3.down = bf16[2,10,16,512]{3,2,1,0:T(8,128)(2,1)S(1)} collective-permute-done((bf16[2,10,16,512]{3,2,1,0:T(8,128)(2,1)S(1)}, bf16[2,10,16,512]{3,2,1,0:T(8,128)(2,1)S(1)}, u32[]{:S(2)}, u32[]{:S(2)}) %collective-permute-start.3) | collective-permute-done | bytes 327712 | tf_op jit(solution)/shard_map/ppermute | solution.py:32
  21.9 1.8 %collective-permute-done.4.far = bf16[2,10,16,512]{3,2,1,0:T(8,128)(2,1)S(1)} collective-permute-done((bf16[2,10,16,512]{3,2,1,0:T(8,128)(2,1)S(1)}, bf16[2,10,16,512]{3,2,1,0:T(8,128)(2,1)S(1)}, u32[]{:S(2)}, u32[]{:S(2)}) %collective-permute-start.4) | collective-permute-done | bytes 327712 | tf_op jit(solution)/shard_map/ppermute | solution.py:32
  23.7 0.5 join.1
  24.2 1.4 %collective-permute-start.10 = (bf16[30,5,16,128]{3,2,1,0:T(8,128)(2,1)S(1)}, bf16[30,5,16,128]{3,2,1,0:T(8,128)(2,1)S(1)}, u32[]{:S(2)}, u32[]{:S(2)}) collective-permute-start(bf16[30,5,16,128]{3,2,1,0:T(8,128)(2,1)S(1)} %get-tuple-element.29.own_a), channel_id=1, source_target_pairs={{0,4},{1,17},{2,6},{3,19},{4,8},{5,21},{6,10},{7,23},{8,12},{9,25}... | collective-permute-start | bytes 1843208 | tf_op jit(solution)/shard_map/ppermute | solution.py:32
  25.6 2.2 %collective-permute-start.13 = (bf16[31,5,16,128]{3,2,1,0:T(8,128)(2,1)S(1)}, bf16[31,5,16,128]{3,2,1,0:T(8,128)(2,1)S(1)}, u32[]{:S(2)}, u32[]{:S(2)}) collective-permute-start(bf16[31,5,16,128]{3,2,1,0:T(8,128)(2,1)S(1)} %get-tuple-element.30.own_b), channel_id=1, source_target_pairs={{0,12},{1,49},{2,14},{3,51},{4,0},{5,53},{6,2},{7,55},{8,4},{9,57}... | collective-permute-start | bytes 1904648 | tf_op jit(solution)/shard_map/ppermute | solution.py:32
  27.8 0.7 %collective-permute-done.5.direct_a = bf16[32,7808]{1,0:T(8,128)(2,1)S(1)} collective-permute-done((bf16[32,7808]{1,0:T(8,128)(2,1)S(1)}, bf16[32,7808]{1,0:T(8,128)(2,1)S(1)}, u32[]{:S(2)}, u32[]{:S(2)}) %collective-permute-start.5) | collective-permute-done | bytes 499744 | tf_op jit(solution)/shard_map/ppermute | solution.py:32
  28.5 5.4 %collective-permute-done.6.direct_b = bf16[32,7808]{1,0:T(8,128)(2,1)S(1)} collective-permute-done((bf16[32,7808]{1,0:T(8,128)(2,1)S(1)}, bf16[32,7808]{1,0:T(8,128)(2,1)S(1)}, u32[]{:S(2)}, u32[]{:S(2)}) %collective-permute-start.6) | collective-permute-done | bytes 499744 | tf_op jit(solution)/shard_map/ppermute | solution.py:32
  34.0 0.0 collective-permute-start.7
  34.0 0.7 %collective-permute-start.11 = (bf16[31,5,16,128]{3,2,1,0:T(8,128)(2,1)S(1)}, bf16[31,5,16,128]{3,2,1,0:T(8,128)(2,1)S(1)}, u32[]{:S(2)}, u32[]{:S(2)}) collective-permute-start(bf16[31,5,16,128]{3,2,1,0:T(8,128)(2,1)S(1)} %get-tuple-element.30.own_b), channel_id=1, source_target_pairs={{0,4},{1,17},{2,6},{3,19},{4,8},{5,21},{6,10},{7,23},{8,12},{9,25}... | collective-permute-start | bytes 1904648 | tf_op jit(solution)/shard_map/ppermute | solution.py:32
  34.7 1.9 %collective-permute-start.12 = (bf16[30,5,16,128]{3,2,1,0:T(8,128)(2,1)S(1)}, bf16[30,5,16,128]{3,2,1,0:T(8,128)(2,1)S(1)}, u32[]{:S(2)}, u32[]{:S(2)}) collective-permute-start(bf16[30,5,16,128]{3,2,1,0:T(8,128)(2,1)S(1)} %get-tuple-element.29.own_a), channel_id=1, source_target_pairs={{0,12},{1,49},{2,14},{3,51},{4,0},{5,53},{6,2},{7,55},{8,4},{9,57}... | collective-permute-start | bytes 1843208 | tf_op jit(solution)/shard_map/ppermute | solution.py:32
  36.6 1.1 %collective-permute-start.8 = (bf16[32,7808]{1,0:T(8,128)(2,1)S(1)}, bf16[32,7808]{1,0:T(8,128)(2,1)S(1)}, u32[]{:S(2)}, u32[]{:S(2)}) collective-permute-start(bf16[32,7808]{1,0:T(8,128)(2,1)S(1)} %collective-permute-done.5.direct_a), channel_id=1, source_target_pairs={{0,1},{1,0},{2,3},{3,2},{4,5},{5,4},{6,7},{7,6},{8,9},{9,8},{10,11... | collective-permute-start | bytes 1499144 | tf_op jit(solution)/shard_map/ppermute | solution.py:32
  37.7 0.4 collective-permute-start.9
  38.1 1.1 %collective-permute-done.8.swapped_a = bf16[32,7808]{1,0:T(8,128)(2,1)S(1)} collective-permute-done((bf16[32,7808]{1,0:T(8,128)(2,1)S(1)}, bf16[32,7808]{1,0:T(8,128)(2,1)S(1)}, u32[]{:S(2)}, u32[]{:S(2)}) %collective-permute-start.8) | collective-permute-done | bytes 499744 | tf_op jit(solution)/shard_map/ppermute | solution.py:32
  39.2 1.4 %collective-permute-start.14 = (bf16[31,5,16,128]{3,2,1,0:T(8,128)(2,1)S(1)}, bf16[31,5,16,128]{3,2,1,0:T(8,128)(2,1)S(1)}, u32[]{:S(2)}, u32[]{:S(2)}) collective-permute-start(bf16[31,5,16,128]{3,2,1,0:T(8,128)(2,1)S(1)} %collective-permute-done.13.down_b), channel_id=1, source_target_pairs={{0,12},{1,49},{2,14},{3,51},{4,0},{5,53},{6,2},{7,55},{8,4},{9,57}... | collective-permute-start | bytes 1904648 | tf_op jit(solution)/shard_map/ppermute | solution.py:32
  40.6 0.0 collective-permute-done.9.swapped_b
  40.6 0.3 collective-permute-start.15
  40.9 3.4 %own_fit.1 = (f32[4,1,3,8,128]{4,3,2,1,0:T(8,128)S(1)}, bf16[7808,128]{1,0:T(8,128)(2,1)S(1)}, bf16[7808,128]{1,0:T(8,128)(2,1)S(1)}) custom-call(s32[5]{0:T(128)S(1)} %stack.23.place, bf16[30,5,16,128]{3,2,1,0:T(8,128)(2,1)S(1)} %get-tuple-element.29.own_a, bf16[31,5,16,128]{3,2,1,0:T(8,128)(2,1)S(1)} %get-tuple-element.30.own_b, ...), custom_call_target="tpu_custom_call" | custom-call | tf_op jit(solution)/shard_map/own_fit/pallas_call | solution.py:369
  44.3 0.4 collective-permute-done.11.up_b
  44.7 5.2 %near_fit.1._.near = f32[4,2,3,8,128]{4,3,2,1,0:T(8,128)S(1)} custom-call(bf16[30,5,16,128]{3,2,1,0:T(8,128)(2,1)S(1)} %collective-permute-done.10.up_a, bf16[31,5,16,128]{3,2,1,0:T(8,128)(2,1)S(1)} %collective-permute-done.11.up_b, bf16[30,5,16,128]{3,2,1,0:T(8,128)(2,1)S(1)} %collective-permute-done.12.down_a, ...), custom_call_target="tpu_custom_call" | custom-call | flops 6000000000 | bytes 18000000 | tf_op jit(solution)/shard_map/near_fit/pallas_call | solution.py:369
  49.9 0.9 %collective-permute-done.14.far_b = bf16[31,5,16,128]{3,2,1,0:T(8,128)(2,1)S(1)} collective-permute-done((bf16[31,5,16,128]{3,2,1,0:T(8,128)(2,1)S(1)}, bf16[31,5,16,128]{3,2,1,0:T(8,128)(2,1)S(1)}, u32[]{:S(2)}, u32[]{:S(2)}) %collective-permute-start.14) | collective-permute-done | bytes 634912 | tf_op jit(solution)/shard_map/ppermute | solution.py:32
  50.8 1.4 %half_fit.1.half = f32[1,560,128]{2,1,0:T(8,128)S(1)} custom-call(f32[4,2,3,8,128]{4,3,2,1,0:T(8,128)S(1)} %near_fit.1._.near, bf16[31,5,16,128]{3,2,1,0:T(8,128)(2,1)S(1)} %collective-permute-done.14.far_b, bf16[7808,128]{1,0:T(8,128)(2,1)S(1)} %get-tuple-element.34.ivar, bf16[7808,128]{1,0:T(8,128)(2,1)S(1)} %get-tuple-element.35.wflux), custom_call_target="tpu_custom_call" | custom-call | tf_op jit(solution)/shard_map/half_fit/pallas_call | solution.py:389
  52.2 0.0 copy-start.3
  52.2 0.0 copy-start.2
  52.2 1.5 %far_fit.1 = (f32[4,3,8,128]{3,2,1,0:T(8,128)S(1)}, f32[4,3,8,128]{3,2,1,0:T(8,128)S(1)}, f32[4,3,8,128]{3,2,1,0:T(8,128)S(1)}, f32[4,3,8,128]{3,2,1,0:T(8,128)S(1)}) custom-call(f32[4,1,3,8,128]{4,3,2,1,0:T(8,128)S(1)} %get-tuple-element.33.own, f32[4,2,3,8,128]{4,3,2,1,0:T(8,128)S(1)} %near_fit.1._.near, f32[1,560,128]{2,1,0:T(8,128)S(1)} %half_fit.1.half, ...), custom_call_target="tpu_custom_call" | custom-call | flops 3000000000 | bytes 9000000 | tf_op jit(solution)/shard_map/far_fit/pallas_call | solution.py:369
  53.7 1.8 %collective-permute-start.16 = (f32[4,3,8,128]{3,2,1,0:T(8,128)S(1)}, f32[4,3,8,128]{3,2,1,0:T(8,128)S(1)}, u32[]{:S(2)}, u32[]{:S(2)}) collective-permute-start(f32[4,3,8,128]{3,2,1,0:T(8,128)S(1)} %get-tuple-element.37), channel_id=1, source_target_pairs={{0,1},{1,0},{2,3},{3,2},{4,5},{5,4},{6,7},{7,6},{8,9},{9,8},{10,11... | collective-permute-start | bytes 147464 | tf_op jit(solution)/shard_map/ppermute | solution.py:32
  55.5 0.2 collective-permute-start.17
  55.7 2.1 %collective-permute-start.18 = (f32[4,3,8,128]{3,2,1,0:T(8,128)S(1)}, f32[4,3,8,128]{3,2,1,0:T(8,128)S(1)}, u32[]{:S(2)}, u32[]{:S(2)}) collective-permute-start(f32[4,3,8,128]{3,2,1,0:T(8,128)S(1)} %get-tuple-element.39), channel_id=1, source_target_pairs={{0,3},{1,66},{2,65},{3,0},{4,7},{5,70},{6,69},{7,4},{8,11},{9,74},... | collective-permute-start | bytes 147464 | tf_op jit(solution)/shard_map/ppermute | solution.py:32
  57.8 0.1 reshape_tile.3.classes
  57.9 0.7 %order.1 = (bf16[128,128]{1,0:T(8,128)(2,1)S(1)}, f32[128,128]{1,0:T(8,128)S(1)}) custom-call(s32[5]{0:T(128)S(1)} %stack.23.place, s32[3]{0:T(128)S(1)} %copy-done.2, s32[1,128]{1,0:T(1,128)S(1)} %reshape_tile.3.classes), custom_call_target="tpu_custom_call" | custom-call | tf_op jit(solution)/shard_map/order/pallas_call | solution.py:400
  58.6 0.0 collective-permute-done.16.part_1
  58.6 1.0 %collective-permute-done.17.part_2 = f32[4,3,8,128]{3,2,1,0:T(8,128)S(1)} collective-permute-done((f32[4,3,8,128]{3,2,1,0:T(8,128)S(1)}, f32[4,3,8,128]{3,2,1,0:T(8,128)S(1)}, u32[]{:S(2)}, u32[]{:S(2)}) %collective-permute-start.17) | collective-permute-done | bytes 49184 | tf_op jit(solution)/shard_map/ppermute | solution.py:32
  59.7 0.8 %collective-permute-done.18.part_3 = f32[4,3,8,128]{3,2,1,0:T(8,128)S(1)} collective-permute-done((f32[4,3,8,128]{3,2,1,0:T(8,128)S(1)}, f32[4,3,8,128]{3,2,1,0:T(8,128)S(1)}, u32[]{:S(2)}, u32[]{:S(2)}) %collective-permute-start.18) | collective-permute-done | bytes 49184 | tf_op jit(solution)/shard_map/ppermute | solution.py:32
  60.5 1.0 %final.1 = (f32[10,32,128]{2,1,0:T(8,128)}, f32[32,128]{1,0:T(8,128)}, f32[1,32]{1,0:T(1,128)}) custom-call(bf16[128,128]{1,0:T(8,128)(2,1)S(1)} %get-tuple-element.23.to_lane, f32[128,128]{1,0:T(8,128)S(1)} %get-tuple-element.24.drop, f32[4,3,8,128]{3,2,1,0:T(8,128)S(1)} %get-tuple-element.36.part_0, f32[4,3,8,128]{3,2,1,0:T(8,128)S(1)} %collective-permute-done.16.part_1, ...), custom_call_target="tpu_custom_call" | custom-call | flops 2000000000 | bytes 6000000 | tf_op jit(solution)/shard_map/final/pallas_call | solution.py:415
  (13 shorter events, 0.1 us)
Async XLA Ops:
  0.8 1.0 %copy-start = (bf16[2,10,7808]{2,0,1:T(2,128)(2,1)S(1)}, bf16[2,10,7808]{2,0,1:T(2,128)(2,1)}, u32[]{:S(2)}) copy-start(bf16[2,10,7808]{2,0,1:T(2,128)(2,1)} %param.11) | copy-start | bytes 936964
  2.4 7.1 %collective-permute-start = (bf16[1,10,16,512]{3,2,1,0:T(8,128)(2,1)S(1)}, bf16[1,10,16,512]{3,2,1,0:T(8,128)(2,1)S(1)}, u32[]{:S(2)}, u32[]{:S(2)}) collective-permute-start(bf16[1,10,16,512]{3,2,1,0:T(8,128)(2,1)S(1)} %prep.1), channel_id=1, source_target_pairs={{0,64},{1,65},{2,66},{3,67},{4,68},{5,69},{6,70},{7,71},{8,72},{9,... | collective-permute-start | bytes 491528 | tf_op jit(solution)/shard_map/ppermute | solution.py:32
  6.0 9.9 %copy-start.1 = (s32[96]{0:T(128)S(1)}, s32[96]{0:T(128)}, u32[]{:S(2)}) copy-start(s32[96]{0:T(128)} %param.10) | copy-start | bytes 1156
  9.5 6.4 %collective-permute-start.1 = (bf16[112,7808]{1,0:T(8,128)(2,1)S(1)}, bf16[112,7808]{1,0:T(8,128)(2,1)S(1)}, u32[]{:S(2)}, u32[]{:S(2)}) collective-permute-start(bf16[112,7808]{1,0:T(8,128)(2,1)S(1)} %get-tuple-element.27), channel_id=1, source_target_pairs={{0,1},{1,0},{2,3},{3,2},{4,5},{5,4},{6,7},{7,6},{8,9},{9,8},{10,11... | collective-permute-start | bytes 5246984 | tf_op jit(solution)/shard_map/ppermute | solution.py:32
  11.2 8.6 %collective-permute-start.2 = (bf16[2,10,16,512]{3,2,1,0:T(8,128)(2,1)S(1)}, bf16[2,10,16,512]{3,2,1,0:T(8,128)(2,1)S(1)}, u32[]{:S(2)}, u32[]{:S(2)}) collective-permute-start(bf16[2,10,16,512]{3,2,1,0:T(8,128)(2,1)S(1)} %pad_maximum_fusion.own), channel_id=1, source_target_pairs={{0,16},{1,5},{2,18},{3,7},{4,20},{5,9},{6,22},{7,11},{8,24},{9,13}... | collective-permute-start | bytes 983048 | tf_op jit(solution)/shard_map/ppermute | solution.py:32
  12.8 9.1 %collective-permute-start.3 = (bf16[2,10,16,512]{3,2,1,0:T(8,128)(2,1)S(1)}, bf16[2,10,16,512]{3,2,1,0:T(8,128)(2,1)S(1)}, u32[]{:S(2)}, u32[]{:S(2)}) collective-permute-start(bf16[2,10,16,512]{3,2,1,0:T(8,128)(2,1)S(1)} %pad_maximum_fusion.own), channel_id=1, source_target_pairs={{0,48},{1,13},{2,50},{3,15},{4,52},{5,1},{6,54},{7,3},{8,56},{9,5}... | collective-permute-start | bytes 983048 | tf_op jit(solution)/shard_map/ppermute | solution.py:32
  14.3 9.4 %collective-permute-start.4 = (bf16[2,10,16,512]{3,2,1,0:T(8,128)(2,1)S(1)}, bf16[2,10,16,512]{3,2,1,0:T(8,128)(2,1)S(1)}, u32[]{:S(2)}, u32[]{:S(2)}) collective-permute-start(bf16[2,10,16,512]{3,2,1,0:T(8,128)(2,1)S(1)} %pad_maximum_fusion.own), channel_id=1, source_target_pairs={{0,32},{1,9},{2,34},{3,11},{4,36},{5,13},{6,38},{7,15},{8,40},{9,1... | collective-permute-start | bytes 983048 | tf_op jit(solution)/shard_map/ppermute | solution.py:32
  17.3 11.2 %collective-permute-start.5 = (bf16[32,7808]{1,0:T(8,128)(2,1)S(1)}, bf16[32,7808]{1,0:T(8,128)(2,1)S(1)}, u32[]{:S(2)}, u32[]{:S(2)}) collective-permute-start(bf16[32,7808]{1,0:T(8,128)(2,1)S(1)} %get-tuple-element.44), channel_id=1, source_target_pairs={{0,2},{1,67},{2,64},{3,1},{4,6},{5,71},{6,68},{7,5},{8,10},{9,75},... | collective-permute-start | bytes 1499144 | tf_op jit(solution)/shard_map/ppermute | solution.py:32
  19.8 14.1 %collective-permute-start.6 = (bf16[32,7808]{1,0:T(8,128)(2,1)S(1)}, bf16[32,7808]{1,0:T(8,128)(2,1)S(1)}, u32[]{:S(2)}, u32[]{:S(2)}) collective-permute-start(bf16[32,7808]{1,0:T(8,128)(2,1)S(1)} %get-tuple-element.43), channel_id=1, source_target_pairs={{0,66},{1,3},{2,0},{3,65},{4,70},{5,7},{6,4},{7,69},{8,74},{9,11},... | collective-permute-start | bytes 1499144 | tf_op jit(solution)/shard_map/ppermute | solution.py:32
  24.2 12.4 %collective-permute-start.10 = (bf16[30,5,16,128]{3,2,1,0:T(8,128)(2,1)S(1)}, bf16[30,5,16,128]{3,2,1,0:T(8,128)(2,1)S(1)}, u32[]{:S(2)}, u32[]{:S(2)}) collective-permute-start(bf16[30,5,16,128]{3,2,1,0:T(8,128)(2,1)S(1)} %get-tuple-element.29.own_a), channel_id=1, source_target_pairs={{0,4},{1,17},{2,6},{3,19},{4,8},{5,21},{6,10},{7,23},{8,12},{9,25}... | collective-permute-start | bytes 1843208 | tf_op jit(solution)/shard_map/ppermute | solution.py:32
  25.6 12.1 %collective-permute-start.13 = (bf16[31,5,16,128]{3,2,1,0:T(8,128)(2,1)S(1)}, bf16[31,5,16,128]{3,2,1,0:T(8,128)(2,1)S(1)}, u32[]{:S(2)}, u32[]{:S(2)}) collective-permute-start(bf16[31,5,16,128]{3,2,1,0:T(8,128)(2,1)S(1)} %get-tuple-element.30.own_b), channel_id=1, source_target_pairs={{0,12},{1,49},{2,14},{3,51},{4,0},{5,53},{6,2},{7,55},{8,4},{9,57}... | collective-permute-start | bytes 1904648 | tf_op jit(solution)/shard_map/ppermute | solution.py:32
  34.0 6.9 %collective-permute-start.7 = (bf16[64,7808]{1,0:T(8,128)(2,1)S(1)}, bf16[64,7808]{1,0:T(8,128)(2,1)S(1)}, u32[]{:S(2)}, u32[]{:S(2)}) collective-permute-start(bf16[64,7808]{1,0:T(8,128)(2,1)S(1)} %coadd.1.mine), channel_id=1, source_target_pairs={{0,1},{1,0},{2,3},{3,2},{4,5},{5,4},{6,7},{7,6},{8,9},{9,8},{10,11... | collective-permute-start | bytes 2998280 | tf_op jit(solution)/shard_map/ppermute | solution.py:32
  34.0 10.7 %collective-permute-start.11 = (bf16[31,5,16,128]{3,2,1,0:T(8,128)(2,1)S(1)}, bf16[31,5,16,128]{3,2,1,0:T(8,128)(2,1)S(1)}, u32[]{:S(2)}, u32[]{:S(2)}) collective-permute-start(bf16[31,5,16,128]{3,2,1,0:T(8,128)(2,1)S(1)} %get-tuple-element.30.own_b), channel_id=1, source_target_pairs={{0,4},{1,17},{2,6},{3,19},{4,8},{5,21},{6,10},{7,23},{8,12},{9,25}... | collective-permute-start | bytes 1904648 | tf_op jit(solution)/shard_map/ppermute | solution.py:32
  34.7 9.6 %collective-permute-start.12 = (bf16[30,5,16,128]{3,2,1,0:T(8,128)(2,1)S(1)}, bf16[30,5,16,128]{3,2,1,0:T(8,128)(2,1)S(1)}, u32[]{:S(2)}, u32[]{:S(2)}) collective-permute-start(bf16[30,5,16,128]{3,2,1,0:T(8,128)(2,1)S(1)} %get-tuple-element.29.own_a), channel_id=1, source_target_pairs={{0,12},{1,49},{2,14},{3,51},{4,0},{5,53},{6,2},{7,55},{8,4},{9,57}... | collective-permute-start | bytes 1843208 | tf_op jit(solution)/shard_map/ppermute | solution.py:32
  36.6 2.6 %collective-permute-start.8 = (bf16[32,7808]{1,0:T(8,128)(2,1)S(1)}, bf16[32,7808]{1,0:T(8,128)(2,1)S(1)}, u32[]{:S(2)}, u32[]{:S(2)}) collective-permute-start(bf16[32,7808]{1,0:T(8,128)(2,1)S(1)} %collective-permute-done.5.direct_a), channel_id=1, source_target_pairs={{0,1},{1,0},{2,3},{3,2},{4,5},{5,4},{6,7},{7,6},{8,9},{9,8},{10,11... | collective-permute-start | bytes 1499144 | tf_op jit(solution)/shard_map/ppermute | solution.py:32
  37.7 2.9 %collective-permute-start.9 = (bf16[32,7808]{1,0:T(8,128)(2,1)S(1)}, bf16[32,7808]{1,0:T(8,128)(2,1)S(1)}, u32[]{:S(2)}, u32[]{:S(2)}) collective-permute-start(bf16[32,7808]{1,0:T(8,128)(2,1)S(1)} %collective-permute-done.6.direct_b), channel_id=1, source_target_pairs={{0,1},{1,0},{2,3},{3,2},{4,5},{5,4},{6,7},{7,6},{8,9},{9,8},{10,11... | collective-permute-start | bytes 1499144 | tf_op jit(solution)/shard_map/ppermute | solution.py:32
  39.2 11.6 %collective-permute-start.14 = (bf16[31,5,16,128]{3,2,1,0:T(8,128)(2,1)S(1)}, bf16[31,5,16,128]{3,2,1,0:T(8,128)(2,1)S(1)}, u32[]{:S(2)}, u32[]{:S(2)}) collective-permute-start(bf16[31,5,16,128]{3,2,1,0:T(8,128)(2,1)S(1)} %collective-permute-done.13.down_b), channel_id=1, source_target_pairs={{0,12},{1,49},{2,14},{3,51},{4,0},{5,53},{6,2},{7,55},{8,4},{9,57}... | collective-permute-start | bytes 1904648 | tf_op jit(solution)/shard_map/ppermute | solution.py:32
  40.6 11.6 %collective-permute-start.15 = (bf16[30,5,16,128]{3,2,1,0:T(8,128)(2,1)S(1)}, bf16[30,5,16,128]{3,2,1,0:T(8,128)(2,1)S(1)}, u32[]{:S(2)}, u32[]{:S(2)}) collective-permute-start(bf16[30,5,16,128]{3,2,1,0:T(8,128)(2,1)S(1)} %collective-permute-done.10.up_a), channel_id=1, source_target_pairs={{0,4},{1,17},{2,6},{3,19},{4,8},{5,21},{6,10},{7,23},{8,12},{9,25}... | collective-permute-start | bytes 1843208 | tf_op jit(solution)/shard_map/ppermute | solution.py:32
  52.2 5.6 %copy-start.3 = (s32[32]{0:T(128)S(1)}, s32[32]{0:T(128)}, u32[]{:S(2)}) copy-start(s32[32]{0:T(128)} %param.13) | copy-start | bytes 388
  52.2 5.7 %copy-start.2 = (s32[3]{0:T(128)S(1)}, s32[3]{0:T(128)}, u32[]{:S(2)}) copy-start(s32[3]{0:T(128)} %counts.1) | copy-start | bytes 40
  53.7 4.9 %collective-permute-start.16 = (f32[4,3,8,128]{3,2,1,0:T(8,128)S(1)}, f32[4,3,8,128]{3,2,1,0:T(8,128)S(1)}, u32[]{:S(2)}, u32[]{:S(2)}) collective-permute-start(f32[4,3,8,128]{3,2,1,0:T(8,128)S(1)} %get-tuple-element.37), channel_id=1, source_target_pairs={{0,1},{1,0},{2,3},{3,2},{4,5},{5,4},{6,7},{7,6},{8,9},{9,8},{10,11... | collective-permute-start | bytes 147464 | tf_op jit(solution)/shard_map/ppermute | solution.py:32
  55.5 4.2 %collective-permute-start.17 = (f32[4,3,8,128]{3,2,1,0:T(8,128)S(1)}, f32[4,3,8,128]{3,2,1,0:T(8,128)S(1)}, u32[]{:S(2)}, u32[]{:S(2)}) collective-permute-start(f32[4,3,8,128]{3,2,1,0:T(8,128)S(1)} %get-tuple-element.38), channel_id=1, source_target_pairs={{0,66},{1,3},{2,0},{3,65},{4,70},{5,7},{6,4},{7,69},{8,74},{9,11},... | collective-permute-start | bytes 147464 | tf_op jit(solution)/shard_map/ppermute | solution.py:32
  55.7 4.7 %collective-permute-start.18 = (f32[4,3,8,128]{3,2,1,0:T(8,128)S(1)}, f32[4,3,8,128]{3,2,1,0:T(8,128)S(1)}, u32[]{:S(2)}, u32[]{:S(2)}) collective-permute-start(f32[4,3,8,128]{3,2,1,0:T(8,128)S(1)} %get-tuple-element.39), channel_id=1, source_target_pairs={{0,3},{1,66},{2,65},{3,0},{4,7},{5,70},{6,69},{7,4},{8,11},{9,74},... | collective-permute-start | bytes 147464 | tf_op jit(solution)/shard_map/ppermute | solution.py:32

commit v8 on v7

--- a/solution.py
+++ b/solution.py
@@ -105,7 +105,7 @@
         coadd[:, lanes] = jnp.dot(select, spectra, preferred_element_type=jnp.float32).astype(jnp.bfloat16)
 
 
-def join_kernel(own, up, down, far, *halves):
+def join_kernel(own, far, up, down, *halves):
     side = SLICES * 16
     row = lax.broadcasted_iota(jnp.int32, (side, side), 0)
     col = lax.broadcasted_iota(jnp.int32, (side, side), 1)
@@ -348,7 +348,8 @@
     over = send(late, core=1)
     swapped = [send(v, core=1) for v in direct]
 
-    near = [pair] + [send(pair, along=0, step=s) for s in (1, -1, 2)]
+    near = [send(pair, along=0, step=s) for s in (2, 1, -1)]
+    near = [pair] + near
 
     near[0], mine = lax.optimization_barrier((near[0], mine))
     cut = pixels // 256

time: 61.6 us -> 62.3 us (1.011)
  waiting for transfers between devices: 14.6 us -> 16.1 us
  starting transfers between devices: 26.1 us -> 25.3 us
    ppermute x19, waiting for transfers between devices: 14.6 us -> 16.1 us  [send(): return lax.ppermute(value, AXES, [(d, moved(d, **how)) for d in range(128)])]
    ppermute x19, starting transfers between devices: 26.1 us -> 25.3 us  [send(): return lax.ppermute(value, AXES, [(d, moved(d, **how)) for d in range(128)])]
  transfers between devices with their start and end apart: 19 -> 19, of which waited for: 10 -> 11; matrix products, arithmetic and copies ran while one was open for 0% -> 0% of each run, Pallas kernels for 25% -> 25%
where the time goes in v8:
time: 62.3 us; the launch traced here: 62.1 us
  starting transfers between devices  25.3 us (41%)
  Pallas kernels  18.7 us (30%)
  waiting for transfers between devices  16.1 us (26%)
  local copies, waits for them, and re-layouts  1.23 us (2%)
  between operations  0.79 us (1%)
    ppermute x19, starting transfers between devices, send(): return lax.ppermute(value, AXES, [(d, moved(d, **how)) for d in range(128)])  25.3 us
    ppermute x19, waiting for transfers between devices, send(): return lax.ppermute(value, AXES, [(d, moved(d, **how)) for d in range(128)])  16.1 us
    pallas_call x3, Pallas kernels, fit(): pl.pallas_call(kernel, out_shape=shapes, in_specs=[smem if v is place els...  10.1 us
    pallas_call x1, Pallas kernels, body(): pl.pallas_call(weight_kernel, out_shape=(jax.ShapeDtypeStruct((count, pix...  3.08 us
    pallas_call x1, Pallas kernels, body(): pl.pallas_call(half_fit_kernel, out_shape=jax.ShapeDtypeStruct((1, ROWS,...  1.37 us
    pallas_call x1, Pallas kernels, body(): pl.pallas_call(coadd_kernel, out_shape=jax.ShapeDtypeStruct((64, pixels),...  1.29 us
  transfers between devices with their start and end apart: 19, of which 11 were waited for; matrix products, arithmetic and copies ran while one was open for 0% of the time, Pallas kernels for 25%

profile of v8, /device:TPU:1, one launch (start us, length us, event | category | flops | bytes accessed | tf_op | source)
XLA Modules:
  0.0 62.1 jit_solution(9621846651042152437)
XLA Ops:
  0.7 0.1 stack.23.place
  0.8 1.0 %copy-done = bf16[2,10,7808]{2,0,1:T(2,128)(2,1)S(1)} copy-done((bf16[2,10,7808]{2,0,1:T(2,128)(2,1)S(1)}, bf16[2,10,7808]{2,0,1:T(2,128)(2,1)}, u32[]{:S(2)}) %copy-start) | copy-done | bytes 312344
  1.7 0.7 %prep.1 = bf16[1,10,16,512]{3,2,1,0:T(8,128)(2,1)S(1)} custom-call(s32[5]{0:T(128)S(1)} %stack.23.place, bf16[10,2,7808]{2,1,0:T(2,128)(2,1)S(1)} %bitcast.9), custom_call_target="tpu_custom_call" | custom-call | flops 700000000 | bytes 2100000 | tf_op jit(solution)/shard_map/prep/pallas_call | solution.py:305
  2.4 3.7 %collective-permute-start = (bf16[1,10,16,512]{3,2,1,0:T(8,128)(2,1)S(1)}, bf16[1,10,16,512]{3,2,1,0:T(8,128)(2,1)S(1)}, u32[]{:S(2)}, u32[]{:S(2)}) collective-permute-start(bf16[1,10,16,512]{3,2,1,0:T(8,128)(2,1)S(1)} %prep.1), channel_id=1, source_target_pairs={{0,64},{1,65},{2,66},{3,67},{4,68},{5,69},{6,70},{7,71},{8,72},{9,... | collective-permute-start | bytes 491528 | tf_op jit(solution)/shard_map/ppermute | solution.py:32
  6.0 3.1 %weight.1 = (bf16[96,7808]{1,0:T(8,128)(2,1)S(1)}, bf16[112,7808]{1,0:T(8,128)(2,1)S(1)}) custom-call(s32[5]{0:T(128)S(1)} %stack.23.place, bf16[96,7808]{1,0:T(8,128)(2,1)} %flux.1, bf16[96,7808]{1,0:T(8,128)(2,1)} %ivar.1, s32[61,96]{1,0:T(8,128)} %bitcast.12, s32[1,96]{1,0:T(1,128)} %bitcast.10), custom_call_target="tpu_custom_call" | custom-call | flops 2300000000 | bytes 6899999 | tf_op jit(solution)/shard_map/weight/pallas_call | solution.py:321
  9.1 0.4 collective-permute-done
  9.5 1.7 %collective-permute-start.1 = (bf16[112,7808]{1,0:T(8,128)(2,1)S(1)}, bf16[112,7808]{1,0:T(8,128)(2,1)S(1)}, u32[]{:S(2)}, u32[]{:S(2)}) collective-permute-start(bf16[112,7808]{1,0:T(8,128)(2,1)S(1)} %get-tuple-element.27), channel_id=1, source_target_pairs={{0,1},{1,0},{2,3},{3,2},{4,5},{5,4},{6,7},{7,6},{8,9},{9,8},{10,11... | collective-permute-start | bytes 5246984 | tf_op jit(solution)/shard_map/ppermute | solution.py:32
  11.2 3.2 %collective-permute-start.2 = (bf16[2,10,16,512]{3,2,1,0:T(8,128)(2,1)S(1)}, bf16[2,10,16,512]{3,2,1,0:T(8,128)(2,1)S(1)}, u32[]{:S(2)}, u32[]{:S(2)}) collective-permute-start(bf16[2,10,16,512]{3,2,1,0:T(8,128)(2,1)S(1)} %pad_maximum_fusion.own), channel_id=1, source_target_pairs={{0,32},{1,9},{2,34},{3,11},{4,36},{5,13},{6,38},{7,15},{8,40},{9,1... | collective-permute-start | bytes 983048 | tf_op jit(solution)/shard_map/ppermute | solution.py:32
  14.4 0.4 collective-permute-start.3
  14.8 2.3 %collective-permute-start.4 = (bf16[2,10,16,512]{3,2,1,0:T(8,128)(2,1)S(1)}, bf16[2,10,16,512]{3,2,1,0:T(8,128)(2,1)S(1)}, u32[]{:S(2)}, u32[]{:S(2)}) collective-permute-start(bf16[2,10,16,512]{3,2,1,0:T(8,128)(2,1)S(1)} %pad_maximum_fusion.own), channel_id=1, source_target_pairs={{0,48},{1,13},{2,50},{3,15},{4,52},{5,1},{6,54},{7,3},{8,56},{9,5}... | collective-permute-start | bytes 983048 | tf_op jit(solution)/shard_map/ppermute | solution.py:32
  17.1 1.3 %coadd.1.mine = bf16[64,7808]{1,0:T(8,128)(2,1)S(1)} custom-call(s32[5]{0:T(128)S(1)} %stack.23.place, s32[1,96]{1,0:T(1,128)S(1)} %bitcast.11, bf16[96,7808]{1,0:T(8,128)(2,1)S(1)} %get-tuple-element.25.own, bf16[112,7808]{1,0:T(8,128)(2,1)S(1)} %collective-permute-done.1.other), custom_call_target="tpu_custom_call" | custom-call | flops 2400000000 | bytes 7200000 | tf_op jit(solution)/shard_map/coadd/pallas_call | solution.py:337
  18.4 0.1 fusion
  18.5 2.5 %collective-permute-start.5 = (bf16[32,7808]{1,0:T(8,128)(2,1)S(1)}, bf16[32,7808]{1,0:T(8,128)(2,1)S(1)}, u32[]{:S(2)}, u32[]{:S(2)}) collective-permute-start(bf16[32,7808]{1,0:T(8,128)(2,1)S(1)} %get-tuple-element.44), channel_id=1, source_target_pairs={{0,2},{1,67},{2,64},{3,1},{4,6},{5,71},{6,68},{7,5},{8,10},{9,75},... | collective-permute-start | bytes 1499144 | tf_op jit(solution)/shard_map/ppermute | solution.py:32
  21.0 0.0 collective-permute-done.2.far
  21.0 1.7 %collective-permute-done.3.up = bf16[2,10,16,512]{3,2,1,0:T(8,128)(2,1)S(1)} collective-permute-done((bf16[2,10,16,512]{3,2,1,0:T(8,128)(2,1)S(1)}, bf16[2,10,16,512]{3,2,1,0:T(8,128)(2,1)S(1)}, u32[]{:S(2)}, u32[]{:S(2)}) %collective-permute-start.3) | collective-permute-done | bytes 327712 | tf_op jit(solution)/shard_map/ppermute | solution.py:32
  22.7 0.4 collective-permute-done.4.down
  23.1 0.5 join.1
  23.6 1.7 %collective-permute-start.10 = (bf16[30,5,16,128]{3,2,1,0:T(8,128)(2,1)S(1)}, bf16[30,5,16,128]{3,2,1,0:T(8,128)(2,1)S(1)}, u32[]{:S(2)}, u32[]{:S(2)}) collective-permute-start(bf16[30,5,16,128]{3,2,1,0:T(8,128)(2,1)S(1)} %get-tuple-element.29.own_a), channel_id=1, source_target_pairs={{0,4},{1,17},{2,6},{3,19},{4,8},{5,21},{6,10},{7,23},{8,12},{9,25}... | collective-permute-start | bytes 1843208 | tf_op jit(solution)/shard_map/ppermute | solution.py:32
  25.3 2.2 %collective-permute-start.13 = (bf16[31,5,16,128]{3,2,1,0:T(8,128)(2,1)S(1)}, bf16[31,5,16,128]{3,2,1,0:T(8,128)(2,1)S(1)}, u32[]{:S(2)}, u32[]{:S(2)}) collective-permute-start(bf16[31,5,16,128]{3,2,1,0:T(8,128)(2,1)S(1)} %get-tuple-element.30.own_b), channel_id=1, source_target_pairs={{0,12},{1,49},{2,14},{3,51},{4,0},{5,53},{6,2},{7,55},{8,4},{9,57}... | collective-permute-start | bytes 1904648 | tf_op jit(solution)/shard_map/ppermute | solution.py:32
  27.5 2.2 %collective-permute-done.5.direct_a = bf16[32,7808]{1,0:T(8,128)(2,1)S(1)} collective-permute-done((bf16[32,7808]{1,0:T(8,128)(2,1)S(1)}, bf16[32,7808]{1,0:T(8,128)(2,1)S(1)}, u32[]{:S(2)}, u32[]{:S(2)}) %collective-permute-start.5) | collective-permute-done | bytes 499744 | tf_op jit(solution)/shard_map/ppermute | solution.py:32
  29.7 5.4 %collective-permute-done.6.direct_b = bf16[32,7808]{1,0:T(8,128)(2,1)S(1)} collective-permute-done((bf16[32,7808]{1,0:T(8,128)(2,1)S(1)}, bf16[32,7808]{1,0:T(8,128)(2,1)S(1)}, u32[]{:S(2)}, u32[]{:S(2)}) %collective-permute-start.6) | collective-permute-done | bytes 499744 | tf_op jit(solution)/shard_map/ppermute | solution.py:32
  35.2 0.0 collective-permute-start.7
  35.2 0.0 collective-permute-start.11
  35.2 2.7 %collective-permute-start.12 = (bf16[30,5,16,128]{3,2,1,0:T(8,128)(2,1)S(1)}, bf16[30,5,16,128]{3,2,1,0:T(8,128)(2,1)S(1)}, u32[]{:S(2)}, u32[]{:S(2)}) collective-permute-start(bf16[30,5,16,128]{3,2,1,0:T(8,128)(2,1)S(1)} %get-tuple-element.29.own_a), channel_id=1, source_target_pairs={{0,12},{1,49},{2,14},{3,51},{4,0},{5,53},{6,2},{7,55},{8,4},{9,57}... | collective-permute-start | bytes 1843208 | tf_op jit(solution)/shard_map/ppermute | solution.py:32
  37.9 1.1 %collective-permute-start.8 = (bf16[32,7808]{1,0:T(8,128)(2,1)S(1)}, bf16[32,7808]{1,0:T(8,128)(2,1)S(1)}, u32[]{:S(2)}, u32[]{:S(2)}) collective-permute-start(bf16[32,7808]{1,0:T(8,128)(2,1)S(1)} %collective-permute-done.5.direct_a), channel_id=1, source_target_pairs={{0,1},{1,0},{2,3},{3,2},{4,5},{5,4},{6,7},{7,6},{8,9},{9,8},{10,11... | collective-permute-start | bytes 1499144 | tf_op jit(solution)/shard_map/ppermute | solution.py:32
  38.9 0.0 collective-permute-done.13.down_b
  38.9 0.1 collective-permute-start.9
  39.0 1.4 %collective-permute-done.8.swapped_a = bf16[32,7808]{1,0:T(8,128)(2,1)S(1)} collective-permute-done((bf16[32,7808]{1,0:T(8,128)(2,1)S(1)}, bf16[32,7808]{1,0:T(8,128)(2,1)S(1)}, u32[]{:S(2)}, u32[]{:S(2)}) %collective-permute-start.8) | collective-permute-done | bytes 499744 | tf_op jit(solution)/shard_map/ppermute | solution.py:32
  40.4 0.5 collective-permute-start.14
  40.9 0.2 collective-permute-done.9.swapped_b
  41.1 0.8 %collective-permute-start.15 = (bf16[30,5,16,128]{3,2,1,0:T(8,128)(2,1)S(1)}, bf16[30,5,16,128]{3,2,1,0:T(8,128)(2,1)S(1)}, u32[]{:S(2)}, u32[]{:S(2)}) collective-permute-start(bf16[30,5,16,128]{3,2,1,0:T(8,128)(2,1)S(1)} %collective-permute-done.10.up_a), channel_id=1, source_target_pairs={{0,4},{1,17},{2,6},{3,19},{4,8},{5,21},{6,10},{7,23},{8,12},{9,25}... | collective-permute-start | bytes 1843208 | tf_op jit(solution)/shard_map/ppermute | solution.py:32
  41.9 0.0 collective-permute-done.7.over
  41.9 3.4 %own_fit.1 = (f32[4,1,3,8,128]{4,3,2,1,0:T(8,128)S(1)}, bf16[7808,128]{1,0:T(8,128)(2,1)S(1)}, bf16[7808,128]{1,0:T(8,128)(2,1)S(1)}) custom-call(s32[5]{0:T(128)S(1)} %stack.23.place, bf16[30,5,16,128]{3,2,1,0:T(8,128)(2,1)S(1)} %get-tuple-element.29.own_a, bf16[31,5,16,128]{3,2,1,0:T(8,128)(2,1)S(1)} %get-tuple-element.30.own_b, ...), custom_call_target="tpu_custom_call" | custom-call | tf_op jit(solution)/shard_map/own_fit/pallas_call | solution.py:370
  45.3 0.0 collective-permute-done.12.down_a
  45.3 0.6 %collective-permute-done.11.up_b = bf16[31,5,16,128]{3,2,1,0:T(8,128)(2,1)S(1)} collective-permute-done((bf16[31,5,16,128]{3,2,1,0:T(8,128)(2,1)S(1)}, bf16[31,5,16,128]{3,2,1,0:T(8,128)(2,1)S(1)}, u32[]{:S(2)}, u32[]{:S(2)}) %collective-permute-start.11) | collective-permute-done | bytes 634912 | tf_op jit(solution)/shard_map/ppermute | solution.py:32
  45.9 5.2 %near_fit.1._.near = f32[4,2,3,8,128]{4,3,2,1,0:T(8,128)S(1)} custom-call(bf16[30,5,16,128]{3,2,1,0:T(8,128)(2,1)S(1)} %collective-permute-done.10.up_a, bf16[31,5,16,128]{3,2,1,0:T(8,128)(2,1)S(1)} %collective-permute-done.11.up_b, bf16[30,5,16,128]{3,2,1,0:T(8,128)(2,1)S(1)} %collective-permute-done.12.down_a, ...), custom_call_target="tpu_custom_call" | custom-call | flops 6000000000 | bytes 18000000 | tf_op jit(solution)/shard_map/near_fit/pallas_call | solution.py:370
  51.1 0.7 %collective-permute-done.14.far_b = bf16[31,5,16,128]{3,2,1,0:T(8,128)(2,1)S(1)} collective-permute-done((bf16[31,5,16,128]{3,2,1,0:T(8,128)(2,1)S(1)}, bf16[31,5,16,128]{3,2,1,0:T(8,128)(2,1)S(1)}, u32[]{:S(2)}, u32[]{:S(2)}) %collective-permute-start.14) | collective-permute-done | bytes 634912 | tf_op jit(solution)/shard_map/ppermute | solution.py:32
  51.7 1.4 %half_fit.1.half = f32[1,560,128]{2,1,0:T(8,128)S(1)} custom-call(f32[4,2,3,8,128]{4,3,2,1,0:T(8,128)S(1)} %near_fit.1._.near, bf16[31,5,16,128]{3,2,1,0:T(8,128)(2,1)S(1)} %collective-permute-done.14.far_b, bf16[7808,128]{1,0:T(8,128)(2,1)S(1)} %get-tuple-element.34.ivar, bf16[7808,128]{1,0:T(8,128)(2,1)S(1)} %get-tuple-element.35.wflux), custom_call_target="tpu_custom_call" | custom-call | tf_op jit(solution)/shard_map/half_fit/pallas_call | solution.py:390
  53.1 0.0 copy-start.3
  53.1 0.0 copy-start.2
  53.2 1.5 %far_fit.1 = (f32[4,3,8,128]{3,2,1,0:T(8,128)S(1)}, f32[4,3,8,128]{3,2,1,0:T(8,128)S(1)}, f32[4,3,8,128]{3,2,1,0:T(8,128)S(1)}, f32[4,3,8,128]{3,2,1,0:T(8,128)S(1)}) custom-call(f32[4,1,3,8,128]{4,3,2,1,0:T(8,128)S(1)} %get-tuple-element.33.own, f32[4,2,3,8,128]{4,3,2,1,0:T(8,128)S(1)} %near_fit.1._.near, f32[1,560,128]{2,1,0:T(8,128)S(1)} %half_fit.1.half, ...), custom_call_target="tpu_custom_call" | custom-call | flops 3000000000 | bytes 9000000 | tf_op jit(solution)/shard_map/far_fit/pallas_call | solution.py:370
  54.7 1.7 %collective-permute-start.16 = (f32[4,3,8,128]{3,2,1,0:T(8,128)S(1)}, f32[4,3,8,128]{3,2,1,0:T(8,128)S(1)}, u32[]{:S(2)}, u32[]{:S(2)}) collective-permute-start(f32[4,3,8,128]{3,2,1,0:T(8,128)S(1)} %get-tuple-element.37), channel_id=1, source_target_pairs={{0,1},{1,0},{2,3},{3,2},{4,5},{5,4},{6,7},{7,6},{8,9},{9,8},{10,11... | collective-permute-start | bytes 147464 | tf_op jit(solution)/shard_map/ppermute | solution.py:32
  56.4 0.8 %collective-permute-start.18 = (f32[4,3,8,128]{3,2,1,0:T(8,128)S(1)}, f32[4,3,8,128]{3,2,1,0:T(8,128)S(1)}, u32[]{:S(2)}, u32[]{:S(2)}) collective-permute-start(f32[4,3,8,128]{3,2,1,0:T(8,128)S(1)} %get-tuple-element.39), channel_id=1, source_target_pairs={{0,3},{1,66},{2,65},{3,0},{4,7},{5,70},{6,69},{7,4},{8,11},{9,74},... | collective-permute-start | bytes 147464 | tf_op jit(solution)/shard_map/ppermute | solution.py:32
  57.3 0.1 reshape_tile.3.classes
  57.3 0.7 %order.1 = (bf16[128,128]{1,0:T(8,128)(2,1)S(1)}, f32[128,128]{1,0:T(8,128)S(1)}) custom-call(s32[5]{0:T(128)S(1)} %stack.23.place, s32[3]{0:T(128)S(1)} %copy-done.2, s32[1,128]{1,0:T(1,128)S(1)} %reshape_tile.3.classes), custom_call_target="tpu_custom_call" | custom-call | tf_op jit(solution)/shard_map/order/pallas_call | solution.py:401
  58.1 2.5 %collective-permute-done.17.part_2 = f32[4,3,8,128]{3,2,1,0:T(8,128)S(1)} collective-permute-done((f32[4,3,8,128]{3,2,1,0:T(8,128)S(1)}, f32[4,3,8,128]{3,2,1,0:T(8,128)S(1)}, u32[]{:S(2)}, u32[]{:S(2)}) %collective-permute-start.17) | collective-permute-done | bytes 49184 | tf_op jit(solution)/shard_map/ppermute | solution.py:32
  60.6 0.6 collective-permute-done.18.part_3
  61.2 1.0 %final.1 = (f32[10,32,128]{2,1,0:T(8,128)}, f32[32,128]{1,0:T(8,128)}, f32[1,32]{1,0:T(1,128)}) custom-call(bf16[128,128]{1,0:T(8,128)(2,1)S(1)} %get-tuple-element.23.to_lane, f32[128,128]{1,0:T(8,128)S(1)} %get-tuple-element.24.drop, f32[4,3,8,128]{3,2,1,0:T(8,128)S(1)} %get-tuple-element.36.part_0, f32[4,3,8,128]{3,2,1,0:T(8,128)S(1)} %collective-permute-done.16.part_1, ...), custom_call_target="tpu_custom_call" | custom-call | flops 2000000000 | bytes 6000000 | tf_op jit(solution)/shard_map/final/pallas_call | solution.py:416
  (13 shorter events, 0.1 us)
Async XLA Ops:
  0.8 1.0 %copy-start = (bf16[2,10,7808]{2,0,1:T(2,128)(2,1)S(1)}, bf16[2,10,7808]{2,0,1:T(2,128)(2,1)}, u32[]{:S(2)}) copy-start(bf16[2,10,7808]{2,0,1:T(2,128)(2,1)} %param.11) | copy-start | bytes 936964
  2.4 7.1 %collective-permute-start = (bf16[1,10,16,512]{3,2,1,0:T(8,128)(2,1)S(1)}, bf16[1,10,16,512]{3,2,1,0:T(8,128)(2,1)S(1)}, u32[]{:S(2)}, u32[]{:S(2)}) collective-permute-start(bf16[1,10,16,512]{3,2,1,0:T(8,128)(2,1)S(1)} %prep.1), channel_id=1, source_target_pairs={{0,64},{1,65},{2,66},{3,67},{4,68},{5,69},{6,70},{7,71},{8,72},{9,... | collective-permute-start | bytes 491528 | tf_op jit(solution)/shard_map/ppermute | solution.py:32
  6.0 11.1 %copy-start.1 = (s32[96]{0:T(128)S(1)}, s32[96]{0:T(128)}, u32[]{:S(2)}) copy-start(s32[96]{0:T(128)} %param.10) | copy-start | bytes 1156
  9.5 7.6 %collective-permute-start.1 = (bf16[112,7808]{1,0:T(8,128)(2,1)S(1)}, bf16[112,7808]{1,0:T(8,128)(2,1)S(1)}, u32[]{:S(2)}, u32[]{:S(2)}) collective-permute-start(bf16[112,7808]{1,0:T(8,128)(2,1)S(1)} %get-tuple-element.27), channel_id=1, source_target_pairs={{0,1},{1,0},{2,3},{3,2},{4,5},{5,4},{6,7},{7,6},{8,9},{9,8},{10,11... | collective-permute-start | bytes 5246984 | tf_op jit(solution)/shard_map/ppermute | solution.py:32
  11.2 9.8 %collective-permute-start.2 = (bf16[2,10,16,512]{3,2,1,0:T(8,128)(2,1)S(1)}, bf16[2,10,16,512]{3,2,1,0:T(8,128)(2,1)S(1)}, u32[]{:S(2)}, u32[]{:S(2)}) collective-permute-start(bf16[2,10,16,512]{3,2,1,0:T(8,128)(2,1)S(1)} %pad_maximum_fusion.own), channel_id=1, source_target_pairs={{0,32},{1,9},{2,34},{3,11},{4,36},{5,13},{6,38},{7,15},{8,40},{9,1... | collective-permute-start | bytes 983048 | tf_op jit(solution)/shard_map/ppermute | solution.py:32
  14.4 8.3 %collective-permute-start.3 = (bf16[2,10,16,512]{3,2,1,0:T(8,128)(2,1)S(1)}, bf16[2,10,16,512]{3,2,1,0:T(8,128)(2,1)S(1)}, u32[]{:S(2)}, u32[]{:S(2)}) collective-permute-start(bf16[2,10,16,512]{3,2,1,0:T(8,128)(2,1)S(1)} %pad_maximum_fusion.own), channel_id=1, source_target_pairs={{0,16},{1,5},{2,18},{3,7},{4,20},{5,9},{6,22},{7,11},{8,24},{9,13}... | collective-permute-start | bytes 983048 | tf_op jit(solution)/shard_map/ppermute | solution.py:32
  14.8 8.3 %collective-permute-start.4 = (bf16[2,10,16,512]{3,2,1,0:T(8,128)(2,1)S(1)}, bf16[2,10,16,512]{3,2,1,0:T(8,128)(2,1)S(1)}, u32[]{:S(2)}, u32[]{:S(2)}) collective-permute-start(bf16[2,10,16,512]{3,2,1,0:T(8,128)(2,1)S(1)} %pad_maximum_fusion.own), channel_id=1, source_target_pairs={{0,48},{1,13},{2,50},{3,15},{4,52},{5,1},{6,54},{7,3},{8,56},{9,5}... | collective-permute-start | bytes 983048 | tf_op jit(solution)/shard_map/ppermute | solution.py:32
  18.5 11.2 %collective-permute-start.5 = (bf16[32,7808]{1,0:T(8,128)(2,1)S(1)}, bf16[32,7808]{1,0:T(8,128)(2,1)S(1)}, u32[]{:S(2)}, u32[]{:S(2)}) collective-permute-start(bf16[32,7808]{1,0:T(8,128)(2,1)S(1)} %get-tuple-element.44), channel_id=1, source_target_pairs={{0,2},{1,67},{2,64},{3,1},{4,6},{5,71},{6,68},{7,5},{8,10},{9,75},... | collective-permute-start | bytes 1499144 | tf_op jit(solution)/shard_map/ppermute | solution.py:32
  21.0 14.1 %collective-permute-start.6 = (bf16[32,7808]{1,0:T(8,128)(2,1)S(1)}, bf16[32,7808]{1,0:T(8,128)(2,1)S(1)}, u32[]{:S(2)}, u32[]{:S(2)}) collective-permute-start(bf16[32,7808]{1,0:T(8,128)(2,1)S(1)} %get-tuple-element.43), channel_id=1, source_target_pairs={{0,66},{1,3},{2,0},{3,65},{4,70},{5,7},{6,4},{7,69},{8,74},{9,11},... | collective-permute-start | bytes 1499144 | tf_op jit(solution)/shard_map/ppermute | solution.py:32
  23.6 14.2 %collective-permute-start.10 = (bf16[30,5,16,128]{3,2,1,0:T(8,128)(2,1)S(1)}, bf16[30,5,16,128]{3,2,1,0:T(8,128)(2,1)S(1)}, u32[]{:S(2)}, u32[]{:S(2)}) collective-permute-start(bf16[30,5,16,128]{3,2,1,0:T(8,128)(2,1)S(1)} %get-tuple-element.29.own_a), channel_id=1, source_target_pairs={{0,4},{1,17},{2,6},{3,19},{4,8},{5,21},{6,10},{7,23},{8,12},{9,25}... | collective-permute-start | bytes 1843208 | tf_op jit(solution)/shard_map/ppermute | solution.py:32
  25.3 13.6 %collective-permute-start.13 = (bf16[31,5,16,128]{3,2,1,0:T(8,128)(2,1)S(1)}, bf16[31,5,16,128]{3,2,1,0:T(8,128)(2,1)S(1)}, u32[]{:S(2)}, u32[]{:S(2)}) collective-permute-start(bf16[31,5,16,128]{3,2,1,0:T(8,128)(2,1)S(1)} %get-tuple-element.30.own_b), channel_id=1, source_target_pairs={{0,12},{1,49},{2,14},{3,51},{4,0},{5,53},{6,2},{7,55},{8,4},{9,57}... | collective-permute-start | bytes 1904648 | tf_op jit(solution)/shard_map/ppermute | solution.py:32
  35.2 6.7 %collective-permute-start.7 = (bf16[64,7808]{1,0:T(8,128)(2,1)S(1)}, bf16[64,7808]{1,0:T(8,128)(2,1)S(1)}, u32[]{:S(2)}, u32[]{:S(2)}) collective-permute-start(bf16[64,7808]{1,0:T(8,128)(2,1)S(1)} %coadd.1.mine), channel_id=1, source_target_pairs={{0,1},{1,0},{2,3},{3,2},{4,5},{5,4},{6,7},{7,6},{8,9},{9,8},{10,11... | collective-permute-start | bytes 2998280 | tf_op jit(solution)/shard_map/ppermute | solution.py:32
  35.2 10.7 %collective-permute-start.11 = (bf16[31,5,16,128]{3,2,1,0:T(8,128)(2,1)S(1)}, bf16[31,5,16,128]{3,2,1,0:T(8,128)(2,1)S(1)}, u32[]{:S(2)}, u32[]{:S(2)}) collective-permute-start(bf16[31,5,16,128]{3,2,1,0:T(8,128)(2,1)S(1)} %get-tuple-element.30.own_b), channel_id=1, source_target_pairs={{0,4},{1,17},{2,6},{3,19},{4,8},{5,21},{6,10},{7,23},{8,12},{9,25}... | collective-permute-start | bytes 1904648 | tf_op jit(solution)/shard_map/ppermute | solution.py:32
  35.2 10.1 %collective-permute-start.12 = (bf16[30,5,16,128]{3,2,1,0:T(8,128)(2,1)S(1)}, bf16[30,5,16,128]{3,2,1,0:T(8,128)(2,1)S(1)}, u32[]{:S(2)}, u32[]{:S(2)}) collective-permute-start(bf16[30,5,16,128]{3,2,1,0:T(8,128)(2,1)S(1)} %get-tuple-element.29.own_a), channel_id=1, source_target_pairs={{0,12},{1,49},{2,14},{3,51},{4,0},{5,53},{6,2},{7,55},{8,4},{9,57}... | collective-permute-start | bytes 1843208 | tf_op jit(solution)/shard_map/ppermute | solution.py:32
  37.9 2.6 %collective-permute-start.8 = (bf16[32,7808]{1,0:T(8,128)(2,1)S(1)}, bf16[32,7808]{1,0:T(8,128)(2,1)S(1)}, u32[]{:S(2)}, u32[]{:S(2)}) collective-permute-start(bf16[32,7808]{1,0:T(8,128)(2,1)S(1)} %collective-permute-done.5.direct_a), channel_id=1, source_target_pairs={{0,1},{1,0},{2,3},{3,2},{4,5},{5,4},{6,7},{7,6},{8,9},{9,8},{10,11... | collective-permute-start | bytes 1499144 | tf_op jit(solution)/shard_map/ppermute | solution.py:32
  38.9 2.2 %collective-permute-start.9 = (bf16[32,7808]{1,0:T(8,128)(2,1)S(1)}, bf16[32,7808]{1,0:T(8,128)(2,1)S(1)}, u32[]{:S(2)}, u32[]{:S(2)}) collective-permute-start(bf16[32,7808]{1,0:T(8,128)(2,1)S(1)} %collective-permute-done.6.direct_b), channel_id=1, source_target_pairs={{0,1},{1,0},{2,3},{3,2},{4,5},{5,4},{6,7},{7,6},{8,9},{9,8},{10,11... | collective-permute-start | bytes 1499144 | tf_op jit(solution)/shard_map/ppermute | solution.py:32
  40.4 11.3 %collective-permute-start.14 = (bf16[31,5,16,128]{3,2,1,0:T(8,128)(2,1)S(1)}, bf16[31,5,16,128]{3,2,1,0:T(8,128)(2,1)S(1)}, u32[]{:S(2)}, u32[]{:S(2)}) collective-permute-start(bf16[31,5,16,128]{3,2,1,0:T(8,128)(2,1)S(1)} %collective-permute-done.13.down_b), channel_id=1, source_target_pairs={{0,12},{1,49},{2,14},{3,51},{4,0},{5,53},{6,2},{7,55},{8,4},{9,57}... | collective-permute-start | bytes 1904648 | tf_op jit(solution)/shard_map/ppermute | solution.py:32
  41.1 12.0 %collective-permute-start.15 = (bf16[30,5,16,128]{3,2,1,0:T(8,128)(2,1)S(1)}, bf16[30,5,16,128]{3,2,1,0:T(8,128)(2,1)S(1)}, u32[]{:S(2)}, u32[]{:S(2)}) collective-permute-start(bf16[30,5,16,128]{3,2,1,0:T(8,128)(2,1)S(1)} %collective-permute-done.10.up_a), channel_id=1, source_target_pairs={{0,4},{1,17},{2,6},{3,19},{4,8},{5,21},{6,10},{7,23},{8,12},{9,25}... | collective-permute-start | bytes 1843208 | tf_op jit(solution)/shard_map/ppermute | solution.py:32
  53.1 4.1 %copy-start.3 = (s32[32]{0:T(128)S(1)}, s32[32]{0:T(128)}, u32[]{:S(2)}) copy-start(s32[32]{0:T(128)} %param.13) | copy-start | bytes 388
  53.1 4.2 %copy-start.2 = (s32[3]{0:T(128)S(1)}, s32[3]{0:T(128)}, u32[]{:S(2)}) copy-start(s32[3]{0:T(128)} %counts.1) | copy-start | bytes 40
  54.7 3.4 %collective-permute-start.16 = (f32[4,3,8,128]{3,2,1,0:T(8,128)S(1)}, f32[4,3,8,128]{3,2,1,0:T(8,128)S(1)}, u32[]{:S(2)}, u32[]{:S(2)}) collective-permute-start(f32[4,3,8,128]{3,2,1,0:T(8,128)S(1)} %get-tuple-element.37), channel_id=1, source_target_pairs={{0,1},{1,0},{2,3},{3,2},{4,5},{5,4},{6,7},{7,6},{8,9},{9,8},{10,11... | collective-permute-start | bytes 147464 | tf_op jit(solution)/shard_map/ppermute | solution.py:32
  56.4 4.2 %collective-permute-start.17 = (f32[4,3,8,128]{3,2,1,0:T(8,128)S(1)}, f32[4,3,8,128]{3,2,1,0:T(8,128)S(1)}, u32[]{:S(2)}, u32[]{:S(2)}) collective-permute-start(f32[4,3,8,128]{3,2,1,0:T(8,128)S(1)} %get-tuple-element.38), channel_id=1, source_target_pairs={{0,66},{1,3},{2,0},{3,65},{4,70},{5,7},{6,4},{7,69},{8,74},{9,11},... | collective-permute-start | bytes 147464 | tf_op jit(solution)/shard_map/ppermute | solution.py:32
  56.4 4.8 %collective-permute-start.18 = (f32[4,3,8,128]{3,2,1,0:T(8,128)S(1)}, f32[4,3,8,128]{3,2,1,0:T(8,128)S(1)}, u32[]{:S(2)}, u32[]{:S(2)}) collective-permute-start(f32[4,3,8,128]{3,2,1,0:T(8,128)S(1)} %get-tuple-element.39), channel_id=1, source_target_pairs={{0,3},{1,66},{2,65},{3,0},{4,7},{5,70},{6,69},{7,4},{8,11},{9,74},... | collective-permute-start | bytes 147464 | tf_op jit(solution)/shard_map/ppermute | solution.py:32
